TPU v7x, 32 devices: a whole 2x2x4 slice. The times are simulated.
32 devices in a mesh: shard: 2 (over x), ctx: 4 (over y, core), tensor: 4 (over z).
Axes of the slice: x: 2, y: 2, z: 4, core: 2. Of those that a mesh axis runs over, the one named last changes fastest.
Arguments:
- inputs: bfloat16 [1024, 4, 1024], P('ctx', 'shard', 'tensor'), may hold values from -6 to 6
- w_query: bfloat16 [2, 1024, 1024], P(None, ('shard', 'ctx'), 'tensor'), may hold values from -0.1875 to 0.1875
- w_key: bfloat16 [2, 1024, 1024], P(None, ('shard', 'ctx'), 'tensor'), may hold values from -0.1875 to 0.1875
- w_value: bfloat16 [2, 1024, 1024], P(None, ('shard', 'ctx'), 'tensor'), may hold values from -0.1875 to 0.1875
- w_out: bfloat16 [2, 1024, 1024], P(None, 'tensor', ('shard', 'ctx')), may hold values from -3 to 3
- w_gate: bfloat16 [2, 1024, 4096], P(None, ('shard', 'ctx'), 'tensor'), may hold values from -0.1875 to 0.1875
- w_up: bfloat16 [2, 1024, 4096], P(None, ('shard', 'ctx'), 'tensor'), may hold values from -0.1875 to 0.1875
- w_down: bfloat16 [2, 4096, 1024], P(None, 'tensor', ('shard', 'ctx')), may hold values from -0.09375 to 0.09375
- attn_gain: float32 [2, 1024], P(None, 'tensor'), may hold values from 0.5 to 1.5
- ffn_gain: float32 [2, 1024], P(None, 'tensor'), may hold values from 0.5 to 1.5
- variate_bias: float32 [2, 16, 2], P(None, 'tensor'), may hold values from -4 to 4
- lengths: int32 [4], P('shard'), may hold values from 512 to 1024, as said below
- variates: int32 [1024, 4], P('ctx', 'shard'), may hold values from 0 to 7
- cotangent: bfloat16 [1024, 4, 1024], P('ctx', 'shard', 'tensor'), may hold values from -6 to 6
Outputs:
- output: bfloat16 [1024, 4, 1024], P('ctx', 'shard', 'tensor')
- input_grad: float32 [1024, 4, 1024], P('ctx', 'shard', 'tensor')
- grad_w_query: float32 [2, 1024, 1024], P(None, ('shard', 'ctx'), 'tensor')
- grad_w_key: float32 [2, 1024, 1024], P(None, ('shard', 'ctx'), 'tensor')
- grad_w_value: float32 [2, 1024, 1024], P(None, ('shard', 'ctx'), 'tensor')
- grad_w_out: float32 [2, 1024, 1024], P(None, 'tensor', ('shard', 'ctx'))
- grad_w_gate: float32 [2, 1024, 4096], P(None, ('shard', 'ctx'), 'tensor')
- grad_w_up: float32 [2, 1024, 4096], P(None, ('shard', 'ctx'), 'tensor')
- grad_w_down: float32 [2, 4096, 1024], P(None, 'tensor', ('shard', 'ctx'))
- grad_attn_gain: float32 [2, 1024], P(None, 'tensor')
- grad_ffn_gain: float32 [2, 1024], P(None, 'tensor')
- grad_variate_bias: float32 [2, 16, 2], P(None, 'tensor')
Inputs may be any that keep to these rules, and one draw needn't show every extreme that they name: `lengths`: of every 2 consecutive slots (those of one index of shard), one, drawn from the seed, has length 1024.
All inputs are finite; a program needn't handle non-finite values.
Results may differ from a plain program's by a relative error of at most 0.034.
Values may be sent and summed in bfloat16 or wider, within the bound.
No kernel may reach another device: no remote copies, remote signals or barrier semaphores. Data moves between devices by JAX's collectives and lax.ppermute only.
A program may use at most 192 MiB of HBM per device.

v0:
```python
import jax
import jax.numpy as jnp
from jax import lax
from jax.sharding import PartitionSpec as P

D = 1024
HD = 64
LAYERS = 2


epsilon = 1e-06
masked = -1e30


def angle_table(positions, half_width):
    index_half = jnp.arange(half_width, dtype=jnp.float32)
    inverse = 10000.0 ** (-(2.0 * index_half) / (2 * half_width))
    return positions.astype(jnp.float32)[:, None] * inverse[None, :]


def rotate(values_in, cosine, sine_table, head_count):
    leading = values_in.shape[:-1]
    width_all = values_in.shape[-1]
    by_head = values_in.reshape(leading + (head_count, width_all // head_count))
    half_width = width_all // head_count // 2
    first_half = by_head[..., :half_width]
    second_half = by_head[..., half_width:]
    cosine = cosine[:, None, None, :]
    sine_table = sine_table[:, None, None, :]
    turned = jnp.concatenate(
        [
            first_half * cosine - second_half * sine_table,
            second_half * cosine + first_half * sine_table,
        ],
        axis=-1,
    )
    return turned.reshape(leading + (width_all,))


def row_total(partial_rows):
    return lax.psum(partial_rows, "tensor")


def inverse_scale(current):
    totals = row_total(jnp.sum(current * current, axis=-1))
    return lax.rsqrt(totals / D + epsilon)


def norm_back(upstream, current, row_scale, gain_row):
    normed = current * row_scale[..., None]
    gain_grad = jnp.sum(upstream * normed, axis=(0, 1))
    scaled = upstream * gain_row
    row_dots = row_total(jnp.sum(scaled * normed, axis=-1))
    return (row_scale[..., None] * (scaled - normed * (row_dots / D)[..., None]), gain_grad)


def spread_rows(share_rows):
    return lax.all_gather(share_rows, "tensor", axis=2, tiled=True)


def collect_rows(partial_value):
    return lax.psum_scatter(
        partial_value.astype(jnp.bfloat16), "tensor", scatter_dimension=2, tiled=True
    ).astype(jnp.float32)


def spread_grads(share_rows):
    return lax.all_gather(share_rows, "tensor", axis=2, tiled=True)


def collect_grads(partial_value):
    return lax.psum_scatter(
        partial_value.astype(jnp.bfloat16), "tensor", scatter_dimension=2, tiled=True
    ).astype(jnp.float32)


def layer_weights(w_query, w_key, w_value, w_out, w_gate, w_up, w_down, layer_index):
    return (
        lax.all_gather(w_query[layer_index], ("shard", "ctx"), axis=0, tiled=True),
        lax.all_gather(w_key[layer_index], ("shard", "ctx"), axis=0, tiled=True),
        lax.all_gather(w_value[layer_index], ("shard", "ctx"), axis=0, tiled=True),
        lax.all_gather(w_out[layer_index], ("shard", "ctx"), axis=1, tiled=True),
        lax.all_gather(w_gate[layer_index], ("shard", "ctx"), axis=0, tiled=True),
        lax.all_gather(w_up[layer_index], ("shard", "ctx"), axis=0, tiled=True),
        lax.all_gather(w_down[layer_index], ("shard", "ctx"), axis=1, tiled=True),
    )


def layer_weights_again(w_query, w_key, w_value, w_out, w_gate, w_up, w_down, layer_index):
    return (
        lax.all_gather(w_query[layer_index], ("shard", "ctx"), axis=0, tiled=True),
        lax.all_gather(w_key[layer_index], ("shard", "ctx"), axis=0, tiled=True),
        lax.all_gather(w_value[layer_index], ("shard", "ctx"), axis=0, tiled=True),
        lax.all_gather(w_out[layer_index], ("shard", "ctx"), axis=1, tiled=True),
        lax.all_gather(w_gate[layer_index], ("shard", "ctx"), axis=0, tiled=True),
        lax.all_gather(w_up[layer_index], ("shard", "ctx"), axis=0, tiled=True),
        lax.all_gather(w_down[layer_index], ("shard", "ctx"), axis=1, tiled=True),
    )


def head_scores(queries, key_rows, same_kind, key_valid, bias_pair):
    raw_scores = (
        jnp.einsum("csd,usd->scu", queries, key_rows, preferred_element_type=jnp.float32) * 0.125
    )
    shifted = raw_scores + jnp.where(same_kind, bias_pair[0], bias_pair[1])
    return jnp.where(key_valid, shifted, masked)


def attend(queries, key_rows, values, same_kind, key_valid, bias_layer):
    head_count = queries.shape[2] // HD
    outputs = []
    sums_log = []
    for head_index in range(head_count):
        columns = slice(head_index * HD, (head_index + 1) * HD)
        scores = head_scores(
            queries[:, :, columns],
            key_rows[:, :, columns],
            same_kind,
            key_valid,
            bias_layer[head_index],
        )
        highest = jnp.max(scores, axis=-1, keepdims=True)
        exponent = jnp.exp(scores - highest)
        totals = jnp.sum(exponent, axis=-1, keepdims=True)
        soft_weights = (exponent / totals).astype(jnp.bfloat16)
        outputs.append(
            jnp.einsum(
                "scu,usd->csd",
                soft_weights,
                values[:, :, columns],
                preferred_element_type=jnp.float32,
            )
        )
        sums_log.append(highest[..., 0] + jnp.log(totals[..., 0]))
    return (jnp.concatenate(outputs, axis=-1).astype(jnp.bfloat16), sums_log)


def attend_back(queries, key_rows, values, same_kind, key_valid, bias_layer, sums_log, out_grad):
    head_count = queries.shape[2] // HD
    query_grads = []
    key_grads = []
    value_grads = []
    bias_grads = []
    for head_index in range(head_count):
        columns = slice(head_index * HD, (head_index + 1) * HD)
        scores = head_scores(
            queries[:, :, columns],
            key_rows[:, :, columns],
            same_kind,
            key_valid,
            bias_layer[head_index],
        )
        soft_float = jnp.exp(scores - sums_log[head_index][..., None])
        soft_grad = jnp.einsum(
            "csd,usd->scu",
            out_grad[:, :, columns],
            values[:, :, columns],
            preferred_element_type=jnp.float32,
        )
        weighted = jnp.sum(soft_float * soft_grad, axis=-1, keepdims=True)
        score_grad = soft_float * (soft_grad - weighted)
        bias_grads.append(
            jnp.stack(
                [
                    jnp.sum(jnp.where(same_kind, score_grad, 0.0)),
                    jnp.sum(jnp.where(same_kind, 0.0, score_grad)),
                ]
            )
        )
        score_low = score_grad.astype(jnp.bfloat16)
        query_grads.append(
            jnp.einsum(
                "scu,usd->csd",
                score_low,
                key_rows[:, :, columns],
                preferred_element_type=jnp.float32,
            )
            * 0.125
        )
        key_grads.append(
            jnp.einsum(
                "scu,csd->usd",
                score_low,
                queries[:, :, columns],
                preferred_element_type=jnp.float32,
            )
            * 0.125
        )
        value_grads.append(
            jnp.einsum(
                "scu,csd->usd",
                soft_float.astype(jnp.bfloat16),
                out_grad[:, :, columns],
                preferred_element_type=jnp.float32,
            )
        )
    return (
        jnp.concatenate(query_grads, axis=-1),
        jnp.concatenate(key_grads, axis=-1),
        jnp.concatenate(value_grads, axis=-1),
        jnp.stack(bias_grads),
    )


def per_device(
    inputs,
    w_query,
    w_key,
    w_value,
    w_out,
    w_gate,
    w_up,
    w_down,
    attn_gain,
    ffn_gain,
    variate_bias,
    lengths,
    variates,
    cotangent,
):
    block_rows = inputs.shape[0]
    slot_length = block_rows * lax.axis_size("ctx")
    positions = lax.axis_index("ctx") * block_rows + jnp.arange(block_rows, dtype=jnp.int32)
    angles = angle_table(positions, HD // 2)
    cosine = jnp.cos(angles)
    sine_table = jnp.sin(angles)
    head_count = w_query.shape[2] // HD
    valid_rows = (positions[:, None] < lengths[None, :]).astype(jnp.float32)
    key_valid = (jnp.arange(slot_length, dtype=jnp.int32)[None, :] < lengths[:, None])[:, None, :]
    query_kinds = variates.T
    kinds_low = variates.astype(jnp.bfloat16)
    current = inputs.astype(jnp.float32)
    kept_layers = []
    for layer_index in range(LAYERS):
        gathered = layer_weights(w_query, w_key, w_value, w_out, w_gate, w_up, w_down, layer_index)
        query_matrix, key_matrix, value_matrix, out_matrix, gate_matrix, up_matrix, down_matrix = (
            gathered
        )
        scale_attn = inverse_scale(current)
        normed = spread_rows(
            (current * scale_attn[..., None] * attn_gain[layer_index]).astype(jnp.bfloat16)
        )
        queries = rotate(
            jnp.einsum("csd,de->cse", normed, query_matrix, preferred_element_type=jnp.float32),
            cosine,
            sine_table,
            head_count,
        ).astype(jnp.bfloat16)
        keys_local = rotate(
            jnp.einsum("csd,de->cse", normed, key_matrix, preferred_element_type=jnp.float32),
            cosine,
            sine_table,
            head_count,
        ).astype(jnp.bfloat16)
        values_local = jnp.einsum(
            "csd,de->cse", normed, value_matrix, preferred_element_type=jnp.float32
        ).astype(jnp.bfloat16)
        all_keys, all_values, all_kinds = (
            lax.all_gather(keys_local, "ctx", axis=0, tiled=True),
            lax.all_gather(values_local, "ctx", axis=0, tiled=True),
            lax.all_gather(kinds_low, "ctx", axis=0, tiled=True),
        )
        all_kind_ids = all_kinds.astype(jnp.int32).T
        same_kind = query_kinds[:, :, None] == all_kind_ids[:, None, :]
        attended, sums_log = attend(
            queries, all_keys, all_values, same_kind, key_valid, variate_bias[layer_index]
        )
        residual = current + collect_rows(
            jnp.einsum("cse,ed->csd", attended, out_matrix, preferred_element_type=jnp.float32)
        )
        scale_ffn = inverse_scale(residual)
        normed_ffn = spread_rows(
            (residual * scale_ffn[..., None] * ffn_gain[layer_index]).astype(jnp.bfloat16)
        )
        gate_pre = jnp.einsum(
            "csd,df->csf", normed_ffn, gate_matrix, preferred_element_type=jnp.float32
        )
        up_part = jnp.einsum(
            "csd,df->csf", normed_ffn, up_matrix, preferred_element_type=jnp.float32
        )
        hidden = (jax.nn.silu(gate_pre) * up_part).astype(jnp.bfloat16)
        next_state = residual + collect_rows(
            jnp.einsum("csf,fd->csd", hidden, down_matrix, preferred_element_type=jnp.float32)
        )
        kept_layers.append(
            (
                current,
                scale_attn,
                normed,
                queries,
                keys_local,
                values_local,
                all_keys,
                all_values,
                same_kind,
                all_kind_ids,
                sums_log,
                attended,
                residual,
                scale_ffn,
                normed_ffn,
                gate_pre,
                up_part,
                hidden,
                gathered,
            )
        )
        current = next_state
    output = (current * valid_rows[..., None]).astype(jnp.bfloat16)
    upstream = cotangent.astype(jnp.float32) * valid_rows[..., None]
    by_layer = [None] * LAYERS
    attn_gain_list = [None] * LAYERS
    ffn_gain_list = [None] * LAYERS
    bias_list = [None] * LAYERS
    for layer_index in reversed(range(LAYERS)):
        (
            state_in,
            scale_attn,
            normed,
            queries,
            keys_local,
            values_local,
            all_keys,
            all_values,
            same_kind,
            all_kind_ids,
            sums_log,
            attended,
            residual,
            scale_ffn,
            normed_ffn,
            gate_pre,
            up_part,
            hidden,
            gathered,
        ) = kept_layers[layer_index]
        matrices = layer_weights_again(
            w_query, w_key, w_value, w_out, w_gate, w_up, w_down, layer_index
        )
        keys_all, values_all = (
            lax.all_gather(keys_local, "ctx", axis=0, tiled=True),
            lax.all_gather(values_local, "ctx", axis=0, tiled=True),
        )
        query_matrix, key_matrix, value_matrix, out_matrix, gate_matrix, up_matrix, down_matrix = (
            matrices
        )
        down_input = spread_grads(upstream.astype(jnp.bfloat16))
        grad_down_w = jnp.einsum(
            "csf,csd->fd", hidden, down_input, preferred_element_type=jnp.float32
        )
        hidden_grad = jnp.einsum(
            "csd,fd->csf", down_input, down_matrix, preferred_element_type=jnp.float32
        )
        sigmoid_gate = jax.nn.sigmoid(gate_pre)
        silu_gate = gate_pre * sigmoid_gate
        gate_grad = (
            hidden_grad * up_part * sigmoid_gate * (1.0 + gate_pre * (1.0 - sigmoid_gate))
        ).astype(jnp.bfloat16)
        up_grad = (hidden_grad * silu_gate).astype(jnp.bfloat16)
        grad_gate_w = jnp.einsum(
            "csd,csf->df", normed_ffn, gate_grad, preferred_element_type=jnp.float32
        )
        grad_up_w = jnp.einsum(
            "csd,csf->df", normed_ffn, up_grad, preferred_element_type=jnp.float32
        )
        ffn_normed_grad = collect_grads(
            jnp.einsum("csf,df->csd", gate_grad, gate_matrix, preferred_element_type=jnp.float32)
            + jnp.einsum("csf,df->csd", up_grad, up_matrix, preferred_element_type=jnp.float32)
        )
        residual_back, ffn_gain_grad = norm_back(
            ffn_normed_grad, residual, scale_ffn, ffn_gain[layer_index]
        )
        residual_grad = upstream + residual_back
        out_input = spread_grads(residual_grad.astype(jnp.bfloat16))
        grad_out_w = jnp.einsum(
            "cse,csd->ed", attended, out_input, preferred_element_type=jnp.float32
        )
        attended_grad = jnp.einsum(
            "csd,ed->cse", out_input, out_matrix, preferred_element_type=jnp.float32
        ).astype(jnp.bfloat16)
        query_grad, key_grad_all, value_grad_all, bias_grad = attend_back(
            queries,
            keys_all,
            values_all,
            same_kind,
            key_valid,
            variate_bias[layer_index],
            sums_log,
            attended_grad,
        )
        key_grad, value_grad = (
            lax.psum_scatter(
                key_grad_all.astype(jnp.bfloat16), "ctx", scatter_dimension=0, tiled=True
            ).astype(jnp.float32),
            lax.psum_scatter(
                value_grad_all.astype(jnp.bfloat16), "ctx", scatter_dimension=0, tiled=True
            ).astype(jnp.float32),
        )
        query_low = rotate(query_grad, cosine, -sine_table, head_count).astype(jnp.bfloat16)
        key_low = rotate(key_grad, cosine, -sine_table, head_count).astype(jnp.bfloat16)
        value_low = value_grad.astype(jnp.bfloat16)
        grad_query_w = jnp.einsum(
            "csd,cse->de", normed, query_low, preferred_element_type=jnp.float32
        )
        grad_key_w = jnp.einsum("csd,cse->de", normed, key_low, preferred_element_type=jnp.float32)
        grad_value_w = jnp.einsum(
            "csd,cse->de", normed, value_low, preferred_element_type=jnp.float32
        )
        attn_normed_grad = collect_grads(
            jnp.einsum("cse,de->csd", query_low, query_matrix, preferred_element_type=jnp.float32)
            + jnp.einsum("cse,de->csd", key_low, key_matrix, preferred_element_type=jnp.float32)
            + jnp.einsum("cse,de->csd", value_low, value_matrix, preferred_element_type=jnp.float32)
        )
        state_back, attn_gain_grad = norm_back(
            attn_normed_grad, state_in, scale_attn, attn_gain[layer_index]
        )
        upstream = residual_grad + state_back
        attn_gain_list[layer_index] = attn_gain_grad
        ffn_gain_list[layer_index] = ffn_gain_grad
        bias_list[layer_index] = bias_grad
        by_layer[layer_index] = (
            lax.psum_scatter(
                grad_query_w.astype(jnp.bfloat16), ("shard", "ctx"), scatter_dimension=0, tiled=True
            ).astype(jnp.float32),
            lax.psum_scatter(
                grad_key_w.astype(jnp.bfloat16), ("shard", "ctx"), scatter_dimension=0, tiled=True
            ).astype(jnp.float32),
            lax.psum_scatter(
                grad_value_w.astype(jnp.bfloat16), ("shard", "ctx"), scatter_dimension=0, tiled=True
            ).astype(jnp.float32),
            lax.psum_scatter(
                grad_out_w.astype(jnp.bfloat16), ("shard", "ctx"), scatter_dimension=1, tiled=True
            ).astype(jnp.float32),
            lax.psum_scatter(
                grad_gate_w.astype(jnp.bfloat16), ("shard", "ctx"), scatter_dimension=0, tiled=True
            ).astype(jnp.float32),
            lax.psum_scatter(
                grad_up_w.astype(jnp.bfloat16), ("shard", "ctx"), scatter_dimension=0, tiled=True
            ).astype(jnp.float32),
            lax.psum_scatter(
                grad_down_w.astype(jnp.bfloat16), ("shard", "ctx"), scatter_dimension=1, tiled=True
            ).astype(jnp.float32),
        )
    stacks = [
        jnp.stack([by_layer[layer_index][member] for layer_index in range(LAYERS)])
        for member in range(7)
    ]
    attn_gain_total, ffn_gain_total, bias_total = lax.psum(
        (jnp.stack(attn_gain_list), jnp.stack(ffn_gain_list), jnp.stack(bias_list)),
        ("shard", "ctx"),
    )
    return (
        output,
        upstream,
        stacks[0],
        stacks[1],
        stacks[2],
        stacks[3],
        stacks[4],
        stacks[5],
        stacks[6],
        attn_gain_total,
        ffn_gain_total,
        bias_total,
    )


def solution(mesh):
    return jax.shard_map(
        per_device,
        mesh=mesh,
        in_specs=(
            P("ctx", "shard", "tensor"),
            P(None, ("shard", "ctx"), "tensor"),
            P(None, ("shard", "ctx"), "tensor"),
            P(None, ("shard", "ctx"), "tensor"),
            P(None, "tensor", ("shard", "ctx")),
            P(None, ("shard", "ctx"), "tensor"),
            P(None, ("shard", "ctx"), "tensor"),
            P(None, "tensor", ("shard", "ctx")),
            P(None, "tensor"),
            P(None, "tensor"),
            P(None, "tensor", None),
            P("shard"),
            P("ctx", "shard"),
            P("ctx", "shard", "tensor"),
        ),
        out_specs=(
            P("ctx", "shard", "tensor"),
            P("ctx", "shard", "tensor"),
            P(None, ("shard", "ctx"), "tensor"),
            P(None, ("shard", "ctx"), "tensor"),
            P(None, ("shard", "ctx"), "tensor"),
            P(None, "tensor", ("shard", "ctx")),
            P(None, ("shard", "ctx"), "tensor"),
            P(None, ("shard", "ctx"), "tensor"),
            P(None, "tensor", ("shard", "ctx")),
            P(None, "tensor"),
            P(None, "tensor"),
            P(None, "tensor", None),
        ),
        check_vma=False,
    )
```

profile of v0, /device:TPU:0, one launch (start us, length us, event | category | flops | bytes accessed | tf_op | source)
XLA Modules:
  0.0 1531.3 jit_solution(2848524258843653660)
XLA Ops:
  110.4 26.3 %reduce-scatter.35.cloned.1.call-done = bf16[256,2,256]{2,0,1:T(8,128)(2,1)} async-done(((bf16[256,2,1024]{2,0,1:T(8,128)(2,1)}), bf16[256,2,256]{2,0,1:T(8,128)(2,1)}) %reduce-scatter.35.cloned.1.call-update) | async-done | bytes 262160 | tf_op jit(solution)/shard_map/reduce_scatter | solution.py:62
  151.1 26.9 %all-gather.39.cloned.1.call-done = bf16[256,2,1024]{2,0,1:T(8,128)(2,1)} async-done(((bf16[256,2,256]{2,0,1:T(8,128)(2,1)}), bf16[256,2,1024]{2,0,1:T(8,128)(2,1)}) %all-gather.39.cloned.1.call-update) | async-done | bytes 1048592 | tf_op jit(solution)/shard_map/all_gather | solution.py:58
  182.6 24.0 %all-gather.59.cloned.1.call-done = bf16[1,1024,1024]{2,1,0:T(8,128)(2,1)} async-done(((bf16[1,128,1024]{2,1,0:T(8,128)(2,1)}), bf16[1,1024,1024]{2,1,0:T(8,128)(2,1)}) %all-gather.59.cloned.1.call-update) | async-done | bytes 2097168 | tf_op jit(solution)/shard_map/all_gather | solution.py:84
  211.7 25.5 %all-gather.61.cloned.1.call-done = bf16[1,1024,1024]{2,1,0:T(8,128)(2,1)} async-done(((bf16[1,1024,128]{2,1,0:T(8,128)(2,1)}), bf16[1,1024,1024]{2,1,0:T(8,128)(2,1)}) %all-gather.61.cloned.1.call-update) | async-done | bytes 2097168 | tf_op jit(solution)/shard_map/all_gather | solution.py:85
  241.5 27.2 %reduce-scatter.37.cloned.1.call-done = bf16[256,2,256]{2,0,1:T(8,128)(2,1)} async-done(((bf16[256,2,1024]{2,0,1:T(8,128)(2,1)}), bf16[256,2,256]{2,0,1:T(8,128)(2,1)}) %reduce-scatter.37.cloned.1.call-update) | async-done | bytes 262160 | tf_op jit(solution)/shard_map/reduce_scatter | solution.py:62
  364.7 38.0 %reduce-scatter.39.cloned.1.call-done = bf16[256,2,256]{2,0,1:T(8,128)(2,1)} async-done(((bf16[256,2,1024]{2,0,1:T(8,128)(2,1)}), bf16[256,2,256]{2,0,1:T(8,128)(2,1)}) %reduce-scatter.39.cloned.1.call-update) | async-done | bytes 262160 | tf_op jit(solution)/shard_map/reduce_scatter | solution.py:62
  416.3 17.7 %all-gather.67.cloned.1.call-done = bf16[1,1024,1024]{2,1,0:T(8,128)(2,1)} async-done(((bf16[1,1024,128]{2,1,0:T(8,128)(2,1)}), bf16[1,1024,1024]{2,1,0:T(8,128)(2,1)}) %all-gather.67.cloned.1.call-update) | async-done | bytes 2097168 | tf_op jit(solution)/shard_map/all_gather | solution.py:85
  438.6 26.0 %all-gather.65.cloned.1.call-done = bf16[1,1024,1024]{2,1,0:T(8,128)(2,1)} async-done(((bf16[1,128,1024]{2,1,0:T(8,128)(2,1)}), bf16[1,1024,1024]{2,1,0:T(8,128)(2,1)}) %all-gather.65.cloned.1.call-update) | async-done | bytes 2097168 | tf_op jit(solution)/shard_map/all_gather | solution.py:84
  464.6 32.3 %all-gather.47.cloned.1.call-done = bf16[256,2,1024]{2,0,1:T(8,128)(2,1)} async-done(((bf16[256,2,256]{2,0,1:T(8,128)(2,1)}), bf16[256,2,1024]{2,0,1:T(8,128)(2,1)}) %all-gather.47.cloned.1.call-update) | async-done | bytes 1048592 | tf_op jit(solution)/shard_map/all_gather | solution.py:58
  501.4 24.4 %all-gather.63.cloned.1.call-done = bf16[1,1024,1024]{2,1,0:T(8,128)(2,1)} async-done(((bf16[1,128,1024]{2,1,0:T(8,128)(2,1)}), bf16[1,1024,1024]{2,1,0:T(8,128)(2,1)}) %all-gather.63.cloned.1.call-update) | async-done | bytes 2097168 | tf_op jit(solution)/shard_map/all_gather | solution.py:83
  541.1 22.9 %reduce-scatter.43.cloned.1.call-done = bf16[256,2,256]{2,0,1:T(8,128)(2,1)} async-done(((bf16[256,2,1024]{2,0,1:T(8,128)(2,1)}), bf16[256,2,256]{2,0,1:T(8,128)(2,1)}) %reduce-scatter.43.cloned.1.call-update) | async-done | bytes 262160 | tf_op jit(solution)/shard_map/reduce_scatter | solution.py:72
  595.1 28.2 %all-gather.51.cloned.1.call-done = bf16[256,2,1024]{2,0,1:T(8,128)(2,1)} async-done(((bf16[256,2,256]{2,0,1:T(8,128)(2,1)}), bf16[256,2,1024]{2,0,1:T(8,128)(2,1)}) %all-gather.51.cloned.1.call-update) | async-done | bytes 1048592 | tf_op jit(solution)/shard_map/all_gather | solution.py:68
  671.5 21.3 %reduce-scatter.47.cloned.1.call-done = bf16[256,2,256]{0,2,1:T(8,128)(2,1)} async-done(((bf16[1024,2,256]{0,2,1:T(8,128)(2,1)}), bf16[256,2,256]{0,2,1:T(8,128)(2,1)}) %reduce-scatter.47.cloned.1.call-update) | async-done | bytes 262160 | tf_op jit(solution)/shard_map/reduce_scatter | solution.py:395
  696.8 27.2 %reduce-scatter.49.cloned.1.call-done = bf16[256,2,256]{2,0,1:T(8,128)(2,1)} async-done(((bf16[256,2,1024]{2,0,1:T(8,128)(2,1)}), bf16[256,2,256]{2,0,1:T(8,128)(2,1)}) %reduce-scatter.49.cloned.1.call-update) | async-done | bytes 262160 | tf_op jit(solution)/shard_map/reduce_scatter | solution.py:72
  737.2 28.7 %all-gather.53.cloned.1.call-done = bf16[256,2,1024]{2,0,1:T(8,128)(2,1)} async-done(((bf16[256,2,256]{2,0,1:T(8,128)(2,1)}), bf16[256,2,1024]{2,0,1:T(8,128)(2,1)}) %all-gather.53.cloned.1.call-update) | async-done | bytes 1048592 | tf_op jit(solution)/shard_map/all_gather | solution.py:68
  775.7 25.4 %reduce-scatter.51.cloned.1.call-done = bf16[256,2,256]{2,0,1:T(8,128)(2,1)} async-done(((bf16[256,2,1024]{2,0,1:T(8,128)(2,1)}), bf16[256,2,256]{2,0,1:T(8,128)(2,1)}) %reduce-scatter.51.cloned.1.call-update) | async-done | bytes 262160 | tf_op jit(solution)/shard_map/reduce_scatter | solution.py:72
  814.6 28.7 %all-gather.55.cloned.1.call-done = bf16[256,2,1024]{2,0,1:T(8,128)(2,1)} async-done(((bf16[256,2,256]{2,0,1:T(8,128)(2,1)}), bf16[256,2,1024]{2,0,1:T(8,128)(2,1)}) %all-gather.55.cloned.1.call-update) | async-done | bytes 1048592 | tf_op jit(solution)/shard_map/all_gather | solution.py:68
  924.3 21.9 %reduce-scatter.85.cloned.1.call-done = bf16[128,1024]{1,0:T(8,128)(2,1)} async-done(((bf16[1024,1024]{1,0:T(8,128)(2,1)}), bf16[128,1024]{1,0:T(8,128)(2,1)}) %reduce-scatter.85.cloned.1.call-update) | async-done | bytes 262160
  948.0 36.0 %reduce-scatter.81.cloned.1.call-done = bf16[128,256]{1,0:T(8,128)(2,1)} async-done(((bf16[1024,256]{1,0:T(8,128)(2,1)}), bf16[128,256]{1,0:T(8,128)(2,1)}) %reduce-scatter.81.cloned.1.call-update) | async-done | bytes 65552
  985.0 43.8 %reduce-scatter.83.cloned.1.call-done = bf16[128,1024]{1,0:T(8,128)(2,1)} async-done(((bf16[1024,1024]{1,0:T(8,128)(2,1)}), bf16[128,1024]{1,0:T(8,128)(2,1)}) %reduce-scatter.83.cloned.1.call-update) | async-done | bytes 262160
  1037.7 35.6 %reduce-scatter.73.cloned.1.call-done = bf16[128,1024]{1,0:T(8,128)(2,1)} async-done(((bf16[1024,1024]{1,0:T(8,128)(2,1)}), bf16[128,1024]{1,0:T(8,128)(2,1)}) %reduce-scatter.73.cloned.1.call-update) | async-done | bytes 262160 | tf_op jit(solution)/shard_map/reduce_scatter | solution.py:434
  1073.3 44.9 %reduce-scatter.71.cloned.1.call-done = bf16[128,1024]{1,0:T(8,128)(2,1)} async-done(((bf16[1024,1024]{1,0:T(8,128)(2,1)}), bf16[128,1024]{1,0:T(8,128)(2,1)}) %reduce-scatter.71.cloned.1.call-update) | async-done | bytes 262160 | tf_op jit(solution)/shard_map/reduce_scatter | solution.py:434
  1120.3 42.5 %reduce-scatter.77.cloned.1.call-done = bf16[128,1024]{1,0:T(8,128)(2,1)} async-done(((bf16[1024,1024]{1,0:T(8,128)(2,1)}), bf16[128,1024]{1,0:T(8,128)(2,1)}) %reduce-scatter.77.cloned.1.call-update) | async-done | bytes 262160 | tf_op jit(solution)/shard_map/reduce_scatter | solution.py:437
  1162.7 44.7 %reduce-scatter.75.cloned.1.call-done = bf16[128,1024]{1,0:T(8,128)(2,1)} async-done(((bf16[1024,1024]{1,0:T(8,128)(2,1)}), bf16[128,1024]{1,0:T(8,128)(2,1)}) %reduce-scatter.75.cloned.1.call-update) | async-done | bytes 262160 | tf_op jit(solution)/shard_map/reduce_scatter | solution.py:437
  1220.4 24.4 %reduce-scatter.79.cloned.1.call-done = bf16[128,256]{1,0:T(8,128)(2,1)} async-done(((bf16[1024,256]{1,0:T(8,128)(2,1)}), bf16[128,256]{1,0:T(8,128)(2,1)}) %reduce-scatter.79.cloned.1.call-update) | async-done | bytes 65552
  1246.5 35.7 %reduce-scatter.69.cloned.1.call-done = bf16[128,256]{1,0:T(8,128)(2,1)} async-done(((bf16[1024,256]{1,0:T(8,128)(2,1)}), bf16[128,256]{1,0:T(8,128)(2,1)}) %reduce-scatter.69.cloned.1.call-update) | async-done | bytes 65552 | tf_op jit(solution)/shard_map/reduce_scatter | solution.py:428
  1282.2 37.0 %reduce-scatter.67.cloned.1.call-done = bf16[128,256]{1,0:T(8,128)(2,1)} async-done(((bf16[1024,256]{1,0:T(8,128)(2,1)}), bf16[128,256]{1,0:T(8,128)(2,1)}) %reduce-scatter.67.cloned.1.call-update) | async-done | bytes 65552 | tf_op jit(solution)/shard_map/reduce_scatter | solution.py:428
  1320.8 35.9 %reduce-scatter.61.cloned.1.call-done = bf16[128,256]{1,0:T(8,128)(2,1)} async-done(((bf16[1024,256]{1,0:T(8,128)(2,1)}), bf16[128,256]{1,0:T(8,128)(2,1)}) %reduce-scatter.61.cloned.1.call-update) | async-done | bytes 65552 | tf_op jit(solution)/shard_map/reduce_scatter | solution.py:422
  1356.7 37.2 %reduce-scatter.59.cloned.1.call-done = bf16[128,256]{1,0:T(8,128)(2,1)} async-done(((bf16[1024,256]{1,0:T(8,128)(2,1)}), bf16[128,256]{1,0:T(8,128)(2,1)}) %reduce-scatter.59.cloned.1.call-update) | async-done | bytes 65552 | tf_op jit(solution)/shard_map/reduce_scatter | solution.py:422
  1395.5 35.8 %reduce-scatter.65.cloned.1.call-done = bf16[128,256]{1,0:T(8,128)(2,1)} async-done(((bf16[1024,256]{1,0:T(8,128)(2,1)}), bf16[128,256]{1,0:T(8,128)(2,1)}) %reduce-scatter.65.cloned.1.call-update) | async-done | bytes 65552 | tf_op jit(solution)/shard_map/reduce_scatter | solution.py:425
  1431.3 37.2 %reduce-scatter.63.cloned.1.call-done = bf16[128,256]{1,0:T(8,128)(2,1)} async-done(((bf16[1024,256]{1,0:T(8,128)(2,1)}), bf16[128,256]{1,0:T(8,128)(2,1)}) %reduce-scatter.63.cloned.1.call-update) | async-done | bytes 65552 | tf_op jit(solution)/shard_map/reduce_scatter | solution.py:425
  1470.1 28.0 %reduce-scatter.57.cloned.1.call-done = bf16[256,2,256]{2,0,1:T(8,128)(2,1)} async-done(((bf16[256,2,1024]{2,0,1:T(8,128)(2,1)}), bf16[256,2,256]{2,0,1:T(8,128)(2,1)}) %reduce-scatter.57.cloned.1.call-update) | async-done | bytes 262160 | tf_op jit(solution)/shard_map/reduce_scatter | solution.py:72
  (625 shorter events, 521.8 us)
Async XLA Ops:
  110.3 67.7 %all-gather.39.cloned.1.call-start = ((), (), s32[]{:S(2)}) async-start(), calls=%async_computation.30 | async-start | bytes 1310720 | tf_op jit(solution)/shard_map/all_gather | solution.py:58
  150.1 87.1 %all-gather.61.cloned.1.call-start = ((), (), s32[]{:S(2)}) async-start(), calls=%async_computation.62 | async-start | bytes 2359296 | tf_op jit(solution)/shard_map/all_gather | solution.py:85
  151.1 117.7 %reduce-scatter.37.cloned.1.call-start = ((), (), s32[]{:S(2)}) async-start(), calls=%async_computation.31 | async-start | bytes 1310720 | tf_op jit(solution)/shard_map/reduce_scatter | solution.py:62
  241.4 68.6 %all-gather.41.cloned.1.call-start = ((), (), s32[]{:S(2)}) async-start(), calls=%async_computation.32 | async-start | bytes 1310720 | tf_op jit(solution)/shard_map/all_gather | solution.py:58
  336.2 66.5 %reduce-scatter.39.cloned.1.call-start = ((), (), s32[]{:S(2)}) async-start(), calls=%async_computation.35 | async-start | bytes 1310720 | tf_op jit(solution)/shard_map/reduce_scatter | solution.py:62
  363.3 70.7 %all-gather.67.cloned.1.call-start = ((), (), s32[]{:S(2)}) async-start(), calls=%async_computation.65 | async-start | bytes 2359296 | tf_op jit(solution)/shard_map/all_gather | solution.py:85
  363.9 100.7 %all-gather.65.cloned.1.call-start = ((), (), s32[]{:S(2)}) async-start(), calls=%async_computation.64 | async-start | bytes 2359296 | tf_op jit(solution)/shard_map/all_gather | solution.py:84
  364.6 132.3 %all-gather.47.cloned.1.call-start = ((), (), s32[]{:S(2)}) async-start(), calls=%async_computation.36 | async-start | bytes 1310720 | tf_op jit(solution)/shard_map/all_gather | solution.py:58
  415.2 110.5 %all-gather.63.cloned.1.call-start = ((), (), s32[]{:S(2)}) async-start(), calls=%async_computation.63 | async-start | bytes 2359296 | tf_op jit(solution)/shard_map/all_gather | solution.py:83
  416.0 148.0 %reduce-scatter.43.cloned.1.call-start = ((), (), s32[]{:S(2)}) async-start(), calls=%async_computation.39 | async-start | bytes 1310720 | tf_op jit(solution)/shard_map/reduce_scatter | solution.py:72
  541.1 82.2 %all-gather.51.cloned.1.call-start = ((), (), s32[]{:S(2)}) async-start(), calls=%async_computation.40 | async-start | bytes 1310720 | tf_op jit(solution)/shard_map/all_gather | solution.py:68
  594.5 70.9 %reduce-scatter.45.cloned.1.call-start = ((), (), s32[]{:S(2)}) async-start(), calls=%async_computation.41 | async-start | bytes 1310720 | tf_op jit(solution)/shard_map/reduce_scatter | solution.py:392
  649.0 75.0 %reduce-scatter.49.cloned.1.call-start = ((), (), s32[]{:S(2)}) async-start(), calls=%async_computation.43 | async-start | bytes 1310720 | tf_op jit(solution)/shard_map/reduce_scatter | solution.py:72
  696.8 69.1 %all-gather.53.cloned.1.call-start = ((), (), s32[]{:S(2)}) async-start(), calls=%async_computation.44 | async-start | bytes 1310720 | tf_op jit(solution)/shard_map/all_gather | solution.py:68
  775.7 67.6 %all-gather.55.cloned.1.call-start = ((), (), s32[]{:S(2)}) async-start(), calls=%async_computation.46 | async-start | bytes 1310720 | tf_op jit(solution)/shard_map/all_gather | solution.py:68
  814.5 93.8 %reduce-scatter.55.cloned.1.call-start = ((), (), s32[]{:S(2)}) async-start(), calls=%async_computation.48 | async-start | bytes 1310720 | tf_op jit(solution)/shard_map/reduce_scatter | solution.py:395
  850.3 68.4 %reduce-scatter.53.cloned.1.call-start = ((), (), s32[]{:S(2)}) async-start(), calls=%async_computation.47 | async-start | bytes 1310720 | tf_op jit(solution)/shard_map/reduce_scatter | solution.py:392
  872.8 73.5 %reduce-scatter.85.cloned.1.call-start = ((), (), s32[]{:S(2)}) async-start(), calls=%async_computation.69 | async-start | bytes 2359296
  878.3 105.7 %reduce-scatter.81.cloned.1.call-start = ((), (), s32[]{:S(2)}) async-start(), calls=%async_computation.67 | async-start | bytes 589824
  881.0 147.8 %reduce-scatter.83.cloned.1.call-start = ((), (), s32[]{:S(2)}) async-start(), calls=%async_computation.68 | async-start | bytes 2359296
  886.7 186.6 %reduce-scatter.73.cloned.1.call-start = ((), (), s32[]{:S(2)}) async-start(), calls=%async_computation.57 | async-start | bytes 2359296 | tf_op jit(solution)/shard_map/reduce_scatter | solution.py:434
  890.8 227.4 %reduce-scatter.71.cloned.1.call-start = ((), (), s32[]{:S(2)}) async-start(), calls=%async_computation.56 | async-start | bytes 2359296 | tf_op jit(solution)/shard_map/reduce_scatter | solution.py:434
  896.1 266.7 %reduce-scatter.77.cloned.1.call-start = ((), (), s32[]{:S(2)}) async-start(), calls=%async_computation.59 | async-start | bytes 2359296 | tf_op jit(solution)/shard_map/reduce_scatter | solution.py:437
  900.3 307.2 %reduce-scatter.75.cloned.1.call-start = ((), (), s32[]{:S(2)}) async-start(), calls=%async_computation.58 | async-start | bytes 2359296 | tf_op jit(solution)/shard_map/reduce_scatter | solution.py:437
  904.2 340.6 %reduce-scatter.79.cloned.1.call-start = ((), (), s32[]{:S(2)}) async-start(), calls=%async_computation.66 | async-start | bytes 589824
  906.8 375.3 %reduce-scatter.69.cloned.1.call-start = ((), (), s32[]{:S(2)}) async-start(), calls=%async_computation.55 | async-start | bytes 589824 | tf_op jit(solution)/shard_map/reduce_scatter | solution.py:428
  908.2 411.0 %reduce-scatter.67.cloned.1.call-start = ((), (), s32[]{:S(2)}) async-start(), calls=%async_computation.54 | async-start | bytes 589824 | tf_op jit(solution)/shard_map/reduce_scatter | solution.py:428
  910.5 446.2 %reduce-scatter.61.cloned.1.call-start = ((), (), s32[]{:S(2)}) async-start(), calls=%async_computation.51 | async-start | bytes 589824 | tf_op jit(solution)/shard_map/reduce_scatter | solution.py:422
  911.9 482.0 %reduce-scatter.59.cloned.1.call-start = ((), (), s32[]{:S(2)}) async-start(), calls=%async_computation.50 | async-start | bytes 589824 | tf_op jit(solution)/shard_map/reduce_scatter | solution.py:422
  921.9 509.4 %reduce-scatter.65.cloned.1.call-start = ((), (), s32[]{:S(2)}) async-start(), calls=%async_computation.53 | async-start | bytes 589824 | tf_op jit(solution)/shard_map/reduce_scatter | solution.py:425
  923.3 545.2 %reduce-scatter.63.cloned.1.call-start = ((), (), s32[]{:S(2)}) async-start(), calls=%async_computation.52 | async-start | bytes 589824 | tf_op jit(solution)/shard_map/reduce_scatter | solution.py:425
  1032.0 466.1 %reduce-scatter.57.cloned.1.call-start = ((), (), s32[]{:S(2)}) async-start(), calls=%async_computation.49 | async-start | bytes 1310720 | tf_op jit(solution)/shard_map/reduce_scatter | solution.py:72
  (162 other events, 3246.9 us)
Sparse Core Ops, SparseCore 0:
  25.3 28.3 all-gather.32
  57.2 16.7 all-gather.36
  85.7 15.5 all-gather.34
  109.6 27.1 reduce-scatter.34
  241.6 27.1 reduce-scatter.36
  281.2 28.7 all-gather.40
  314.2 15.4 all-gather.44
  336.3 16.2 all-gather.42
  364.4 39.9 all-gather.48
  406.8 27.1 all-gather.66
  436.7 27.8 all-gather.64
  466.7 30.1 all-gather.46
  499.5 26.1 all-gather.62
  642.2 23.1 reduce-scatter.44
  667.8 24.9 reduce-scatter.46
  850.4 23.1 reduce-scatter.54
  876.6 24.9 reduce-scatter.52
  905.0 41.1 reduce-scatter.84
  949.9 34.1 reduce-scatter.80
  987.5 41.2 reduce-scatter.82
  1032.1 41.1 reduce-scatter.72
  1076.9 41.2 reduce-scatter.70
  1121.5 41.1 reduce-scatter.76
  1166.2 41.2 reduce-scatter.74
  1210.5 34.1 reduce-scatter.78
  1248.0 34.0 reduce-scatter.68
  1285.1 34.0 reduce-scatter.66
  1322.6 34.0 reduce-scatter.60
  1359.8 34.0 reduce-scatter.58
  1397.1 34.0 reduce-scatter.64
  1434.4 34.1 reduce-scatter.62
  1470.9 27.1 reduce-scatter.56
Sparse Core Ops, SparseCore 1:
  112.4 27.7 all-gather.56
  149.3 28.6 all-gather.38
  180.5 26.0 all-gather.58
  209.2 28.0 all-gather.60
  361.4 41.2 reduce-scatter.38
  536.9 27.1 reduce-scatter.42
  566.2 25.7 reduce-scatter.40
  594.6 28.6 all-gather.50
  696.8 27.1 reduce-scatter.48
  737.0 28.7 all-gather.52
  775.7 25.4 reduce-scatter.50
  814.5 28.7 all-gather.54
where the time goes:
time: 1540 us; the launch traced here: 1530 us
  waiting for transfers between devices  1030 us (67%)
  blocking collectives  179 us (12%)
  matrix products  166 us (11%)
  other arithmetic  78.4 us (5%)
  local copies, waits for them, and re-layouts  51.7 us (3%)
  between operations  18.3 us (1%)
    unnamed x48, waiting for transfers between devices  129 us
    reduce_scatter x4, waiting for transfers between devices, collect_rows(): lax.psum_scatter(partial_value.astype(jnp.bfloat16), 'tensor', scatter_di...  108 us
    reduce_scatter x4, waiting for transfers between devices, collect_grads(): lax.psum_scatter(partial_value.astype(jnp.bfloat16), 'tensor', scatter_di...  104 us
    reduce_scatter x2, waiting for transfers between devices, per_device(): lax.psum_scatter(grad_up_w.astype(jnp.bfloat16), ('shard', 'ctx'), scatte...  87.2 us
    all_gather x4, waiting for transfers between devices, spread_grads(): return lax.all_gather(share_rows, 'tensor', axis=2, tiled=True)  85.5 us
    reduce_scatter x2, waiting for transfers between devices, per_device(): lax.psum_scatter(grad_gate_w.astype(jnp.bfloat16), ('shard', 'ctx'), scat...  80.5 us
    psum x8, blocking collectives, row_total(): return lax.psum(partial_rows, 'tensor')  78.3 us
    reduce_scatter x2, waiting for transfers between devices, per_device(): lax.psum_scatter(grad_query_w.astype(jnp.bfloat16), ('shard', 'ctx'), sca...  73.1 us
  transfers between devices with their start and end apart: 44, of which 38 were waited for; matrix products, arithmetic and copies ran while one was open for 12% of the time, Pallas kernels for 0%

commit v1 on v0

v1 whole, which is shorter than its diff:
```python
import jax
import jax.numpy as jnp
from jax import lax
from jax.sharding import PartitionSpec as P

HD = 64
LAYERS = 2
epsilon = 1e-06
masked = -1e30
F32 = jnp.float32
LOW = jnp.bfloat16
AXES = ("shard", "ctx", "tensor")


def bits_of(count):
    width = count.bit_length() - 1
    assert 1 << width == count
    return width


def dot(left, right, left_dim, right_dim):
    return lax.dot_general(
        left, right, (((left_dim,), (right_dim,)), ((), ())), preferred_element_type=F32
    )


class Place:
    def __init__(self, mesh):
        self.n_shard = mesh.shape["shard"]
        self.n_ctx = mesh.shape["ctx"]
        assert mesh.shape["tensor"] == 4 and self.n_ctx % 2 == 0
        self.s_bits = bits_of(self.n_shard)
        self.o_bits = bits_of(self.n_ctx // 2)
        self.dp = [("s", i) for i in reversed(range(self.s_bits))] + [
            ("o", i) for i in reversed(range(self.o_bits))
        ]

    def locate(self):
        shard = lax.axis_index("shard")
        ctx = lax.axis_index("ctx")
        tensor = lax.axis_index("tensor")
        self.o = ctx // 2
        self.c = ctx % 2
        self.zh = tensor // 2
        self.zl = tensor % 2
        self.dp_bit = [((shard if kind == "s" else self.o) >> i) & 1 for kind, i in self.dp]

    def move(self, array, route):
        pairs = []
        for shard in range(self.n_shard):
            for ctx in range(self.n_ctx):
                for tensor in range(4):
                    s, o, c, zh, zl = route(shard, ctx // 2, ctx % 2, tensor // 2, tensor % 2)
                    source = (shard * self.n_ctx + ctx) * 4 + tensor
                    target = (s * self.n_ctx + 2 * o + c) * 4 + 2 * zh + zl
                    pairs.append((source, target))
        return lax.ppermute(array, AXES, pairs)

    def swap_core(self, array):
        return self.move(array, lambda s, o, c, zh, zl: (s, o, 1 - c, zh, zl))

    def swap_zl(self, array):
        return self.move(array, lambda s, o, c, zh, zl: (s, o, c, zh, 1 - zl))

    def swap_zh(self, array):
        return self.move(array, lambda s, o, c, zh, zl: (s, o, c, 1 - zh, zl))

    def swap_dp(self, array, index):
        kind, i = self.dp[index]
        if kind == "s":
            return self.move(array, lambda s, o, c, zh, zl: (s ^ (1 << i), o, c, zh, zl))
        return self.move(array, lambda s, o, c, zh, zl: (s, o ^ (1 << i), c, zh, zl))

    def near(self, array):
        return self.move(array, lambda s, o, c, zh, zl: (s, o, zh, c, zl))

    def far(self, array):
        return self.move(array, lambda s, o, c, zh, zl: (s, o, zh, 1 - c, zl))

    def far_back(self, array):
        return self.move(array, lambda s, o, c, zh, zl: (s, o, 1 - zh, c, zl))


def flip_if(bit, array, axis):
    return jnp.where(bit == 1, jnp.flip(array, axis), array)


def pick(flag, one, two):
    return jnp.where(flag == 1, one, two)


def to_frame(place, rows):
    lead = rows.shape[:-1]
    k = len(place.dp)
    blocks = 2 ** (k + 1)
    width = rows.shape[-1] // blocks
    cut = rows.reshape(lead + (2,) * (k + 1) + (width,))
    n = len(lead)
    for i in range(k):
        cut = flip_if(place.dp_bit[i], cut, n + i)
    cut = flip_if(place.zh, cut, n + k)
    first = lax.index_in_dim(cut, 0, n + k, keepdims=False)
    second = lax.index_in_dim(cut, 1, n + k, keepdims=False)
    order = tuple(range(n)) + tuple(reversed(range(n, n + k))) + (n + k,)
    second = second.transpose(order)
    half = rows.shape[-1] // 2
    return jnp.concatenate([first.reshape(lead + (half,)), second.reshape(lead + (half,))], -1)


def from_frame(place, rows):
    lead = rows.shape[:-1]
    k = len(place.dp)
    blocks = 2 ** (k + 1)
    width = rows.shape[-1] // blocks
    n = len(lead)
    half = rows.shape[-1] // 2
    first = rows[..., :half].reshape(lead + (2,) * k + (width,))
    second = rows[..., half:].reshape(lead + (2,) * k + (width,))
    order = tuple(range(n)) + tuple(reversed(range(n, n + k))) + (n + k,)
    second = second.transpose(order)
    cut = jnp.stack([first, second], n + k)
    for i in range(k):
        cut = flip_if(place.dp_bit[i], cut, n + i)
    cut = flip_if(place.zh, cut, n + k)
    return cut.reshape(lead + (rows.shape[-1],))


def gather_rows(place, natural):
    k = len(place.dp)
    halves = []
    for part, order in ((place.near(natural), range(k)), (place.far(natural), reversed(range(k)))):
        pieces = [part]
        for index in order:
            received = [place.swap_dp(piece, index) for piece in pieces]
            pieces = [piece for pair in zip(pieces, received) for piece in pair]
        halves += pieces
    return jnp.concatenate(halves, 0)


def scatter_rows(place, partial):
    k = len(place.dp)
    half = partial.shape[0] // 2
    ends = []
    for part, order in ((partial[:half], range(k)), (partial[half:], reversed(range(k)))):
        for index in order:
            middle = part.shape[0] // 2
            received = place.swap_dp(part[middle:], index)
            part = (part[:middle].astype(F32) + received.astype(F32)).astype(LOW)
        ends.append(part)
    return place.near(ends[0]).astype(F32) + place.far_back(ends[1]).astype(F32)


def gather_feats(place, share):
    other = place.swap_zl(share)
    half = jnp.concatenate([pick(place.zl, other, share), pick(place.zl, share, other)], -1)
    rest = place.swap_core(half)
    return jnp.concatenate([pick(place.c, rest, half), pick(place.c, half, rest)], -1)


def scatter_feats(place, partial):
    wide = partial.shape[-1] // 2
    first, second = partial[:, :wide], partial[:, wide:]
    received = place.swap_core(pick(place.c, first, second).astype(LOW))
    kept = pick(place.c, second, first) + received.astype(F32)
    width = wide // 2
    first, second = kept[:, :width], kept[:, width:]
    received = place.swap_zl(pick(place.zl, first, second).astype(LOW))
    return pick(place.zl, second, first) + received.astype(F32)


def gather_tokens(place, natural):
    positions, slots, width = natural.shape
    half = slots // 2
    first, second = natural[:, :half], natural[:, half:]
    received = place.swap_zh(pick(place.zh, first, second))
    own = pick(place.zh, second, first)
    two = jnp.stack([pick(place.zh, received, own), pick(place.zh, own, received)], 2)
    other = place.swap_zl(two)
    four = jnp.stack([pick(place.zl, other, two), pick(place.zl, two, other)], 3)
    full = four.reshape(positions, half, 4 * width).transpose(1, 0, 2)
    rest = place.swap_core(full)
    both = jnp.concatenate([pick(place.c, rest, full), pick(place.c, full, rest)], 1)
    return to_frame(place, both.reshape(half * 2 * positions, 4 * width))


def place_tokens(place, rows, positions, slots):
    half = slots // 2
    width = rows.shape[-1] // 4
    cut = from_frame(place, rows).reshape(half, 2, positions, 2, 2, width)
    cut = pick(place.c, cut[:, 1], cut[:, 0])
    cut = pick(place.zl, cut[:, :, :, 1], cut[:, :, :, 0])
    own = pick(place.zh, cut[:, :, 1], cut[:, :, 0])
    received = place.swap_zh(pick(place.zh, cut[:, :, 0], cut[:, :, 1]))
    both = jnp.concatenate(
        [pick(place.zh, received, own), pick(place.zh, own, received)], 0
    )
    return both.transpose(1, 0, 2)


def gather_keys(place, own):
    pieces = [own]
    for index in reversed(range(place.s_bits, len(place.dp))):
        received = [place.swap_dp(piece, index) for piece in pieces]
        pieces = pieces + received
    return jnp.concatenate(pieces, 1)


def scatter_keys(place, partial):
    for index in range(place.s_bits, len(place.dp)):
        middle = partial.shape[1] // 2
        received = place.swap_dp(partial[:, middle:].astype(LOW), index)
        partial = partial[:, :middle] + received.astype(F32)
    return partial


def rotate(values, cosine, sine):
    lead = values.shape[:-1]
    heads = values.shape[-1] // HD
    cut = values.reshape(lead + (heads, 2, HD // 2))
    first, second = cut[..., 0, :], cut[..., 1, :]
    cosine = cosine[:, None, :]
    sine = sine[:, None, :]
    turned = jnp.stack(
        [first * cosine - second * sine, second * cosine + first * sine], axis=-2
    )
    return turned.reshape(values.shape)


def head_scores(queries, keys, same_kind, key_valid, bias_pair):
    raw = jnp.einsum("scd,sud->scu", queries, keys, preferred_element_type=F32) * 0.125
    shifted = raw + jnp.where(same_kind, bias_pair[0], bias_pair[1])
    return jnp.where(key_valid, shifted, masked)


def attend(queries, keys, values, same_kind, key_valid, bias):
    outputs = []
    logs = []
    for head in range(queries.shape[2] // HD):
        cols = slice(head * HD, (head + 1) * HD)
        scores = head_scores(
            queries[:, :, cols], keys[:, :, cols], same_kind, key_valid, bias[head]
        )
        highest = jnp.max(scores, axis=-1, keepdims=True)
        exponent = jnp.exp(scores - highest)
        totals = jnp.sum(exponent, axis=-1, keepdims=True)
        weights = (exponent / totals).astype(LOW)
        outputs.append(
            jnp.einsum("scu,sud->scd", weights, values[:, :, cols], preferred_element_type=F32)
        )
        logs.append(highest[..., 0] + jnp.log(totals[..., 0]))
    return jnp.concatenate(outputs, axis=-1).astype(LOW), logs


def attend_back(queries, keys, values, same_kind, key_valid, bias, logs, out_grad):
    query_grads, key_grads, value_grads, bias_grads = [], [], [], []
    for head in range(queries.shape[2] // HD):
        cols = slice(head * HD, (head + 1) * HD)
        scores = head_scores(
            queries[:, :, cols], keys[:, :, cols], same_kind, key_valid, bias[head]
        )
        soft = jnp.exp(scores - logs[head][..., None])
        soft_grad = jnp.einsum(
            "scd,sud->scu", out_grad[:, :, cols], values[:, :, cols], preferred_element_type=F32
        )
        weighted = jnp.sum(soft * soft_grad, axis=-1, keepdims=True)
        score_grad = soft * (soft_grad - weighted)
        bias_grads.append(
            jnp.stack(
                [
                    jnp.sum(jnp.where(same_kind, score_grad, 0.0)),
                    jnp.sum(jnp.where(same_kind, 0.0, score_grad)),
                ]
            )
        )
        low = score_grad.astype(LOW)
        query_grads.append(
            jnp.einsum("scu,sud->scd", low, keys[:, :, cols], preferred_element_type=F32) * 0.125
        )
        key_grads.append(
            jnp.einsum("scu,scd->sud", low, queries[:, :, cols], preferred_element_type=F32)
            * 0.125
        )
        value_grads.append(
            jnp.einsum(
                "scu,scd->sud",
                soft.astype(LOW),
                out_grad[:, :, cols],
                preferred_element_type=F32,
            )
        )
    return (
        jnp.concatenate(query_grads, axis=-1),
        jnp.concatenate(key_grads, axis=-1),
        jnp.concatenate(value_grads, axis=-1),
        jnp.stack(bias_grads),
    )


def per_device(place):
    def run(
        inputs,
        w_query,
        w_key,
        w_value,
        w_out,
        w_gate,
        w_up,
        w_down,
        attn_gain,
        ffn_gain,
        variate_bias,
        lengths,
        variates,
        cotangent,
    ):
        place.locate()
        positions, slots, quarter = inputs.shape
        D = quarter * 4
        half_slots = slots // 2
        block = 2 * positions
        n_o = place.n_ctx // 2
        tokens = half_slots * block
        heads = w_query.shape[2] // HD
        own_quarter = 2 * place.c + place.zl

        small = jnp.concatenate(
            [attn_gain.reshape(-1), ffn_gain.reshape(-1), variate_bias.reshape(-1)]
        )
        small = lax.all_gather(small, "tensor", axis=0)
        cut = LAYERS * quarter
        natural_gains = [
            small[:, i * cut : (i + 1) * cut]
            .reshape(4, LAYERS, quarter)
            .transpose(1, 0, 2)
            .reshape(LAYERS, D)
            for i in range(2)
        ]
        attn_gains = to_frame(place, natural_gains[0])
        ffn_gains = to_frame(place, natural_gains[1])
        biases = lax.dynamic_index_in_dim(
            small[:, 2 * cut :].reshape(4, LAYERS, heads, 2), own_quarter, 0, keepdims=False
        )

        kinds = lax.all_gather(variates, "ctx", axis=0)
        kinds = kinds.reshape((2,) * place.o_bits + (block, slots))
        for i in range(place.o_bits):
            kinds = flip_if(place.dp_bit[place.s_bits + i], kinds, i)
        kinds = kinds.reshape(n_o, block, slots)
        kinds = pick(place.zh, kinds[:, :, half_slots:], kinds[:, :, :half_slots])
        kinds = kinds.reshape(n_o * block, half_slots).T
        own_kinds = kinds[:, :block]
        same_kind = own_kinds[:, :, None] == kinds[:, None, :]
        own_lengths = pick(place.zh, lengths[half_slots:], lengths[:half_slots])
        own_positions = place.o * block + jnp.arange(block, dtype=jnp.int32)
        chips = jnp.arange(n_o, dtype=jnp.int32) ^ place.o
        key_positions = (
            chips[:, None] * block + jnp.arange(block, dtype=jnp.int32)[None, :]
        ).reshape(-1)
        key_valid = (key_positions[None, :] < own_lengths[:, None])[:, None, :]
        valid = (own_positions[None, :] < own_lengths[:, None]).astype(F32).reshape(tokens, 1)
        inverse = 10000.0 ** (-(2.0 * jnp.arange(HD // 2, dtype=F32)) / HD)
        angles = own_positions.astype(F32)[:, None] * inverse[None, :]
        cosine, sine = jnp.cos(angles), jnp.sin(angles)

        def share_of(rows):
            return lax.dynamic_slice_in_dim(rows, own_quarter * quarter, quarter, -1)

        full = gather_tokens(place, inputs)
        packed = []
        for layer in range(LAYERS):
            attn_pack = jnp.concatenate(
                [w_query[layer], w_key[layer], w_value[layer], w_out[layer].T], 1
            )
            ffn_pack = jnp.concatenate([w_gate[layer], w_up[layer], w_down[layer].T], 1)
            packed.append((gather_rows(place, attn_pack), gather_rows(place, ffn_pack)))

        current = share_of(full).astype(F32)
        kept = []
        for layer in range(LAYERS):
            attn_w, ffn_w = packed[layer]
            hidden = ffn_w.shape[1] // 3
            width = attn_w.shape[1] // 4
            full_float = full.astype(F32)
            scale = lax.rsqrt(jnp.mean(full_float * full_float, -1, keepdims=True) + epsilon)
            normed = (full_float * scale * attn_gains[layer]).astype(LOW)
            three = dot(normed, attn_w[:, : 3 * width], 1, 0)
            three = three.reshape(half_slots, block, 3 * width)
            queries = rotate(three[:, :, :width], cosine, sine).astype(LOW)
            keys = rotate(three[:, :, width : 2 * width], cosine, sine).astype(LOW)
            values = three[:, :, 2 * width :].astype(LOW)
            both = gather_keys(place, jnp.concatenate([keys, values], -1))
            keys, values = both[:, :, :width], both[:, :, width:]
            attended, logs = attend(queries, keys, values, same_kind, key_valid, biases[layer])
            flat = attended.reshape(tokens, width)
            middle = current + scatter_feats(place, dot(flat, attn_w[:, 3 * width :], 1, 1))
            full_mid = gather_feats(place, middle.astype(LOW))
            mid_float = full_mid.astype(F32)
            scale_mid = lax.rsqrt(jnp.mean(mid_float * mid_float, -1, keepdims=True) + epsilon)
            normed_mid = (mid_float * scale_mid * ffn_gains[layer]).astype(LOW)
            gate_up = dot(normed_mid, ffn_w[:, : 2 * hidden], 1, 0)
            gate, up = gate_up[:, :hidden], gate_up[:, hidden:]
            hid = (jax.nn.silu(gate) * up).astype(LOW)
            current = middle + scatter_feats(place, dot(hid, ffn_w[:, 2 * hidden :], 1, 1))
            kept.append(
                (
                    full,
                    scale,
                    normed,
                    queries,
                    keys,
                    values,
                    attended,
                    logs,
                    full_mid,
                    scale_mid,
                    normed_mid,
                    gate,
                    up,
                    hid,
                )
            )
            full = gather_feats(place, current.astype(LOW))

        output = place_tokens(place, (full * valid.astype(LOW)), positions, slots)

        upstream_full = gather_tokens(place, cotangent) * valid.astype(LOW)
        upstream = share_of(upstream_full).astype(F32)

        def norm_back(partial, full_rows, row_scale, gain, before, before_full):
            shared = scatter_feats(place, partial)
            own_rows = share_of(full_rows).astype(F32) * row_scale
            gain_grad = jnp.sum(shared * own_rows, 0)
            moved = before + row_scale * (shared * share_of(gain))
            moved_full = gather_feats(place, moved.astype(LOW)).astype(F32)
            rows = full_rows.astype(F32) * row_scale
            dots = jnp.sum((moved_full - before_full.astype(F32)) * rows, -1, keepdims=True) / D
            after = moved - own_rows * dots
            after_full = (moved_full - rows * dots).astype(LOW)
            return after, after_full, gain_grad

        weight_grads = [None] * LAYERS
        gain_grads = [None] * LAYERS
        bias_grads = [None] * LAYERS
        for layer in reversed(range(LAYERS)):
            attn_w, ffn_w = packed[layer]
            hidden = ffn_w.shape[1] // 3
            width = attn_w.shape[1] // 4
            (
                full,
                scale,
                normed,
                queries,
                keys,
                values,
                attended,
                logs,
                full_mid,
                scale_mid,
                normed_mid,
                gate,
                up,
                hid,
            ) = kept[layer]
            hid_grad = dot(upstream_full, ffn_w[:, 2 * hidden :], 1, 0)
            sig = jax.nn.sigmoid(gate)
            gate_grad = (hid_grad * up * sig * (1.0 + gate * (1.0 - sig))).astype(LOW)
            up_grad = (hid_grad * gate * sig).astype(LOW)
            pair = jnp.concatenate([gate_grad, up_grad], 1)
            normed_grad = dot(pair, ffn_w[:, : 2 * hidden], 1, 1)
            ffn_grad = jnp.concatenate(
                [dot(normed_mid, pair, 0, 0).astype(LOW), dot(upstream_full, hid, 0, 0).astype(LOW)],
                1,
            )
            ffn_out = scatter_rows(place, ffn_grad)
            middle, middle_full, ffn_gain_grad = norm_back(
                normed_grad, full_mid, scale_mid, ffn_gains[layer], upstream, upstream_full
            )
            flat_grad = dot(middle_full, attn_w[:, 3 * width :], 1, 0).astype(LOW)
            out_grad = flat_grad.reshape(half_slots, block, width)
            query_grad, key_grad, value_grad, bias_grads[layer] = attend_back(
                queries, keys, values, same_kind, key_valid, biases[layer], logs, out_grad
            )
            key_value = scatter_keys(place, jnp.concatenate([key_grad, value_grad], -1))
            three = jnp.concatenate(
                [
                    rotate(query_grad, cosine, -sine),
                    rotate(key_value[:, :, :width], cosine, -sine),
                    key_value[:, :, width:],
                ],
                -1,
            )
            three = three.astype(LOW).reshape(tokens, 3 * width)
            normed_grad = dot(three, attn_w[:, : 3 * width], 1, 1)
            attn_grad = jnp.concatenate(
                [
                    dot(normed, three, 0, 0).astype(LOW),
                    dot(middle_full, attended.reshape(tokens, width), 0, 0).astype(LOW),
                ],
                1,
            )
            attn_out = scatter_rows(place, attn_grad)
            upstream, upstream_full, attn_gain_grad = norm_back(
                normed_grad, full, scale, attn_gains[layer], middle, middle_full
            )
            weight_grads[layer] = (
                attn_out[:, :width],
                attn_out[:, width : 2 * width],
                attn_out[:, 2 * width : 3 * width],
                attn_out[:, 3 * width :].T,
                ffn_out[:, :hidden],
                ffn_out[:, hidden : 2 * hidden],
                ffn_out[:, 2 * hidden :].T,
            )
            gain_grads[layer] = (attn_gain_grad, ffn_gain_grad)
        input_grad = place_tokens(place, upstream_full, positions, slots).astype(F32)

        mine = jnp.stack(
            [gain_grads[layer][i] for i in range(2) for layer in range(LAYERS)]
        )
        wide = lax.dynamic_update_slice_in_dim(
            jnp.zeros((2 * LAYERS, D), F32), mine, own_quarter * quarter, 1
        )
        wide = from_frame(place, wide)
        bias_wide = lax.dynamic_update_slice_in_dim(
            jnp.zeros((LAYERS, 4 * heads, 2), F32), jnp.stack(bias_grads), own_quarter * heads, 1
        )
        wide, bias_wide = lax.psum((wide, bias_wide), AXES)
        tensor = lax.axis_index("tensor")
        gains_out = lax.dynamic_slice_in_dim(wide, tensor * quarter, quarter, 1)
        bias_out = lax.dynamic_slice_in_dim(bias_wide, tensor * heads, heads, 1)
        stacks = [
            jnp.stack([weight_grads[layer][member] for layer in range(LAYERS)])
            for member in range(7)
        ]
        return (output, input_grad, *stacks, gains_out[:LAYERS], gains_out[LAYERS:], bias_out)

    return run


def solution(mesh):
    column = P(None, ("shard", "ctx"), "tensor")
    row = P(None, "tensor", ("shard", "ctx"))
    tokens = P("ctx", "shard", "tensor")
    gain = P(None, "tensor")
    bias = P(None, "tensor", None)
    return jax.shard_map(
        per_device(Place(mesh)),
        mesh=mesh,
        in_specs=(
            tokens, column, column, column, row, column, column, row,
            gain, gain, bias, P("shard"), P("ctx", "shard"), tokens,
        ),
        out_specs=(
            tokens, tokens, column, column, column, row, column, column, row, gain, gain, bias,
        ),
        check_vma=False,
    )
```

time: 1540 us -> 753 us (0.49)
  waiting for transfers between devices: 1030 us -> 216 us
  starting transfers between devices: 3.42 us -> 158 us
  blocking collectives: 179 us -> 73.1 us
  matrix products: 166 us -> 85.9 us
  local copies, waits for them, and re-layouts: 51.7 us -> 113 us
    reduce_scatter x22 -> x0, waiting for transfers between devices: 629 us -> none  [the longest x4 108 us: collect_rows(): lax.psum_scatter(partial_value.astype(jnp.bfloat16), 'tensor', scatter_di...]
    all_gather x18 -> x0, waiting for transfers between devices: 277 us -> none  [the longest x4 85.5 us: spread_grads(): return lax.all_gather(share_rows, 'tensor', axis=2, tiled=True)]
    ppermute x0 -> x100, waiting for transfers between devices: none -> 216 us  [move(): return lax.ppermute(array, AXES, pairs)]
    ppermute x0 -> x100, starting transfers between devices: none -> 158 us  [move(): return lax.ppermute(array, AXES, pairs)]
    unnamed x48 -> x0, waiting for transfers between devices: 129 us -> none
    all_gather x9 -> x1, blocking collectives: 87.9 us -> 5.17 us  [run(): kinds = lax.all_gather(variates, 'ctx', axis=0)]
    dot_general x90 -> x72, matrix products: 166 us -> 85.9 us  [the longest x24 38.3 us: dot(): lax.dot_general(left, right, (((left_dim,), (right_dim,)), ((), ())), pre...]
    psum x9 -> x1, blocking collectives: 90.8 us -> 40.3 us  [run(): wide, bias_wide = lax.psum((wide, bias_wide), AXES)]
  transfers between devices with their start and end apart: 44 -> 100, of which waited for: 38 -> 40; matrix products, arithmetic and copies ran while one was open for 12% -> 33% of each run, Pallas kernels for 0% -> 0%
where the time goes in v1:
time: 753 us; the launch traced here: 743 us
  waiting for transfers between devices  216 us (29%)
  starting transfers between devices  158 us (21%)
  local copies, waits for them, and re-layouts  113 us (15%)
  other arithmetic  89.8 us (12%)
  matrix products  85.9 us (11%)
  blocking collectives  73.1 us (10%)
    ppermute x100, waiting for transfers between devices, move(): return lax.ppermute(array, AXES, pairs)  216 us
    ppermute x100, starting transfers between devices, move(): return lax.ppermute(array, AXES, pairs)  158 us
    unnamed x391, local copies, waits for them, and re-layouts  70.9 us
    psum x1, blocking collectives, run(): wide, bias_wide = lax.psum((wide, bias_wide), AXES)  40.3 us
    dot_general x24, matrix products, dot(): lax.dot_general(left, right, (((left_dim,), (right_dim,)), ((), ())), pre...  38.3 us
    unnamed x1, blocking collectives  27.7 us
    dot_general x8, matrix products, head_scores(): jnp.einsum('scd,sud->scu', queries, keys, preferred_element_type=F32)  16.5 us
  transfers between devices with their start and end apart: 100, of which 40 were waited for; matrix products, arithmetic and copies ran while one was open for 33% of the time, Pallas kernels for 0%

profile of v1, /device:TPU:0, one launch (start us, length us, event | category | flops | bytes accessed | tf_op | source)
XLA Modules:
  0.0 742.7 jit_solution(16769668756249959237)
XLA Ops:
  22.5 27.7 %all-reduce = f32[4160]{0:T(1024)S(1)} all-reduce(f32[4160]{0:T(1024)S(1)} %maximum_dynamic-update-slice_fusion), channel_id=2, replica_groups=mesh['shard'=2,'ctx'=4,'tensor'=4] {'tensor'}, use_global_device_ids=true, to_apply=%add | all-reduce | flops 4160 | bytes 33280
  50.6 5.2 all-gather.1
  67.3 7.8 %collective-permute-done.54 = bf16[256,1,256]{0,2,1:T(8,128)(2,1)S(1)} collective-permute-done((bf16[256,1,256]{0,2,1:T(8,128)(2,1)S(1)}, bf16[256,1,256]{0,2,1:T(8,128)(2,1)S(1)}, u32[]{:S(2)}, u32[]{:S(2)}) %collective-permute-start.54) | collective-permute-done | bytes 131104 | tf_op jit(solution)/shard_map/ppermute | solution.py:57
  116.5 7.4 %collective-permute-start.41 = (bf16[128,3072]{0,1:T(8,128)(2,1)}, bf16[128,3072]{0,1:T(8,128)(2,1)}, u32[]{:S(2)}, u32[]{:S(2)}) collective-permute-start(bf16[128,3072]{0,1:T(8,128)(2,1)} %pad_maximum_fusion.26), channel_id=1, source_target_pairs={{0,0},{1,1},{2,4},{3,5},{4,2},{5,3},{6,6},{7,7},{8,8},{9,9},{10,12... | collective-permute-start | bytes 2359304 | tf_op jit(solution)/shard_map/ppermute | solution.py:57
  131.7 14.0 %collective-permute-start.56 = (bf16[1,256,1024]{1,2,0:T(8,128)(2,1)S(1)}, bf16[1,256,1024]{1,2,0:T(8,128)(2,1)}, u32[]{:S(2)}, u32[]{:S(2)}) collective-permute-start(bf16[1,256,1024]{1,2,0:T(8,128)(2,1)S(1)} %bitcast.553), channel_id=1, source_target_pairs={{0,4},{1,5},{2,6},{3,7},{4,0},{5,1},{6,2},{7,3},{8,12},{9,13},{10,... | collective-permute-start | bytes 1572872 | tf_op jit(solution)/shard_map/ppermute | solution.py:57
  163.2 12.4 %collective-permute-done.11 = bf16[1,512,512]{2,1,0:T(8,128)(2,1)S(1)} collective-permute-done((bf16[1,512,512]{2,1,0:T(8,128)(2,1)S(1)}, bf16[1,512,512]{2,1,0:T(8,128)(2,1)S(1)}, u32[]{:S(2)}, u32[]{:S(2)}) %collective-permute-start.11) | collective-permute-done | bytes 524320 | tf_op jit(solution)/shard_map/ppermute | solution.py:57
  192.3 8.8 %collective-permute-start.12 = (bf16[512,512]{1,0:T(8,128)(2,1)S(1)}, bf16[512,512]{1,0:T(8,128)(2,1)S(1)}, u32[]{:S(2)}, u32[]{:S(2)}) collective-permute-start(bf16[512,512]{1,0:T(8,128)(2,1)S(1)} %select_convert_fusion.7), channel_id=1, source_target_pairs={{0,4},{1,5},{2,6},{3,7},{4,0},{5,1},{6,2},{7,3},{8,12},{9,13},{10,... | collective-permute-start | bytes 1572872 | tf_op jit(solution)/shard_map/ppermute | solution.py:57
  206.7 6.2 collective-permute-done.13
  214.7 7.3 collective-permute-done.22
  222.5 16.3 %collective-permute-done.19 = bf16[128,3072]{0,1:T(8,128)(2,1)S(1)} collective-permute-done((bf16[128,3072]{0,1:T(8,128)(2,1)}, bf16[128,3072]{0,1:T(8,128)(2,1)S(1)}, u32[]{:S(2)}, u32[]{:S(2)}) %collective-permute-start.19) | collective-permute-done | bytes 786464 | tf_op jit(solution)/shard_map/ppermute | solution.py:57
  239.6 13.7 %constant_dynamic-update-slice_fusion.15 = bf16[1024,3072]{0,1:T(8,128)(2,1)S(1)} fusion(bf16[1024,3072]{0,1:T(8,128)(2,1)S(1)} %constant_dynamic-update-slice_fusion.16, bf16[128,3072]{0,1:T(8,128)(2,1)} %collective-permute-done.20), kind=kLoop, calls=%fused_computation.620 | loop fusion | bytes 1572864
  260.3 5.0 collective-permute-done.23
  280.6 6.5 collective-permute-done.25
  289.2 5.7 collective-permute-done.26
  305.2 11.2 %collective-permute-done.44 = bf16[128,3072]{0,1:T(8,128)(2,1)} collective-permute-done((bf16[128,3072]{0,1:T(8,128)(2,1)}, bf16[128,3072]{0,1:T(8,128)(2,1)}, u32[]{:S(2)}, u32[]{:S(2)}) %collective-permute-start.44) | collective-permute-done | bytes 786464 | tf_op jit(solution)/shard_map/ppermute | solution.py:57
  318.5 8.5 %collective-permute-done.36 = bf16[1,512,512]{2,1,0:T(8,128)(2,1)S(1)} collective-permute-done((bf16[1,512,512]{2,1,0:T(8,128)(2,1)S(1)}, bf16[1,512,512]{2,1,0:T(8,128)(2,1)S(1)}, u32[]{:S(2)}, u32[]{:S(2)}) %collective-permute-start.36) | collective-permute-done | bytes 524320 | tf_op jit(solution)/shard_map/ppermute | solution.py:57
  349.2 6.2 collective-permute-done.38
  356.5 6.5 collective-permute-done.39
  383.3 6.8 collective-permute-done.50
  406.0 9.7 %collective-permute-done.94 = bf16[256,3072]{1,0:T(8,128)(2,1)S(1)} collective-permute-done((bf16[256,3072]{1,0:T(8,128)(2,1)S(1)}, bf16[256,3072]{1,0:T(8,128)(2,1)S(1)}, u32[]{:S(2)}, u32[]{:S(2)}) %collective-permute-start.94) | collective-permute-done | bytes 1572896 | tf_op jit(solution)/shard_map/ppermute | solution.py:57
  470.5 9.2 %collective-permute-done.61 = bf16[1,512,512]{1,2,0:T(8,128)(2,1)S(1)} collective-permute-done((bf16[1,512,512]{1,2,0:T(8,128)(2,1)S(1)}, bf16[1,512,512]{1,2,0:T(8,128)(2,1)S(1)}, u32[]{:S(2)}, u32[]{:S(2)}) %collective-permute-start.61) | collective-permute-done | bytes 524320 | tf_op jit(solution)/shard_map/ppermute | solution.py:57
  491.8 6.5 collective-permute-done.82
  506.7 10.9 %collective-permute-start.87 = (bf16[128,1024]{0,1:T(8,128)(2,1)S(1)}, bf16[128,1024]{0,1:T(8,128)(2,1)S(1)}, u32[]{:S(2)}, u32[]{:S(2)}) collective-permute-start(bf16[128,1024]{0,1:T(8,128)(2,1)S(1)} %add_convert_fusion.12), channel_id=1, source_target_pairs={{0,4},{1,5},{2,0},{3,1},{4,6},{5,7},{6,2},{7,3},{8,12},{9,13},{10,... | collective-permute-start | bytes 786440 | tf_op jit(solution)/shard_map/ppermute | solution.py:57
  518.6 11.0 %collective-permute-start.65 = (bf16[512,512]{1,0:T(8,128)(2,1)S(1)}, bf16[512,512]{1,0:T(8,128)(2,1)S(1)}, u32[]{:S(2)}, u32[]{:S(2)}) collective-permute-start(bf16[512,512]{1,0:T(8,128)(2,1)S(1)} %pad_maximum_fusion.41), channel_id=1, source_target_pairs={{0,4},{1,5},{2,6},{3,7},{4,0},{5,1},{6,2},{7,3},{8,12},{9,13},{10,... | collective-permute-start | bytes 1572872 | tf_op jit(solution)/shard_map/ppermute | solution.py:57
  546.2 6.6 collective-permute-done.67
  555.7 5.8 collective-permute-done.68
  561.6 17.3 %collective-permute-done.88 = bf16[256,3072]{1,0:T(8,128)(2,1)S(1)} collective-permute-done((bf16[256,3072]{1,0:T(8,128)(2,1)S(1)}, bf16[256,3072]{1,0:T(8,128)(2,1)S(1)}, u32[]{:S(2)}, u32[]{:S(2)}) %collective-permute-start.88) | collective-permute-done | bytes 1572896 | tf_op jit(solution)/shard_map/ppermute | solution.py:57
  597.0 8.5 %fusion.52 = (f32[]{:T(128)}, f32[]{:T(128)}, f32[]{:T(128)}, f32[]{:T(128)}, f32[]{:T(128)}, /*index=5*/f32[]{:T(128)}, f32[]{:T(128)}, f32[]{:T(128)}, f32[]{:...) fusion(s32[1024]{0:T(1024)S(1)} %bitcast.632, ...), kind=kLoop, calls=%fused_computation.122 | loop fusion | flops 25690100 | bytes 29382720 | tf_op jit(solution)/shard_map/reduce_sum | solution.py:270
  641.4 7.4 collective-permute-start.90
  652.1 5.8 collective-permute-done.72
  659.8 8.2 %collective-permute-start.81 = (bf16[128,1024]{0,1:T(8,128)(2,1)}, bf16[128,1024]{0,1:T(8,128)(2,1)}, u32[]{:S(2)}, u32[]{:S(2)}) collective-permute-start(bf16[128,1024]{0,1:T(8,128)(2,1)} %add_convert_fusion.14), channel_id=1, source_target_pairs={{0,4},{1,5},{2,0},{3,1},{4,6},{5,7},{6,2},{7,3},{8,12},{9,13},{10,... | collective-permute-start | bytes 786440 | tf_op jit(solution)/shard_map/ppermute | solution.py:57
  672.5 40.3 %all-reduce.1 = (f32[4,1024]{1,0:T(4,128)S(1)}, f32[2,16,2]{1,2,0:T(2,128)S(1)}) all-reduce(f32[4,1024]{1,0:T(4,128)S(1)} %bitcast.617, f32[2,16,2]{1,2,0:T(2,128)S(1)} %dynamic_update_slice.7), channel_id=1, replica_groups=mesh['shard'=2,'ctx'=4,'tensor'=4] {'shard','ctx','tensor'}, use_global_device_ids=true, to_apply=%region_36.37 | all-reduce | flops 4160 | bytes 33280 | tf_op jit(solution)/shard_map/psum | solution.py:527
  (959 shorter events, 405.4 us)
Async XLA Ops:
  5.4 69.8 %collective-permute-start.3 = (bf16[128,1024]{0,1:T(8,128)(2,1)}, bf16[128,1024]{0,1:T(8,128)(2,1)}, u32[]{:S(2)}, u32[]{:S(2)}) collective-permute-start(bf16[128,1024]{0,1:T(8,128)(2,1)} %pad_maximum_fusion.50), channel_id=1, source_target_pairs={{0,0},{1,1},{2,4},{3,5},{4,2},{5,3},{6,6},{7,7},{8,8},{9,9},{10,12... | collective-permute-start | bytes 786440 | tf_op jit(solution)/shard_map/ppermute | solution.py:57
  9.0 84.2 %collective-permute-start.7 = (bf16[128,1024]{0,1:T(8,128)(2,1)}, bf16[128,1024]{0,1:T(8,128)(2,1)}, u32[]{:S(2)}, u32[]{:S(2)}) collective-permute-start(bf16[128,1024]{0,1:T(8,128)(2,1)} %pad_maximum_fusion.50), channel_id=1, source_target_pairs={{0,2},{1,3},{2,6},{3,7},{4,0},{5,1},{6,4},{7,5},{8,10},{9,11},{10,... | collective-permute-start | bytes 786440 | tf_op jit(solution)/shard_map/ppermute | solution.py:57
  12.5 65.8 %collective-permute-start.28 = (bf16[128,1024]{0,1:T(8,128)(2,1)}, bf16[128,1024]{0,1:T(8,128)(2,1)}, u32[]{:S(2)}, u32[]{:S(2)}) collective-permute-start(bf16[128,1024]{0,1:T(8,128)(2,1)} %pad_maximum_fusion.54), channel_id=1, source_target_pairs={{0,0},{1,1},{2,4},{3,5},{4,2},{5,3},{6,6},{7,7},{8,8},{9,9},{10,12... | collective-permute-start | bytes 786440 | tf_op jit(solution)/shard_map/ppermute | solution.py:57
  16.1 90.1 %collective-permute-start.32 = (bf16[128,1024]{0,1:T(8,128)(2,1)}, bf16[128,1024]{0,1:T(8,128)(2,1)S(1)}, u32[]{:S(2)}, u32[]{:S(2)}) collective-permute-start(bf16[128,1024]{0,1:T(8,128)(2,1)} %pad_maximum_fusion.54), channel_id=1, source_target_pairs={{0,2},{1,3},{2,6},{3,7},{4,0},{5,1},{6,4},{7,5},{8,10},{9,11},{10,... | collective-permute-start | bytes 786440 | tf_op jit(solution)/shard_map/ppermute | solution.py:57
  18.5 47.2 %collective-permute-start = (bf16[256,1,256]{0,2,1:T(8,128)(2,1)}, bf16[256,1,256]{0,2,1:T(8,128)(2,1)}, u32[]{:S(2)}, u32[]{:S(2)}) collective-permute-start(bf16[256,1,256]{0,2,1:T(8,128)(2,1)} %broadcast_select_fusion.39), channel_id=1, source_target_pairs={{0,2},{1,3},{2,0},{3,1},{4,6},{5,7},{6,4},{7,5},{8,10},{9,11},{10,... | collective-permute-start | bytes 393224 | tf_op jit(solution)/shard_map/ppermute | solution.py:57
  93.2 37.2 %collective-permute-start.16 = (bf16[128,3072]{0,1:T(8,128)(2,1)S(1)}, bf16[128,3072]{0,1:T(8,128)(2,1)}, u32[]{:S(2)}, u32[]{:S(2)}) collective-permute-start(bf16[128,3072]{0,1:T(8,128)(2,1)S(1)} %copy-done.70), channel_id=1, source_target_pairs={{0,0},{1,1},{2,4},{3,5},{4,2},{5,3},{6,6},{7,7},{8,8},{9,9},{10,12... | collective-permute-start | bytes 2359304 | tf_op jit(solution)/shard_map/ppermute | solution.py:57
  106.2 45.4 %collective-permute-start.20 = (bf16[128,3072]{0,1:T(8,128)(2,1)S(1)}, bf16[128,3072]{0,1:T(8,128)(2,1)}, u32[]{:S(2)}, u32[]{:S(2)}) collective-permute-start(bf16[128,3072]{0,1:T(8,128)(2,1)S(1)} %copy-done.70), channel_id=1, source_target_pairs={{0,2},{1,3},{2,6},{3,7},{4,0},{5,1},{6,4},{7,5},{8,10},{9,11},{10,... | collective-permute-start | bytes 2359304 | tf_op jit(solution)/shard_map/ppermute | solution.py:57
  125.1 88.5 %collective-permute-start.45 = (bf16[128,3072]{0,1:T(8,128)(2,1)}, bf16[128,3072]{0,1:T(8,128)(2,1)}, u32[]{:S(2)}, u32[]{:S(2)}) collective-permute-start(bf16[128,3072]{0,1:T(8,128)(2,1)} %pad_maximum_fusion.26), channel_id=1, source_target_pairs={{0,2},{1,3},{2,6},{3,7},{4,0},{5,1},{6,4},{7,5},{8,10},{9,11},{10,... | collective-permute-start | bytes 2359304 | tf_op jit(solution)/shard_map/ppermute | solution.py:57
  147.8 53.4 %collective-permute-start.17 = (bf16[128,3072]{0,1:T(8,128)(2,1)}, bf16[128,3072]{0,1:T(8,128)(2,1)}, u32[]{:S(2)}, u32[]{:S(2)}) collective-permute-start(bf16[128,3072]{0,1:T(8,128)(2,1)} %collective-permute-done.16), channel_id=1, source_target_pairs={{0,8},{1,9},{2,10},{3,11},{4,12},{5,13},{6,14},{7,15},{8,0},{9,1},... | collective-permute-start | bytes 2359304 | tf_op jit(solution)/shard_map/ppermute | solution.py:57
  151.6 50.3 %collective-permute-start.18 = (bf16[128,3072]{0,1:T(8,128)(2,1)}, bf16[128,3072]{0,1:T(8,128)(2,1)}, u32[]{:S(2)}, u32[]{:S(2)}) collective-permute-start(bf16[128,3072]{0,1:T(8,128)(2,1)} %collective-permute-done.16), channel_id=1, source_target_pairs={{0,16},{1,17},{2,18},{3,19},{4,20},{5,21},{6,22},{7,23},{8,24},{9,... | collective-permute-start | bytes 2359304 | tf_op jit(solution)/shard_map/ppermute | solution.py:57
  152.1 101.3 %collective-permute-start.21 = (bf16[128,3072]{0,1:T(8,128)(2,1)}, bf16[128,3072]{0,1:T(8,128)(2,1)}, u32[]{:S(2)}, u32[]{:S(2)}) collective-permute-start(bf16[128,3072]{0,1:T(8,128)(2,1)} %collective-permute-done.20), channel_id=1, source_target_pairs={{0,16},{1,17},{2,18},{3,19},{4,20},{5,21},{6,22},{7,23},{8,24},{9,... | collective-permute-start | bytes 2359304 | tf_op jit(solution)/shard_map/ppermute | solution.py:57
  201.8 37.0 %collective-permute-start.19 = (bf16[128,3072]{0,1:T(8,128)(2,1)}, bf16[128,3072]{0,1:T(8,128)(2,1)S(1)}, u32[]{:S(2)}, u32[]{:S(2)}) collective-permute-start(bf16[128,3072]{0,1:T(8,128)(2,1)} %collective-permute-done.18), channel_id=1, source_target_pairs={{0,8},{1,9},{2,10},{3,11},{4,12},{5,13},{6,14},{7,15},{8,0},{9,1},... | collective-permute-start | bytes 2359304 | tf_op jit(solution)/shard_map/ppermute | solution.py:57
  212.9 83.3 %collective-permute-start.42 = (bf16[128,3072]{0,1:T(8,128)(2,1)}, bf16[128,3072]{0,1:T(8,128)(2,1)}, u32[]{:S(2)}, u32[]{:S(2)}) collective-permute-start(bf16[128,3072]{0,1:T(8,128)(2,1)} %collective-permute-done.41), channel_id=1, source_target_pairs={{0,8},{1,9},{2,10},{3,11},{4,12},{5,13},{6,14},{7,15},{8,0},{9,1},... | collective-permute-start | bytes 2359304 | tf_op jit(solution)/shard_map/ppermute | solution.py:57
  213.6 82.1 %collective-permute-start.43 = (bf16[128,3072]{0,1:T(8,128)(2,1)}, bf16[128,3072]{0,1:T(8,128)(2,1)}, u32[]{:S(2)}, u32[]{:S(2)}) collective-permute-start(bf16[128,3072]{0,1:T(8,128)(2,1)} %collective-permute-done.41), channel_id=1, source_target_pairs={{0,16},{1,17},{2,18},{3,19},{4,20},{5,21},{6,22},{7,23},{8,24},{9,... | collective-permute-start | bytes 2359304 | tf_op jit(solution)/shard_map/ppermute | solution.py:57
  222.0 123.0 %collective-permute-start.46 = (bf16[128,3072]{0,1:T(8,128)(2,1)}, bf16[128,3072]{0,1:T(8,128)(2,1)}, u32[]{:S(2)}, u32[]{:S(2)}) collective-permute-start(bf16[128,3072]{0,1:T(8,128)(2,1)} %collective-permute-done.45), channel_id=1, source_target_pairs={{0,16},{1,17},{2,18},{3,19},{4,20},{5,21},{6,22},{7,23},{8,24},{9,... | collective-permute-start | bytes 2359304 | tf_op jit(solution)/shard_map/ppermute | solution.py:57
  265.3 39.3 %collective-permute-start.47 = (bf16[128,3072]{0,1:T(8,128)(2,1)}, bf16[128,3072]{0,1:T(8,128)(2,1)}, u32[]{:S(2)}, u32[]{:S(2)}) collective-permute-start(bf16[128,3072]{0,1:T(8,128)(2,1)} %collective-permute-done.45), channel_id=1, source_target_pairs={{0,8},{1,9},{2,10},{3,11},{4,12},{5,13},{6,14},{7,15},{8,0},{9,1},... | collective-permute-start | bytes 2359304 | tf_op jit(solution)/shard_map/ppermute | solution.py:57
  304.6 51.6 %collective-permute-start.48 = (bf16[128,3072]{0,1:T(8,128)(2,1)}, bf16[128,3072]{0,1:T(8,128)(2,1)S(1)}, u32[]{:S(2)}, u32[]{:S(2)}) collective-permute-start(bf16[128,3072]{0,1:T(8,128)(2,1)} %collective-permute-done.47), channel_id=1, source_target_pairs={{0,16},{1,17},{2,18},{3,19},{4,20},{5,21},{6,22},{7,23},{8,24},{9,... | collective-permute-start | bytes 2359304 | tf_op jit(solution)/shard_map/ppermute | solution.py:57
  378.9 36.7 %collective-permute-start.94 = (bf16[256,3072]{1,0:T(8,128)(2,1)S(1)}, bf16[256,3072]{1,0:T(8,128)(2,1)S(1)}, u32[]{:S(2)}, u32[]{:S(2)}) collective-permute-start(bf16[256,3072]{1,0:T(8,128)(2,1)S(1)} %get-tuple-element.102), channel_id=1, source_target_pairs={{0,16},{1,17},{2,18},{3,19},{4,20},{5,21},{6,22},{7,23},{8,24},{9,... | collective-permute-start | bytes 4718600 | tf_op jit(solution)/shard_map/ppermute | solution.py:57
  418.4 67.7 %collective-permute-start.98 = (bf16[128,3072]{1,0:T(8,128)(2,1)}, bf16[128,3072]{1,0:T(8,128)(2,1)}, u32[]{:S(2)}, u32[]{:S(2)}) collective-permute-start(bf16[128,3072]{1,0:T(8,128)(2,1)} %slice.1292), channel_id=1, source_target_pairs={{0,16},{1,17},{2,18},{3,19},{4,20},{5,21},{6,22},{7,23},{8,24},{9,... | collective-permute-start | bytes 2359304 | tf_op jit(solution)/shard_map/ppermute | solution.py:57
  420.8 66.6 %collective-permute-start.95 = (bf16[128,3072]{1,0:T(8,128)(2,1)}, bf16[128,3072]{1,0:T(8,128)(2,1)}, u32[]{:S(2)}, u32[]{:S(2)}) collective-permute-start(bf16[128,3072]{1,0:T(8,128)(2,1)} %slice.1288), channel_id=1, source_target_pairs={{0,8},{1,9},{2,10},{3,11},{4,12},{5,13},{6,14},{7,15},{8,0},{9,1},... | collective-permute-start | bytes 2359304 | tf_op jit(solution)/shard_map/ppermute | solution.py:57
  487.3 42.2 %collective-permute-start.99 = (bf16[128,3072]{1,0:T(8,128)(2,1)S(1)}, bf16[128,3072]{1,0:T(8,128)(2,1)S(1)}, u32[]{:S(2)}, u32[]{:S(2)}) collective-permute-start(bf16[128,3072]{1,0:T(8,128)(2,1)S(1)} %add_convert_fusion.4), channel_id=1, source_target_pairs={{0,4},{1,5},{2,0},{3,1},{4,6},{5,7},{6,2},{7,3},{8,12},{9,13},{10,... | collective-permute-start | bytes 2359304 | tf_op jit(solution)/shard_map/ppermute | solution.py:57
  488.8 40.8 %collective-permute-start.96 = (bf16[128,3072]{1,0:T(8,128)(2,1)S(1)}, bf16[128,3072]{1,0:T(8,128)(2,1)S(1)}, u32[]{:S(2)}, u32[]{:S(2)}) collective-permute-start(bf16[128,3072]{1,0:T(8,128)(2,1)S(1)} %add_convert_fusion.5), channel_id=1, source_target_pairs={{0,0},{1,1},{2,4},{3,5},{4,2},{5,3},{6,6},{7,7},{8,8},{9,9},{10,12... | collective-permute-start | bytes 2359304 | tf_op jit(solution)/shard_map/ppermute | solution.py:57
  506.7 48.2 %collective-permute-start.87 = (bf16[128,1024]{0,1:T(8,128)(2,1)S(1)}, bf16[128,1024]{0,1:T(8,128)(2,1)S(1)}, u32[]{:S(2)}, u32[]{:S(2)}) collective-permute-start(bf16[128,1024]{0,1:T(8,128)(2,1)S(1)} %add_convert_fusion.12), channel_id=1, source_target_pairs={{0,4},{1,5},{2,0},{3,1},{4,6},{5,7},{6,2},{7,3},{8,12},{9,13},{10,... | collective-permute-start | bytes 786440 | tf_op jit(solution)/shard_map/ppermute | solution.py:57
  517.7 37.2 %collective-permute-start.84 = (bf16[128,1024]{0,1:T(8,128)(2,1)S(1)}, bf16[128,1024]{0,1:T(8,128)(2,1)S(1)}, u32[]{:S(2)}, u32[]{:S(2)}) collective-permute-start(bf16[128,1024]{0,1:T(8,128)(2,1)S(1)} %add_convert_fusion.13), channel_id=1, source_target_pairs={{0,0},{1,1},{2,4},{3,5},{4,2},{5,3},{6,6},{7,7},{8,8},{9,9},{10,12... | collective-permute-start | bytes 786440 | tf_op jit(solution)/shard_map/ppermute | solution.py:57
  542.4 36.5 %collective-permute-start.88 = (bf16[256,3072]{1,0:T(8,128)(2,1)S(1)}, bf16[256,3072]{1,0:T(8,128)(2,1)S(1)}, u32[]{:S(2)}, u32[]{:S(2)}) collective-permute-start(bf16[256,3072]{1,0:T(8,128)(2,1)S(1)} %get-tuple-element.98), channel_id=1, source_target_pairs={{0,16},{1,17},{2,18},{3,19},{4,20},{5,21},{6,22},{7,23},{8,24},{9,... | collective-permute-start | bytes 4718600 | tf_op jit(solution)/shard_map/ppermute | solution.py:57
  582.4 54.5 %collective-permute-start.92 = (bf16[128,3072]{1,0:T(8,128)(2,1)}, bf16[128,3072]{1,0:T(8,128)(2,1)}, u32[]{:S(2)}, u32[]{:S(2)}) collective-permute-start(bf16[128,3072]{1,0:T(8,128)(2,1)} %slice.1281), channel_id=1, source_target_pairs={{0,16},{1,17},{2,18},{3,19},{4,20},{5,21},{6,22},{7,23},{8,24},{9,... | collective-permute-start | bytes 2359304 | tf_op jit(solution)/shard_map/ppermute | solution.py:57
  584.0 55.2 %collective-permute-start.89 = (bf16[128,3072]{1,0:T(8,128)(2,1)}, bf16[128,3072]{1,0:T(8,128)(2,1)}, u32[]{:S(2)}, u32[]{:S(2)}) collective-permute-start(bf16[128,3072]{1,0:T(8,128)(2,1)} %slice.1277), channel_id=1, source_target_pairs={{0,8},{1,9},{2,10},{3,11},{4,12},{5,13},{6,14},{7,15},{8,0},{9,1},... | collective-permute-start | bytes 2359304 | tf_op jit(solution)/shard_map/ppermute | solution.py:57
  639.2 74.9 %collective-permute-start.93 = (bf16[128,3072]{1,0:T(8,128)(2,1)}, bf16[128,3072]{1,0:T(8,128)(2,1)S(1)}, u32[]{:S(2)}, u32[]{:S(2)}) collective-permute-start(bf16[128,3072]{1,0:T(8,128)(2,1)} %add_convert_fusion.6), channel_id=1, source_target_pairs={{0,4},{1,5},{2,0},{3,1},{4,6},{5,7},{6,2},{7,3},{8,12},{9,13},{10,... | collective-permute-start | bytes 2359304 | tf_op jit(solution)/shard_map/ppermute | solution.py:57
  641.4 72.7 %collective-permute-start.90 = (bf16[128,3072]{1,0:T(8,128)(2,1)}, bf16[128,3072]{1,0:T(8,128)(2,1)}, u32[]{:S(2)}, u32[]{:S(2)}) collective-permute-start(bf16[128,3072]{1,0:T(8,128)(2,1)} %add_convert_fusion.7), channel_id=1, source_target_pairs={{0,0},{1,1},{2,4},{3,5},{4,2},{5,3},{6,6},{7,7},{8,8},{9,9},{10,12... | collective-permute-start | bytes 2359304 | tf_op jit(solution)/shard_map/ppermute | solution.py:57
  658.3 62.9 %collective-permute-start.73 = (bf16[512,256]{1,0:T(8,128)(2,1)S(1)}, bf16[512,256]{1,0:T(8,128)(2,1)}, u32[]{:S(2)}, u32[]{:S(2)}) collective-permute-start(bf16[512,256]{1,0:T(8,128)(2,1)S(1)} %get-tuple-element.128), channel_id=1, source_target_pairs={{0,1},{1,0},{2,3},{3,2},{4,5},{5,4},{6,7},{7,6},{8,9},{9,8},{10,11... | collective-permute-start | bytes 786440 | tf_op jit(solution)/shard_map/ppermute | solution.py:57
  659.8 62.5 %collective-permute-start.81 = (bf16[128,1024]{0,1:T(8,128)(2,1)}, bf16[128,1024]{0,1:T(8,128)(2,1)}, u32[]{:S(2)}, u32[]{:S(2)}) collective-permute-start(bf16[128,1024]{0,1:T(8,128)(2,1)} %add_convert_fusion.14), channel_id=1, source_target_pairs={{0,4},{1,5},{2,0},{3,1},{4,6},{5,7},{6,2},{7,3},{8,12},{9,13},{10,... | collective-permute-start | bytes 786440 | tf_op jit(solution)/shard_map/ppermute | solution.py:57
  668.8 53.6 %collective-permute-start.78 = (bf16[128,1024]{0,1:T(8,128)(2,1)}, bf16[128,1024]{0,1:T(8,128)(2,1)}, u32[]{:S(2)}, u32[]{:S(2)}) collective-permute-start(bf16[128,1024]{0,1:T(8,128)(2,1)} %add_convert_fusion.15), channel_id=1, source_target_pairs={{0,0},{1,1},{2,4},{3,5},{4,2},{5,3},{6,6},{7,7},{8,8},{9,9},{10,12... | collective-permute-start | bytes 786440 | tf_op jit(solution)/shard_map/ppermute | solution.py:57
  (233 other events, 2845.7 us)

commit v2 on v1

v2 whole, which is shorter than its diff:
```python
import functools

import jax
import jax.numpy as jnp
from jax import lax
from jax.experimental import pallas as pl
from jax.experimental.pallas import tpu as pltpu
from jax.sharding import PartitionSpec as P

HD = 64
LAYERS = 2
epsilon = 1e-06
masked = -1e30
F32 = jnp.float32
LOW = jnp.bfloat16
AXES = ("shard", "o", "c", "zh", "zl")


def bits_of(count):
    width = count.bit_length() - 1
    assert 1 << width == count
    return width


def dot(left, right, left_dim, right_dim):
    return lax.dot_general(
        left, right, (((left_dim,), (right_dim,)), ((), ())), preferred_element_type=F32
    )


class Place:
    def __init__(self, mesh):
        self.n_shard = mesh.shape["shard"]
        self.n_o = mesh.shape["o"]
        self.n_ctx = 2 * self.n_o
        assert mesh.shape["zh"] == mesh.shape["zl"] == 2
        self.s_bits = bits_of(self.n_shard)
        self.o_bits = bits_of(self.n_o)
        self.dp = [("s", i) for i in reversed(range(self.s_bits))] + [
            ("o", i) for i in reversed(range(self.o_bits))
        ]

    def locate(self):
        self.zh = lax.axis_index("zh")
        self.zl = lax.axis_index("zl")
        self.s = lax.axis_index("shard")
        self.o = lax.axis_index("o")
        self.c = lax.axis_index("c")
        self.dp_bit = [((self.s if kind == "s" else self.o) >> i) & 1 for kind, i in self.dp]

    def away(self, bits):
        away_s = away_o = 0
        for bit, (kind, i) in zip(bits, self.dp):
            if kind == "s":
                away_s |= bit << i
            else:
                away_o |= bit << i
        return away_s, away_o

    def move(self, array, route):
        pairs = []
        for shard in range(self.n_shard):
            for ctx in range(self.n_ctx):
                for tensor in range(4):
                    s, o, c, zh, zl = route(shard, ctx // 2, ctx % 2, tensor // 2, tensor % 2)
                    source = (shard * self.n_ctx + ctx) * 4 + tensor
                    target = (s * self.n_ctx + 2 * o + c) * 4 + 2 * zh + zl
                    pairs.append((source, target))
        return lax.ppermute(array, AXES, pairs)

    def swap_core(self, array):
        return self.move(array, lambda s, o, c, zh, zl: (s, o, 1 - c, zh, zl))

    def swap_zl(self, array):
        return self.move(array, lambda s, o, c, zh, zl: (s, o, c, zh, 1 - zl))

    def swap_zh(self, array):
        return self.move(array, lambda s, o, c, zh, zl: (s, o, c, 1 - zh, zl))

    def swap_dp(self, array, index):
        kind, i = self.dp[index]
        if kind == "s":
            return self.move(array, lambda s, o, c, zh, zl: (s ^ (1 << i), o, c, zh, zl))
        return self.move(array, lambda s, o, c, zh, zl: (s, o ^ (1 << i), c, zh, zl))

    def near(self, array):
        return self.move(array, lambda s, o, c, zh, zl: (s, o, zh, c, zl))

    def far(self, array):
        return self.move(array, lambda s, o, c, zh, zl: (s, o, zh, 1 - c, zl))

    def far_back(self, array):
        return self.move(array, lambda s, o, c, zh, zl: (s, o, 1 - zh, c, zl))


def flip_if(bit, array, axis):
    return jnp.where(bit == 1, jnp.flip(array, axis), array)


def pick(flag, one, two):
    return jnp.where(flag == 1, one, two)


VMEM = pl.BlockSpec(memory_space=pltpu.VMEM)
SMEM = pl.BlockSpec(memory_space=pltpu.SMEM)
HBM = pl.BlockSpec(memory_space=pl.ANY)
MIB = 1024 * 1024
WORK = {
    "frame": 2,
    "qkv": 5,
    "attend": 8,
    "ffn": 9,
    "ffn_back": 10,
    "ffn_weights": 9,
    "attend_back_far": 9,
    "attend_back_near": 6,
    "qkv_back": 5,
    "attn_weights": 4,
    "leave": 3,
}


def shape(dims, kind):
    return jax.ShapeDtypeStruct(dims, kind)


def launch(body, outs, operands, specs, scratch=(), name=None):
    return pl.pallas_call(
        body,
        out_shape=outs,
        in_specs=specs,
        out_specs=[VMEM] * len(outs),
        scratch_shapes=list(scratch),
        compiler_params=pltpu.CompilerParams(vmem_limit_bytes=52 * MIB),
        cost_estimate=pl.CostEstimate(
            flops=int(WORK[name] * 1.15e9), bytes_accessed=1024, transcendentals=0
        ),
        name=name,
    )(*operands)


def load_rows(pieces, layout, spot, buffer, sems):
    copies = []
    for array, row, count, target, col in layout:
        source = pieces[array].at[pl.ds(pl.multiple_of(row(spot), count), count)]
        here = buffer.at[
            pl.ds(pl.multiple_of(target(spot), count), count),
            pl.ds(col, pieces[array].shape[1]),
        ]
        copies.append(pltpu.make_async_copy(source, here, sems.at[len(copies)]))
    for copy in copies:
        copy.start()
    return copies


def feature_start(spot, dc, dz, width):
    return pl.multiple_of((2 * (spot[0] ^ dc) + (spot[1] ^ dz)) * width, width)


def join_feats(spot, pieces, full):
    width = pieces[0].shape[1]
    for i, piece in enumerate(pieces):
        full[:, pl.ds(feature_start(spot, i // 2, i % 2, width), width)] = piece[...]


def each_rows(total, step, body):
    step = min(step, total)

    def one(i, carry):
        body(pl.ds(pl.multiple_of(i * step, step), step))
        return carry

    lax.fori_loop(0, total // step, one, 0)


def norm_rows(full, gain, normed, scale):
    def one(rows):
        x = full[rows, :].astype(F32)
        r = lax.rsqrt(jnp.mean(x * x, axis=1, keepdims=True) + epsilon)
        scale[rows, :] = r
        normed[rows, :] = (x * r * gain[...]).astype(LOW)

    each_rows(full.shape[0], 128, one)


def finish_back(spot, pieces, before_full, rows_full, scale, moved, full, own):
    width = moved.shape[1]
    depth = full.shape[1]
    join_feats(spot, pieces, full)
    start = feature_start(spot, 0, 0, width)

    def one(rows):
        u = full[rows, :].astype(F32)
        n = rows_full[rows, :].astype(F32) * scale[rows, :]
        dots = jnp.sum((u - before_full[rows, :].astype(F32)) * n, axis=1, keepdims=True)
        dots = dots * (1.0 / depth)
        full[rows, :] = (u - n * dots).astype(LOW)
        mine = rows_full[rows, pl.ds(start, width)].astype(F32) * scale[rows, :]
        own[rows, :] = moved[rows, :] - mine * dots

    each_rows(full.shape[0], 128, one)


def turn(values, cosine, sine):
    width = values.shape[1]
    lane = lax.broadcasted_iota(jnp.int32, values.shape, 1) % HD
    other = jnp.where(
        lane < HD // 2, pltpu.roll(values, width - HD // 2, 1), pltpu.roll(values, HD // 2, 1)
    )
    return values * cosine + other * sine


def store_parts(parts, spot, product, width):
    for i, part in enumerate(parts):
        part[...] = product(feature_start(spot, i // 2, i % 2, width)).astype(part.dtype)


def part_shapes(tokens, width):
    return [
        shape((tokens, width), F32),
        shape((tokens, width), F32),
        shape((tokens, width), LOW),
        shape((tokens, width), LOW),
    ]


def qkv_body(layout, joined, spot, *rest):
    pieces, rest = rest[: 1 if joined else 4], rest[1 if joined else 4 :]
    gain, cosine, sine = rest[:3]
    rest = rest[3:]
    count = 1 + max(entry[0] for entry in layout)
    weights = rest[:count]
    rest = rest[count:]
    if joined:
        full = pieces[0]
    else:
        full, rest = rest[0], rest[1:]
    normed, scale, queries, key_value, buffer, sems = rest
    copies = load_rows(weights, layout, spot, buffer, sems)
    if not joined:
        join_feats(spot, pieces, full)
    norm_rows(full, gain, normed, scale)
    for copy in copies:
        copy.wait()
    width = queries.shape[1]
    for i in range(3):
        product = dot(normed[...], buffer[:, i * width : (i + 1) * width], 1, 0)
        if i < 2:
            product = turn(product, cosine[...], sine[...])
        if i == 0:
            queries[...] = (product * 0.125).astype(LOW)
        else:
            key_value[:, (i - 1) * width : i * width] = product.astype(LOW)


def scores_of(q, k, same, row, step):
    return dot(q, k, 1, 1) + row + jnp.where(same, step, 0.0)


def attend_body(slots, n_blocks, layout, spot, bias, queries, own_kinds, kinds, masks, *rest):
    count = 1 + max(entry[0] for entry in layout)
    blocks = rest[:n_blocks]
    weights = rest[n_blocks : n_blocks + count]
    attended, logs, part0, part1, part2, part3, buffer, sems = rest[n_blocks + count :]
    copies = load_rows(weights, layout, spot, buffer, sems)
    tokens, width = queries.shape
    heads = width // HD
    size = tokens // slots
    wide = 2 * HD
    chunk = min(size, 256)
    side = lax.broadcasted_iota(jnp.int32, (1, wide), 1) // HD
    for slot in range(slots):
        keys = pl.ds(slot * size, size)
        for start in range(0, size, chunk):
            rows = pl.ds(slot * size + start, chunk)
            same = [
                own_kinds[rows, :] == kinds[slot : slot + 1, b * size : (b + 1) * size]
                for b in range(n_blocks)
            ]
            for pair in range(heads // 2):
                cols = slice(pair * wide, (pair + 1) * wide)
                values = slice(width + pair * wide, width + (pair + 1) * wide)
                both = queries[rows, cols]
                results = []
                for half in range(2):
                    head = 2 * pair + half
                    q = jnp.where(side == half, both, jnp.zeros_like(both))
                    step = bias[2 * head] - bias[2 * head + 1]
                    base = bias[2 * head + 1]
                    scores = [
                        scores_of(
                            q,
                            blocks[b][keys, cols],
                            same[b],
                            masks[slot : slot + 1, b * size : (b + 1) * size] + base,
                            step,
                        )
                        for b in range(n_blocks)
                    ]
                    highest = functools.reduce(
                        jnp.maximum, [jnp.max(s, axis=1, keepdims=True) for s in scores]
                    )
                    powers = [jnp.exp(s - highest) for s in scores]
                    total = functools.reduce(
                        lambda a, b: a + b, [jnp.sum(p, axis=1, keepdims=True) for p in powers]
                    )
                    product = functools.reduce(
                        lambda a, b: a + b,
                        [
                            dot(powers[b].astype(LOW), blocks[b][keys, values], 1, 0)
                            for b in range(n_blocks)
                        ],
                    )
                    results.append(product * (1.0 / total))
                    logs[rows, head : head + 1] = highest + jnp.log(total)
                attended[rows, cols] = jnp.where(side == 0, results[0], results[1]).astype(LOW)
    for copy in copies:
        copy.wait()
    share = part0.shape[1]
    last = slice(3 * width, 4 * width)
    store_parts(
        (part0, part1, part2, part3),
        spot,
        lambda start: dot(attended[...], buffer[pl.ds(start, share), last], 1, 1),
        share,
    )


def ffn_body(layout, spot, p0, p1, p2, p3, gain, *rest):
    count = 1 + max(entry[0] for entry in layout)
    weights = rest[:count]
    full, normed, scale, gate, up, hid, part0, part1, part2, part3, buffer, sems = rest[count:]
    copies = load_rows(weights, layout, spot, buffer, sems)
    join_feats(spot, (p0, p1, p2, p3), full)
    norm_rows(full, gain, normed, scale)
    for copy in copies:
        copy.wait()
    hidden = hid.shape[1]
    tile = 256

    def one(i, carry):
        start = pl.multiple_of(i * tile, tile)
        here = pl.ds(start, tile)
        g = dot(normed[...], buffer[:, here], 1, 0)
        u = dot(normed[...], buffer[:, pl.ds(pl.multiple_of(hidden + start, tile), tile)], 1, 0)
        gate[:, here] = g.astype(LOW)
        up[:, here] = u.astype(LOW)
        hid[:, here] = (g * jax.nn.sigmoid(g) * u).astype(LOW)
        return carry

    lax.fori_loop(0, hidden // tile, one, 0)
    share = part0.shape[1]
    store_parts(
        (part0, part1, part2, part3),
        spot,
        lambda start: dot(hid[...], buffer[pl.ds(start, share), 2 * hidden : 3 * hidden], 1, 1),
        share,
    )


def ffn_back_body(finish, layout, spot, *rest):
    count = 1 + max(entry[0] for entry in layout)
    if finish:
        p0, p1, p2, p3, before_full, rows_full, scale, moved = rest[:8]
        rest = rest[8:]
    else:
        full_in = rest[0]
        rest = rest[1:]
    gate, up = rest[:2]
    weights = rest[2 : 2 + count]
    rest = rest[2 + count :]
    if finish:
        full, own = rest[:2]
        rest = rest[2:]
    gate_grad, up_grad, part0, part1, part2, part3, buffer, sems = rest
    copies = load_rows(weights, layout, spot, buffer, sems)
    if finish:
        finish_back(
            spot, (p0, p1, p2, p3), before_full, rows_full, scale, moved, full, own
        )
    else:
        full = full_in
    for copy in copies:
        copy.wait()
    hidden = gate.shape[1]
    tile = 256

    def one(i, carry):
        start = pl.multiple_of(i * tile, tile)
        here = pl.ds(start, tile)
        grad = dot(
            full[...], buffer[:, pl.ds(pl.multiple_of(2 * hidden + start, tile), tile)], 1, 0
        )
        g = gate[:, here].astype(F32)
        sig = jax.nn.sigmoid(g)
        gate_grad[:, here] = (
            grad * up[:, here].astype(F32) * sig * (1.0 + g * (1.0 - sig))
        ).astype(LOW)
        up_grad[:, here] = (grad * g * sig).astype(LOW)
        return carry

    lax.fori_loop(0, hidden // tile, one, 0)
    share = part0.shape[1]
    store_parts(
        (part0, part1, part2, part3),
        spot,
        lambda start: dot(gate_grad[...], buffer[pl.ds(start, share), :hidden], 1, 1)
        + dot(up_grad[...], buffer[pl.ds(start, share), hidden : 2 * hidden], 1, 1),
        share,
    )


def grad_columns(pairs, blocks, operands, rows, out, out_rows):
    col = 0
    for left, right in pairs:
        right = operands[right]
        width = right.shape[1]
        for start in range(0, width, 512):
            tile = min(512, width - start)
            out[out_rows, col : col + tile] = dot(
                blocks[left][:, rows], right[:, start : start + tile], 0, 0
            ).astype(LOW)
            col += tile


def arrange(operands, pairs, spot, order, scratch):
    blocks = {}
    for buffer, left in zip(scratch, sorted({left for left, _ in pairs})):
        width = buffer.shape[1] // len(order)
        for i, block in enumerate(order):
            at = pl.multiple_of(block(spot) * width, width)
            buffer[:, i * width : (i + 1) * width] = operands[left][:, pl.ds(at, width)]
        blocks[left] = buffer
    return blocks


def weight_grad_group_body(pairs, order, fit, spot, *refs):
    operands, (out,) = refs[: len(refs) - 1 - fit], refs[len(refs) - 1 - fit :][:1]
    blocks = arrange(operands, pairs, spot, order, refs[len(refs) - fit :]) if fit else operands
    step = min(256, out.shape[0])
    for start in range(0, out.shape[0], step):
        rows = slice(start, start + step)
        grad_columns(pairs, blocks, operands, rows, out, rows)


def relative_order(k):
    def bits(i):
        return [(i >> (k - 1 - j)) & 1 for j in range(k)]

    first = [(tuple(bits(i)), 0) for i in range(2**k)]
    second = [(tuple(reversed(bits(i))), 1) for i in range(2**k)]
    return first + second


def weight_grad_sent_body(pairs, order, fit, spot, *refs):
    operands, outs = refs[: len(refs) - 4 - fit], refs[len(refs) - 4 - fit :][:4]
    blocks = arrange(operands, pairs, spot, order, refs[len(refs) - fit :]) if fit else operands
    depth = outs[0].shape[0]
    for i, out in zip((1, 3, 0, 2), outs):
        rows = slice(i * depth, (i + 1) * depth)
        grad_columns(pairs, blocks, operands, rows, out, slice(0, depth))


def attend_back_body(
    slots, n_blocks, first_block, first, layout, spot, bias, queries, attended, logs, *rest
):
    count = 1 + max([entry[0] for entry in layout] + [-1])
    own_kinds, kinds, masks = rest[:3]
    blocks = rest[3 : 3 + n_blocks]
    rest = rest[3 + n_blocks :]
    tokens, width = queries.shape
    if first:
        p0, p1, p2, p3, before_full, rows_full, scale, moved = rest[:8]
        weights = rest[8 : 8 + count]
        full, own, out_grad, deltas, query_grad, same_sum = rest[8 + count : 14 + count]
        grads = rest[14 + count : 14 + count + n_blocks]
        buffer, sems = rest[14 + count + n_blocks :]
        copies = load_rows(weights, layout, spot, buffer, sems)
        finish_back(
            spot, (p0, p1, p2, p3), before_full, rows_full, scale, moved, full, own
        )
        for copy in copies:
            copy.wait()
        out_grad[...] = dot(full[...], buffer[:, 3 * width :], 1, 0).astype(LOW)
    else:
        out_grad, deltas, query_before = rest[:3]
        query_grad, same_sum = rest[3:5]
        grads = rest[5 : 5 + n_blocks]
    heads = width // HD
    size = tokens // slots
    wide = 2 * HD
    side = lax.broadcasted_iota(jnp.int32, (1, wide), 1) // HD
    if first:
        for head in range(heads):
            cols = slice(head // 2 * wide, (head // 2 + 1) * wide)
            product = attended[:, cols].astype(F32) * out_grad[:, cols].astype(F32)
            deltas[:, head : head + 1] = jnp.sum(
                jnp.where(side == head % 2, product, 0.0), axis=1, keepdims=True
            )
    same_sum[...] = jnp.zeros_like(same_sum)
    for slot in range(slots):
        keys = pl.ds(slot * size, size)
        for pair in range(heads // 2):
            cols = slice(pair * wide, (pair + 1) * wide)
            values = slice(width + pair * wide, width + (pair + 1) * wide)
            both = queries[keys, cols]
            grad_both = out_grad[keys, cols]
            query_total = None
            for b in range(n_blocks):
                place_b = first_block + b
                these = slice(place_b * size, (place_b + 1) * size)
                same = own_kinds[keys, :] == kinds[slot : slot + 1, these]
                k = blocks[b][keys, cols]
                v = blocks[b][keys, values]
                key_total = value_total = None
                for half in range(2):
                    head = 2 * pair + half
                    q = jnp.where(side == half, both, jnp.zeros_like(both))
                    g = jnp.where(side == half, grad_both, jnp.zeros_like(both))
                    step = bias[2 * head] - bias[2 * head + 1]
                    base = bias[2 * head + 1]
                    scores = scores_of(q, k, same, masks[slot : slot + 1, these] + base, step)
                    soft = jnp.exp(scores - logs[keys, head : head + 1])
                    soft_grad = dot(g, v, 1, 1)
                    score_grad = soft * (soft_grad - deltas[keys, head : head + 1])
                    same_sum[head : head + 1, :] += jnp.sum(
                        jnp.where(same, score_grad, 0.0), axis=0, keepdims=True
                    )
                    low = score_grad.astype(LOW)
                    masked_k = jnp.where(side == half, k, jnp.zeros_like(k))
                    query_part = dot(low, masked_k, 1, 0)
                    key_part = dot(low, q, 0, 0)
                    value_part = dot(soft.astype(LOW), g, 0, 0)
                    query_total = query_part if query_total is None else query_total + query_part
                    key_total = key_part if key_total is None else key_total + key_part
                    value_total = value_part if value_total is None else value_total + value_part
                grads[b][keys, cols] = key_total.astype(grads[b].dtype)
                grads[b][keys, values] = value_total.astype(grads[b].dtype)
            query_total = query_total * 0.125
            if not first:
                query_total = query_total + query_before[keys, cols]
            query_grad[keys, cols] = query_total


def qkv_back_body(layout, n_received, spot, query_grad, key_value, cosine, sine, *rest):
    count = 1 + max(entry[0] for entry in layout)
    received = rest[:n_received]
    weights = rest[n_received : n_received + count]
    three, part0, part1, part2, part3, buffer, sems = rest[n_received + count :]
    copies = load_rows(weights, layout, spot, buffer, sems)
    width = query_grad.shape[1]
    total = key_value[...]
    for other in received:
        total = total + other[...].astype(F32)
    three[:, :width] = turn(query_grad[...], cosine[...], -sine[...]).astype(LOW)
    three[:, width : 2 * width] = turn(total[:, :width], cosine[...], -sine[...]).astype(LOW)
    three[:, 2 * width :] = total[:, width:].astype(LOW)
    for copy in copies:
        copy.wait()
    share = part0.shape[1]
    store_parts(
        (part0, part1, part2, part3),
        spot,
        lambda start: dot(three[...], buffer[pl.ds(start, share), : 3 * width], 1, 1),
        share,
    )


def frame_body(slots, masked_rows, table, spot, mine, other, *rest):
    valid, full = (rest[0], rest[1]) if masked_rows else (None, rest[0])
    positions = mine.shape[2]
    blocks = table.shape[0]
    lanes = full.shape[1] // blocks
    for near in range(2):
        source = mine if near == 0 else other
        for slot in range(slots):
            start = pl.multiple_of((2 * slot + (spot[0] ^ near)) * positions, positions)
            for spot_out in range(blocks):
                block = table[spot_out]
                per = blocks // 4
                quarter = block // per
                which = (2 * ((quarter // 2) ^ spot[2])) + ((quarter % 2) ^ spot[1])
                lane = pl.multiple_of((block % per) * lanes, lanes)
                values = source[which, slot, :, pl.ds(lane, lanes)]
                if masked_rows:
                    values = values * valid[pl.ds(start, positions), :].astype(LOW)
                full[pl.ds(start, positions), spot_out * lanes : (spot_out + 1) * lanes] = values


def unframe(slots, table, spot, full, keep, send):
    positions = keep.shape[1]
    blocks = table.shape[0]
    lanes = full.shape[1] // blocks
    per = blocks // 4
    for away, out in ((0, keep), (1, send)):
        quarter = 2 * (spot[2] ^ away) + spot[1]
        for slot in range(slots):
            start = pl.multiple_of((2 * slot + spot[0]) * positions, positions)
            for i in range(per):
                at = table[quarter * per + i]
                lane = pl.multiple_of(at * lanes, lanes)
                out[slot, :, i * lanes : (i + 1) * lanes] = full[
                    pl.ds(start, positions), pl.ds(lane, lanes)
                ]


def leave_body(slots, finish, fit, spot, table, *rest):
    pieces, rest = rest[:4], rest[4:]
    if finish:
        before_full, rows_full, scale, moved = rest[:4]
        outs, full, own = rest[4:-2], rest[-2], rest[-1]
        finish_back(spot, pieces, before_full, rows_full, scale, moved, full, own)
    else:
        outs, full = rest[:-1], rest[-1]
        join_feats(spot, pieces, full)
    if fit:
        unframe(slots, table, spot, full, *outs)
    else:
        outs[0][...] = full[...]


def after(value, *others):
    return lax.optimization_barrier((value, others))[0]


def take_rows(place, natural, other):
    same = (place.c == place.zh).astype(jnp.int32)
    kept = pick(same, natural, other)
    received = place.swap_core(pick(same, other, natural))
    return pick(same, kept, received), pick(same, received, kept)


def return_rows(place, first, second):
    same = (place.c == place.zh).astype(jnp.int32)
    kept = pick(same, first, second)
    received = place.swap_core(pick(same, second, first))
    return pick(same, kept, received), pick(same, received, kept)


def gather_rows_swap(place, both, waits=()):
    k = len(place.dp)
    pieces, layout, early = [], [], []
    count = both[0].shape[0]
    for side, order in ((0, list(range(k))), (1, list(reversed(range(k))))):
        held, blocks = [both[side]], [(0,) * k]
        for index in order:
            send = held[0] if len(held) == 1 else jnp.concatenate(after(held, *waits), 0)
            held.append(place.swap_dp(send, index))
            if len(held) == 2:
                early.append(held[1])
            blocks += [b[:index] + (1 - b[index],) + b[index + 1 :] for b in blocks]
        at = 0
        for piece in held:
            for row in range(0, piece.shape[0], count):
                target = row_block(place, blocks[at], side)
                layout.append(
                    (
                        len(pieces),
                        lambda spot, row=row: row,
                        count,
                        lambda spot, target=target: target(spot) * count,
                        0,
                    )
                )
                at += 1
            pieces.append(piece)
    return pieces, layout, early


def row_block(place, bits, side):
    away_s, away_o = place.away(bits)
    chips = place.n_o
    return lambda spot: (
        ((spot[3] ^ away_s) * chips + (spot[4] ^ away_o)) * 2 + (spot[2] ^ side)
    )


def gather_rows_group(place, chunks):
    both = jnp.concatenate(
        [jnp.concatenate([chunk[side] for chunk in chunks], 1) for side in range(2)], 0
    )
    rows = lax.all_gather(both, ("shard", "o"), axis=0, tiled=True)
    chips = place.n_shard * place.n_o
    count = rows.shape[0] // (2 * chips)
    layout = [
        (
            0,
            lambda spot, i=i: i * count,
            count,
            lambda spot, i=i: (i - i % 2 + (i % 2 ^ spot[2])) * count,
            0,
        )
        for i in range(2 * chips)
    ]
    return [rows], layout


def join_chunks(*chunks):
    arrays, layout, column = [], [], 0
    for pieces, lay in chunks:
        layout += [(a + len(arrays), row, count, target, column) for a, row, count, target, _ in lay]
        arrays = arrays + pieces
        column += pieces[0].shape[1]
    return arrays, layout


def scatter_rows_group(place, partial):
    rows = lax.psum_scatter(partial, ("shard", "o"), scatter_dimension=0, tiled=True)
    half = rows.shape[0] // 2
    return rows[:half], rows[half:]


def scatter_start(place, sent, other_sent):
    return place.swap_dp(sent, 0), place.swap_dp(other_sent, len(place.dp) - 1)


def scatter_rest(place, received, kept, waits=()):
    k = len(place.dp)
    ends = []
    for got, keep, order in (
        (received[0], kept[0], list(range(k))),
        (received[1], kept[1], list(reversed(range(k)))),
    ):
        part = (keep.astype(F32) + got.astype(F32)).astype(LOW)
        for index in order[1:]:
            middle = part.shape[0] // 2
            got = place.swap_dp(after(part[middle:], *waits), index)
            part = (part[:middle].astype(F32) + got.astype(F32)).astype(LOW)
        ends.append(part)
    return ends


def gather_feats(place, share):
    other = place.swap_zl(share)
    return [share, other, place.swap_core(share), place.swap_core(other)]


def scatter_feats(place, parts, beside=None):
    kept, kept_pair, sent, sent_pair = parts
    middle = (kept_pair + place.swap_core(sent_pair).astype(F32)).astype(LOW)
    near = kept + place.swap_core(sent).astype(F32)
    received = place.swap_zl(middle)
    done = None if beside is None else beside(middle)
    return near + after(received, done).astype(F32), done


def gather_keys(place, own):
    pieces = [own]
    for index in reversed(range(place.s_bits, len(place.dp))):
        pieces = pieces + [place.swap_dp(piece, index) for piece in pieces]
    return pieces


def per_device(place):
    def run(
        inputs,
        w_query,
        w_key,
        w_value,
        w_out,
        w_gate,
        w_up,
        w_down,
        attn_gain,
        ffn_gain,
        variate_bias,
        lengths,
        variates,
        cotangent,
    ):
        place.locate()
        positions, slots, quarter = inputs.shape
        depth = quarter * 4
        half_slots = slots // 2
        block = 2 * positions
        n_o = place.n_ctx // 2
        tokens = half_slots * block
        width = w_query.shape[2]
        heads = width // HD
        hidden = w_gate.shape[2]
        own_quarter = 2 * place.c + place.zl
        spot = jnp.stack([place.c, place.zl, place.zh, place.s, place.o]).astype(jnp.int32)
        k = len(place.dp)
        n_blocks = 2 ** (k + 1)
        block_rows = depth // n_blocks
        table = jnp.arange(n_blocks, dtype=jnp.int32)
        block_rows = depth // n_blocks
        lanes_fit = block_rows % 128 == 0

        attn_packs = [
            jnp.concatenate([w_query[i], w_key[i], w_value[i], w_out[i].T], 1)
            for i in range(LAYERS)
        ]

        def swap_slots(natural):
            first, second = natural[:, :half_slots], natural[:, half_slots:]
            return place.swap_zh(pick(place.zh, first, second).transpose(1, 0, 2))

        def token_quarters(natural, received):
            first, second = natural[:, :half_slots], natural[:, half_slots:]
            own = pick(place.zh, second, first).transpose(1, 0, 2)
            two = jnp.stack([own, received])
            other = place.swap_zl(two)
            mine = jnp.stack([two, other], 1).reshape(4, half_slots, positions, quarter)
            return mine, place.swap_core(mine), other

        def token_rows(quarters, valid):
            mine, other = quarters[:2]
            if lanes_fit:
                operands = [table, spot, mine, other] + ([] if valid is None else [valid])
                return launch(
                    functools.partial(frame_body, half_slots, valid is not None),
                    [shape((tokens, depth), LOW)],
                    operands,
                    [SMEM, SMEM] + [VMEM] * (len(operands) - 2),
                    name="frame",
                )[0]
            by_core = jnp.stack([pick(place.c, other, mine), pick(place.c, mine, other)], 0)
            cut = by_core.reshape(2, 2, 2, half_slots, positions, quarter)
            cut = flip_if(place.zl, flip_if(place.zh, cut, 1), 2)
            rows = cut.transpose(3, 0, 4, 1, 2, 5).reshape(tokens, depth)
            return rows if valid is None else rows * valid.astype(LOW)

        def natural_rows(pieces, pending=()):
            outs = [shape((half_slots, positions, quarter), LOW)] * 2
            scratch = [pltpu.VMEM((tokens, depth), LOW)]
            if pending:
                scratch.append(pltpu.VMEM((tokens, quarter), F32))
            outs = launch(
                functools.partial(leave_body, half_slots, bool(pending), lanes_fit),
                outs if lanes_fit else [shape((tokens, depth), LOW)],
                [spot, table, *pieces, *pending],
                [SMEM] * 2 + [VMEM] * (4 + len(pending)),
                scratch,
                name="leave",
            )
            if lanes_fit:
                keep, send = outs
            else:
                cut = outs[0].reshape(
                    half_slots, 2, positions, 2, 2, quarter
                )
                cut = pick(place.c, cut[:, 1], cut[:, 0])
                cut = pick(place.zl, cut[:, :, :, 1], cut[:, :, :, 0])
                keep = pick(place.zh, cut[:, :, 1], cut[:, :, 0])
                send = pick(place.zh, cut[:, :, 0], cut[:, :, 1])
            received = place.swap_zh(send)
            both = jnp.concatenate(
                [pick(place.zh, received, keep), pick(place.zh, keep, received)], 0
            )
            return both.transpose(1, 0, 2)

        zh_done = swap_slots(inputs)
        mine, other, zl_done = token_quarters(inputs, zh_done)
        small = jnp.concatenate(
            [attn_gain.reshape(-1), ffn_gain.reshape(-1), variate_bias.reshape(-1)]
        ).reshape(1, -1)
        small = after(small, zh_done)
        pair = jnp.stack([small, place.swap_zh(small)], 0)
        all_small = jnp.stack([pair, place.swap_zl(pair)], 2)
        all_small = flip_if(place.zl, flip_if(place.zh, all_small, 0), 2)
        small = all_small.reshape(4, -1)
        cut = LAYERS * quarter
        natural_gains = jnp.concatenate(
            [
                small[:, i * cut : (i + 1) * cut]
                .reshape(4, LAYERS, quarter)
                .transpose(1, 0, 2)
                .reshape(LAYERS, depth)
                for i in range(2)
            ]
        )
        gains = natural_gains
        biases = lax.dynamic_index_in_dim(
            small[:, 2 * cut :].reshape(4, LAYERS, 2 * heads), own_quarter, 0, keepdims=False
        )

        ffn_chunks = [(w_gate[i], w_up[i], w_down[i].T) for i in range(LAYERS)]

        def take_late(natural, start, use):
            natural = after(natural, start)
            return take_rows(place, natural, after(place.swap_zh(natural), use))

        attn_both = take_late(attn_packs[0], zh_done, zh_done)
        gate = after(ffn_chunks[0][0], attn_both)
        gate_other = place.swap_zh(gate)
        *first_attn, early = gather_rows_swap(place, attn_both)
        up = after(ffn_chunks[0][1], early)
        up_other = place.swap_zh(up)

        own_kinds = after(variates.astype(F32), zl_done)
        rest = place.swap_core(own_kinds)
        own_kinds = jnp.concatenate(
            [pick(place.c, rest, own_kinds), pick(place.c, own_kinds, rest)], 0
        )
        own_kinds = pick(place.zh, own_kinds[:, half_slots:], own_kinds[:, :half_slots]).T
        kinds = jnp.concatenate(gather_keys(place, own_kinds), 1)
        own_kinds = own_kinds.reshape(tokens, 1)
        own_lengths = pick(place.zh, lengths[half_slots:], lengths[:half_slots])
        own_positions = place.o * block + jnp.arange(block, dtype=jnp.int32)
        chips = jnp.arange(n_o, dtype=jnp.int32) ^ place.o
        key_positions = (
            chips[:, None] * block + jnp.arange(block, dtype=jnp.int32)[None, :]
        ).reshape(-1)
        masks = jnp.where(key_positions[None, :] < own_lengths[:, None], 0.0, masked).astype(F32)
        valid = (own_positions[None, :] < own_lengths[:, None]).astype(F32).reshape(tokens, 1)
        index = jnp.arange(width, dtype=jnp.int32) % HD
        inverse = 10000.0 ** (-(2.0 * (index % (HD // 2)).astype(F32)) / HD)
        angles = own_positions.astype(F32)[:, None] * inverse[None, :]
        cosine = jnp.tile(jnp.cos(angles), (half_slots, 1))
        sine = jnp.tile(
            jnp.where(index < HD // 2, -1.0, 1.0)[None, :] * jnp.sin(angles), (half_slots, 1)
        )

        def share_of(rows):
            return lax.dynamic_slice_in_dim(rows, own_quarter * quarter, quarter, -1)

        attn_buffer = [
            pltpu.VMEM((depth, 4 * width), LOW),
            pltpu.SemaphoreType.DMA((n_blocks,)),
        ]
        ffn_buffer = [
            pltpu.VMEM((depth, 3 * hidden), LOW),
            pltpu.SemaphoreType.DMA((2 * n_blocks,)),
        ]
        rows_low = shape((tokens, depth), LOW)
        column = shape((tokens, 1), F32)
        share_f32 = shape((tokens, quarter), F32)
        parts = part_shapes(tokens, quarter)

        if lanes_fit:
            full = launch(
                functools.partial(frame_body, half_slots, False),
                [rows_low],
                [table, spot, mine, other],
                [SMEM, SMEM, VMEM, VMEM],
                name="frame",
            )[0]
        else:
            by_core = jnp.stack([pick(place.c, other, mine), pick(place.c, mine, other)], 0)
            cut4 = by_core.reshape(2, 2, 2, half_slots, positions, quarter)
            cut4 = flip_if(place.zl, flip_if(place.zh, cut4, 1), 2)
            full = cut4.transpose(3, 0, 4, 1, 2, 5).reshape(tokens, depth)

        pieces = [full]
        current = share_of(full).astype(F32)
        kept, weights = [], []
        attn_w, attn_lay = first_attn
        nothing = ()
        for layer in range(LAYERS):
            first, more = layer == 0, layer + 1 < LAYERS
            outs = launch(
                functools.partial(qkv_body, attn_lay, layer == 0),
                ([] if layer == 0 else [rows_low])
                + [
                    rows_low,
                    column,
                    shape((tokens, width), LOW),
                    shape((tokens, 2 * width), LOW),
                ],
                [spot, *pieces, gains[layer : layer + 1], cosine, sine, *attn_w],
                [SMEM] + [VMEM] * (3 + len(pieces)) + [HBM] * len(attn_w),
                attn_buffer,
                name="qkv",
            )
            if layer > 0:
                full, outs = outs[0], outs[1:]
            normed, scale, queries, key_value = outs
            blocks = gather_keys(place, key_value)
            if first:
                gate_both = take_rows(place, gate, after(gate_other, key_value))
                up_both = take_rows(place, up, after(up_other, key_value))
                down = after(ffn_chunks[0][2], key_value)
                down_other = place.swap_zh(down)
                blocks = after(blocks, down_other, gate_both, up_both)
                gate_up = gather_rows_group(place, after((gate_both, up_both), blocks))
            if layer == LAYERS - 1:
                late_cotangent = after(cotangent, key_value)
                cotangent_quarters = token_quarters(late_cotangent, swap_slots(late_cotangent))
                upstream_full = token_rows(cotangent_quarters, valid)
                blocks = after(blocks, upstream_full)
            if more:
                attn_next = after(attn_packs[layer + 1], blocks)
                attn_other = place.swap_zh(attn_next)
            attended, logs, *sums = launch(
                functools.partial(attend_body, half_slots, n_o, attn_lay),
                [shape((tokens, width), LOW), shape((tokens, heads), F32), *parts],
                [spot, biases[layer], queries, own_kinds, kinds, masks, *blocks, *attn_w],
                [SMEM] * 2 + [VMEM] * (4 + n_o) + [HBM] * len(attn_w),
                attn_buffer,
                name="attend",
            )
            if more:
                sums = after(sums, attn_other)
                chunks = ffn_chunks[layer + 1]
                others = [place.swap_zh(after(chunks[0], sums))]
            if first:
                down_both = take_rows(place, down, after(down_other, attended))

            def reduce_side(sent):
                return list(others) if more else []

            shared, _ = scatter_feats(place, sums, reduce_side)
            middle = current + shared
            if first:
                down_w, down_lay, early = gather_rows_swap(place, down_both, (middle,))
            mid_pieces = gather_feats(place, middle.astype(LOW))
            if more:
                others.append(place.swap_zh(after(chunks[1], middle)))
                attn_both = take_rows(place, attn_next, after(attn_other, middle))
                mid_pieces = after(mid_pieces, others[1], attn_both)
            if first:
                mid_pieces = after(mid_pieces, down_w)
                ffn_w, ffn_lay = join_chunks(gate_up, (down_w, down_lay))
            if more:
                others.append(place.swap_zh(after(chunks[2], mid_pieces)))
                next_w, next_lay, early = gather_rows_swap(
                    place, after(attn_both, mid_pieces, ffn_w), nothing
                )
            full_mid, normed_mid, scale_mid, gate, up, hid, *sums = launch(
                functools.partial(ffn_body, ffn_lay),
                [
                    rows_low,
                    rows_low,
                    column,
                    *[shape((tokens, hidden), LOW)] * 3,
                    *parts,
                ],
                [
                    spot,
                    *mid_pieces,
                    gains[LAYERS + layer : LAYERS + layer + 1],
                    *ffn_w,
                ],
                [SMEM] + [VMEM] * 5 + [HBM] * len(ffn_w),
                ffn_buffer,
                name="ffn",
            )
            weights.append((attn_w, attn_lay, ffn_w, ffn_lay))
            if more:
                sums = after(sums, early)

            def take_side(sent):
                return [
                    take_rows(place, chunk, after(other, sent))
                    for chunk, other in zip(chunks, others)
                ]

            shared, ffn_both = scatter_feats(place, sums, take_side if more else None)
            if more:
                attn_w, attn_lay = next_w, next_lay
                ffn_w, ffn_lay = gather_rows_group(place, ffn_both)
            current = middle + shared
            kept.append(
                (
                    full,
                    normed,
                    scale,
                    queries,
                    blocks,
                    attended,
                    logs,
                    full_mid,
                    normed_mid,
                    scale_mid,
                    gate,
                    up,
                    hid,
                )
            )
            pieces = gather_feats(place, current.astype(LOW))

        last = pieces
        natural_valid = (
            ((2 * place.o + place.c) * positions + jnp.arange(positions, dtype=jnp.int32))[:, None]
            < lengths[None, :]
        )

        upstream = share_of(upstream_full).astype(F32)

        def step_back(sums, full_rows, row_scale, gain, before, beside):
            shared, done = scatter_feats(place, sums, beside)
            own_rows = share_of(full_rows).astype(F32) * row_scale
            gain_grad = jnp.sum(shared * own_rows, 0)
            moved = before + row_scale * (shared * share_of(gain)[None, :])
            return moved, gather_feats(place, moved.astype(LOW)), gain_grad, done

        sent_order = [row_block(place, bits, side) for bits, side in relative_order(k)]
        group_order = [
            lambda spot, i=i: i - i % 2 + (i % 2 ^ spot[2]) for i in range(n_blocks)
        ]

        def weight_grads_of(swapped, pairs, operands, columns, name, ready):
            operands = after(operands, ready)
            lefts = sorted({left for left, _ in pairs})
            order = sent_order if swapped else group_order
            scratch = []
            if lanes_fit:
                scratch = [pltpu.VMEM((tokens, depth), LOW) for _ in lefts]
            else:
                index = jnp.stack([block(spot) for block in order])
                operands = [
                    jnp.take(array.reshape(tokens, n_blocks, block_rows), index, axis=1).reshape(
                        tokens, depth
                    )
                    if i in lefts
                    else array
                    for i, array in enumerate(operands)
                ]
            return launch(
                functools.partial(
                    weight_grad_sent_body if swapped else weight_grad_group_body,
                    pairs,
                    order,
                    len(scratch),
                ),
                [shape((depth // 4, columns), LOW)] * 4
                if swapped
                else [shape((depth, columns), LOW)],
                [spot, *operands],
                [SMEM] + [VMEM] * len(operands),
                scratch,
                name=name,
            )

        weight_grads = [None] * LAYERS

        def keep_grads(layer, ffn_out, attn_out):
            attn_out, ffn_out = attn_out.astype(F32), ffn_out.astype(F32)
            weight_grads[layer] = (
                attn_out[:, :width],
                attn_out[:, width : 2 * width],
                attn_out[:, 2 * width : 3 * width],
                attn_out[:, 3 * width :].T,
                ffn_out[:, :hidden],
                ffn_out[:, hidden : 2 * hidden],
                ffn_out[:, 2 * hidden :].T,
            )

        late = None
        gain_grads = [None] * LAYERS
        bias_grads = [None] * LAYERS
        half_keys = max(n_o // 2, 1)
        pending = None
        for layer in reversed(range(LAYERS)):
            attn_w, attn_lay, ffn_w, ffn_lay = weights[layer]
            (
                full,
                normed,
                scale,
                queries,
                blocks,
                attended,
                logs,
                full_mid,
                normed_mid,
                scale_mid,
                gate,
                up,
                hid,
            ) = kept[layer]
            hidden_low = shape((tokens, hidden), LOW)
            if pending is None:
                gate_grad, up_grad, *sums = launch(
                    functools.partial(ffn_back_body, False, ffn_lay),
                    [hidden_low, hidden_low, *parts],
                    [spot, upstream_full, gate, up, *ffn_w],
                    [SMEM] + [VMEM] * 3 + [HBM] * len(ffn_w),
                    ffn_buffer,
                    name="ffn_back",
                )
            else:
                upstream_full, upstream, gate_grad, up_grad, *sums = launch(
                    functools.partial(ffn_back_body, True, ffn_lay),
                    [rows_low, share_f32, hidden_low, hidden_low, *parts],
                    [spot, *pending, gate, up, *ffn_w],
                    [SMEM] + [VMEM] * 10 + [HBM] * len(ffn_w),
                    ffn_buffer,
                    name="ffn_back",
                )
            if layer == LAYERS - 1:
                output = natural_rows(last)
                sums = after(sums, output)
                output = output * natural_valid[:, :, None].astype(LOW)
            if late is not None:
                late_ffn, late_got, late_kept = late
                sums = after(sums, late_got)
            ffn_grads = functools.partial(
                weight_grads_of,
                False,
                ((0, 1), (0, 2), (3, 4)),
                [normed_mid, gate_grad, up_grad, upstream_full, hid],
                3 * hidden,
                "ffn_weights",
            )

            def ffn_side(sent):
                partial = ffn_grads(sent)
                if late is None:
                    return partial, None
                ends = scatter_rest(place, after(late_got, sent), late_kept)
                return after(partial, ends), ends

            moved, pieces, ffn_gain_grad, (ffn_partial, late_ends) = step_back(
                sums, full_mid, scale_mid, gains[LAYERS + layer], upstream, ffn_side
            )
            ffn_rows = scatter_rows_group(place, *ffn_partial)
            if late is not None:
                own_ffn, other_ffn = return_rows(place, *after(late_ffn, moved))
                pieces = after(pieces, other_ffn)
                others = [
                    place.swap_zh(after(other_ffn[:, :hidden], pieces)),
                ]
            common = [queries, attended, logs, own_kinds, kinds, masks]
            later = blocks[half_keys:] if n_o > 1 else blocks
            early = blocks[:half_keys] if n_o > 1 else []
            start = half_keys if n_o > 1 else 0
            middle_full, middle, out_grad, deltas, query_grad, same_sum, *sent = launch(
                functools.partial(
                    attend_back_body, half_slots, len(later), start, True, attn_lay
                ),
                [
                    rows_low,
                    share_f32,
                    shape((tokens, width), LOW),
                    shape((tokens, heads), F32),
                    shape((tokens, width), F32),
                    shape((heads, block), F32),
                    *[shape((tokens, 2 * width), LOW)] * len(later),
                ],
                [
                    spot,
                    biases[layer],
                    *common,
                    *later,
                    *pieces,
                    upstream_full,
                    full_mid,
                    scale_mid,
                    moved,
                    *attn_w,
                ],
                [SMEM] * 2 + [VMEM] * (6 + len(later) + 8) + [HBM] * len(attn_w),
                attn_buffer,
                name="attend_back_far",
            )
            if late is not None:
                out_grad = after(out_grad, others[0])
                others.append(place.swap_zh(after(other_ffn[:, hidden : 2 * hidden], out_grad)))
                own_attn, other_attn = return_rows(place, *after(late_ends, out_grad))
            query_grad, same_sum_near, *near = launch(
                functools.partial(attend_back_body, half_slots, len(early), 0, False, []),
                [
                    shape((tokens, width), F32),
                    shape((heads, block), F32),
                    *[shape((tokens, 2 * width), F32)] * len(early),
                ],
                [spot, biases[layer], *common, *early, out_grad, deltas, query_grad],
                [SMEM] * 2 + [VMEM] * (6 + len(early) + 3),
                name="attend_back_near",
            )
            same_total = jnp.sum(same_sum, 1) + jnp.sum(same_sum_near, 1)
            bias_grads[layer] = jnp.stack([same_total, -same_total], 1)
            received = [place.swap_dp(piece, place.s_bits) for piece in sent]
            for index in range(place.s_bits + 1, k):
                near = [a + b.astype(F32) for a, b in zip(near, received)]
                middle_at = len(near) // 2
                received = [
                    place.swap_dp(piece.astype(LOW), index) for piece in near[middle_at:]
                ]
                near = near[:middle_at]
            if late is not None:
                received = after(received, others[1], other_attn)
                others.append(place.swap_zh(after(other_ffn[:, 2 * hidden :], received)))
            three, *sums = launch(
                functools.partial(qkv_back_body, attn_lay, 1),
                [shape((tokens, 3 * width), LOW), *parts],
                [spot, query_grad, near[0], cosine, sine, received[0], *attn_w],
                [SMEM] + [VMEM] * 5 + [HBM] * len(attn_w),
                attn_buffer,
                name="qkv_back",
            )
            if late is not None:
                sums = after(sums, others[2])
                others.append(place.swap_zh(after(other_attn, sums)))
            attn_grads = functools.partial(
                weight_grads_of,
                True,
                ((0, 1), (2, 3)),
                [normed, three, middle_full, attended],
                4 * width,
                "attn_weights",
            )

            def attn_side(sent):
                partial = attn_grads(sent)
                if late is None:
                    return partial, None
                rows = return_rows(place, *after(ffn_rows, sent))
                return after(partial, rows), rows

            moved, pieces, attn_gain_grad, (attn_partial, last_rows) = step_back(
                sums, full, scale, gains[layer], middle, attn_side
            )
            pending = [*pieces, middle_full, full, scale, moved]
            gain_grads[layer] = (attn_gain_grad, ffn_gain_grad)
            if late is not None:
                last_own, last_other = last_rows
                last_sent = [place.swap_zh(after(last_other[:, :hidden], moved))]
                pieces = after(pieces, others[3])
                last_sent += [
                    place.swap_zh(after(last_other[:, i * hidden : (i + 1) * hidden], pieces))
                    for i in range(1, 3)
                ]
                keep_grads(
                    layer + 1,
                    own_ffn.astype(F32) + jnp.concatenate(others[:3], 1).astype(F32),
                    own_attn.astype(F32) + others[3].astype(F32),
                )
            sent, other_sent, *attn_kept = after(attn_partial, moved)
            late = (ffn_rows, scatter_start(place, sent, other_sent), attn_kept)

        mine = jnp.stack([gain_grads[layer][i] for i in range(2) for layer in range(LAYERS)])
        wide = lax.dynamic_update_slice_in_dim(
            jnp.zeros((2 * LAYERS, depth), F32), mine, own_quarter * quarter, 1
        )
        bias_wide = lax.dynamic_update_slice_in_dim(
            jnp.zeros((LAYERS, 4 * heads, 2), F32), jnp.stack(bias_grads), own_quarter * heads, 1
        )
        total = jnp.concatenate([wide.reshape(-1), bias_wide.reshape(-1)])
        total = after(total, *pending)
        total = total + place.swap_core(total)
        for i in range(k):
            total = total + place.swap_dp(total, i)
        total = total + place.swap_zl(total)
        total_zh = place.swap_zh(total)
        input_grad = natural_rows(pending[:4], pending[4:]).astype(F32)
        total = total + total_zh
        own_attn, other_attn = return_rows(place, *scatter_rest(place, *late[1:]))
        attn_out = own_attn.astype(F32) + place.swap_zh(other_attn).astype(F32)
        ffn_out = last_own.astype(F32) + jnp.concatenate(last_sent, 1).astype(F32)
        keep_grads(0, ffn_out, attn_out)
        wide = total[: wide.size].reshape(wide.shape)
        bias_wide = total[wide.size :].reshape(bias_wide.shape)
        tensor = 2 * place.zh + place.zl
        gains_out = lax.dynamic_slice_in_dim(wide, tensor * quarter, quarter, 1)
        bias_out = lax.dynamic_slice_in_dim(bias_wide, tensor * heads, heads, 1)
        stacks = [
            jnp.stack([weight_grads[layer][member] for layer in range(LAYERS)])
            for member in range(7)
        ]
        return (output, input_grad, *stacks, gains_out[:LAYERS], gains_out[LAYERS:], bias_out)

    return run


def solution(mesh):
    n_ctx = mesh.shape["ctx"]
    dims = (mesh.shape["shard"], n_ctx // 2, 2, 2, mesh.shape["tensor"] // 2)
    mesh = jax.sharding.Mesh(mesh.devices.reshape(dims), AXES)
    ctx, tensor = ("o", "c"), ("zh", "zl")
    column = P(None, ("shard", "o", "c"), tensor)
    row = P(None, tensor, ("shard", "o", "c"))
    tokens = P(ctx, "shard", tensor)
    gain = P(None, tensor)
    bias = P(None, tensor, None)
    return jax.shard_map(
        per_device(Place(mesh)),
        mesh=mesh,
        in_specs=(
            tokens, column, column, column, row, column, column, row,
            gain, gain, bias, P("shard"), P(ctx, "shard"), tokens,
        ),
        out_specs=(
            tokens, tokens, column, column, column, row, column, column, row, gain, gain, bias,
        ),
        check_vma=False,
    )
```

time: 753 us -> 648 us (0.86)
  Pallas kernels: 0 us -> 140 us
  waiting for transfers between devices: 216 us -> 315 us
  matrix products: 85.9 us -> 0 us
  local copies, waits for them, and re-layouts: 113 us -> 32.8 us
  starting transfers between devices: 158 us -> 82.4 us
  blocking collectives: 73.1 us -> 0 us
  other arithmetic: 89.8 us -> 52.8 us
  between operations: 6.94 us -> 17.5 us
    pallas_call x0 -> x22, Pallas kernels: none -> 140 us  [launch(): pl.pallas_call(body, out_shape=outs, in_specs=specs, out_specs=[VMEM] * l...]
    ppermute x100 -> x117, waiting for transfers between devices: 216 us -> 314 us  [move(): return lax.ppermute(array, AXES, pairs)]
    dot_general x72 -> x0, matrix products: 85.9 us -> none  [the longest x24 38.3 us: dot(): lax.dot_general(left, right, (((left_dim,), (right_dim,)), ((), ())), pre...]
    ppermute x100 -> x117, starting transfers between devices: 158 us -> 81.9 us  [move(): return lax.ppermute(array, AXES, pairs)]
    unnamed x391 -> x230, local copies, waits for them, and re-layouts: 70.9 us -> 15.3 us
    psum x1 -> x0, blocking collectives: 40.3 us -> none  [run(): wide, bias_wide = lax.psum((wide, bias_wide), AXES)]
    unnamed x1 -> x0, blocking collectives: 27.7 us -> none
    reduce_sum x19 -> x4, other arithmetic: 17.3 us -> 0.48 us  [run(): same_total = jnp.sum(same_sum, 1) + jnp.sum(same_sum_near, 1)]
  transfers between devices with their start and end apart: 100 -> 121, of which waited for: 40 -> 62; matrix products, arithmetic and copies ran while one was open for 33% -> 11% of each run, Pallas kernels for 0% -> 18%
where the time goes in v2:
time: 648 us; the launch traced here: 641 us
  waiting for transfers between devices  315 us (49%)
  Pallas kernels  140 us (22%)
  starting transfers between devices  82.4 us (13%)
  other arithmetic  52.8 us (8%)
  local copies, waits for them, and re-layouts  32.8 us (5%)
  between operations  17.5 us (3%)
    ppermute x117, waiting for transfers between devices, move(): return lax.ppermute(array, AXES, pairs)  314 us
    pallas_call x22, Pallas kernels, launch(): pl.pallas_call(body, out_shape=outs, in_specs=specs, out_specs=[VMEM] * l...  140 us
    ppermute x117, starting transfers between devices, move(): return lax.ppermute(array, AXES, pairs)  81.9 us
    unnamed x230, local copies, waits for them, and re-layouts  15.3 us
  transfers between devices with their start and end apart: 121, of which 62 were waited for; matrix products, arithmetic and copies ran while one was open for 11% of the time, Pallas kernels for 18%

profile of v2, /device:TPU:0, one launch (start us, length us, event | category | flops | bytes accessed | tf_op | source)
XLA Modules:
  0.0 640.9 jit_solution(2151297756057434501)
XLA Ops:
  25.8 9.1 %collective-permute-done.4 = f32[2,1,1040]{2,1,0:T(1,128)S(1)} collective-permute-done((f32[2,1,1040]{2,1,0:T(1,128)S(1)}, f32[2,1,1040]{2,1,0:T(1,128)S(1)}, u32[]{:S(2)}, u32[]{:S(2)}) %collective-permute-start.4) | collective-permute-done | bytes 8352 | tf_op jit(solution)/shard_map/ppermute | solution.py:69
  78.3 11.9 %collective-permute-done.14 = bf16[128,1024]{1,0:T(8,128)(2,1)S(1)} collective-permute-done((bf16[128,1024]{1,0:T(8,128)(2,1)S(1)}, bf16[128,1024]{1,0:T(8,128)(2,1)S(1)}, u32[]{:S(2)}, u32[]{:S(2)}) %collective-permute-start.14) | collective-permute-done | bytes 262176 | tf_op jit(solution)/shard_map/ppermute | solution.py:69
  99.2 8.1 %attend.2 = (bf16[512,256]{1,0:T(8,128)(2,1)S(1)}, f32[512,4]{1,0:T(8,128)S(1)}, f32[512,256]{1,0:T(8,128)}, f32[512,256]{1,0:T(8,128)}, bf16[512,256]{1,0:T(8,128)(2,1)S(1)}, /*index=5*/bf16[512,256]{1,0:T(8,128)(2,1)S(1)}) custom-call(s32[5]{0:T(128)S(1)} %stack.168.spot, f32[8]{0:T(128)S(1)} %get-tuple-element.628.bias, ...), custom_call_target="tpu_custom_call" | custom-call | flops 9200000000 | bytes 1024 | tf_op jit(solution)/shard_map/attend/pallas_call | solution.py:128
  119.8 7.4 %collective-permute-done.23 = bf16[128,1024]{1,0:T(8,128)(2,1)S(1)} collective-permute-done((bf16[128,1024]{1,0:T(8,128)(2,1)}, bf16[128,1024]{1,0:T(8,128)(2,1)S(1)}, u32[]{:S(2)}, u32[]{:S(2)}) %collective-permute-start.23) | collective-permute-done | bytes 262176 | tf_op jit(solution)/shard_map/ppermute | solution.py:69
  140.3 13.1 %collective-permute-done.27 = bf16[128,1024]{1,0:T(8,128)(2,1)S(1)} collective-permute-done((bf16[128,1024]{1,0:T(8,128)(2,1)S(1)}, bf16[128,1024]{1,0:T(8,128)(2,1)S(1)}, u32[]{:S(2)}, u32[]{:S(2)}) %collective-permute-start.27) | collective-permute-done | bytes 262176 | tf_op jit(solution)/shard_map/ppermute | solution.py:69
  161.9 9.0 %ffn.2 = (bf16[512,1024]{1,0:T(8,128)(2,1)}, bf16[512,1024]{1,0:T(8,128)(2,1)}, f32[512,1]{1,0:T(8,128)S(1)}, bf16[512,1024]{1,0:T(8,128)(2,1)}, bf16[512,1024]{...) custom-call(s32[5]{0:T(128)S(1)} %stack.168.spot, ...), custom_call_target="tpu_custom_call" | custom-call | flops 10350000128 | bytes 1024 | tf_op jit(solution)/shard_map/ffn/pallas_call | solution.py:128
  178.6 8.9 %collective-permute-done.41 = bf16[128,1024]{1,0:T(8,128)(2,1)S(1)} collective-permute-done((bf16[128,1024]{1,0:T(8,128)(2,1)S(1)}, bf16[128,1024]{1,0:T(8,128)(2,1)S(1)}, u32[]{:S(2)}, u32[]{:S(2)}) %collective-permute-start.41) | collective-permute-done | bytes 262176 | tf_op jit(solution)/shard_map/ppermute | solution.py:69
  200.1 7.0 %collective-permute-done.43.rest_1_ = bf16[512,256]{1,0:T(8,128)(2,1)S(1)} collective-permute-done((bf16[512,256]{1,0:T(8,128)(2,1)S(1)}, bf16[512,256]{1,0:T(8,128)(2,1)S(1)}, u32[]{:S(2)}, u32[]{:S(2)}) %collective-permute-start.43) | collective-permute-done | bytes 262176 | tf_op jit(solution)/shard_map/ppermute | solution.py:69
  227.5 6.4 collective-permute-done.50
  237.9 22.0 %collective-permute-done.48.rest_1_.rest_3_ = bf16[512,512]{1,0:T(8,128)(2,1)S(1)} collective-permute-done((bf16[512,512]{1,0:T(8,128)(2,1)S(1)}, bf16[512,512]{1,0:T(8,128)(2,1)S(1)}, u32[]{:S(2)}, u32[]{:S(2)}) %collective-permute-start.48) | collective-permute-done | bytes 524320 | tf_op jit(solution)/shard_map/ppermute | solution.py:69
  260.7 7.9 %attend.3 = (bf16[512,256]{1,0:T(8,128)(2,1)S(1)}, f32[512,4]{1,0:T(8,128)S(1)}, f32[512,256]{1,0:T(8,128)}, f32[512,256]{1,0:T(8,128)}, bf16[512,256]{1,0:T(8,128)(2,1)S(1)}, /*index=5*/bf16[512,256]{1,0:T(8,128)(2,1)S(1)}) custom-call(s32[5]{0:T(128)S(1)} %stack.168.spot, f32[8]{0:T(128)S(1)} %get-tuple-element.629.bias, ...), custom_call_target="tpu_custom_call" | custom-call | flops 9200000000 | bytes 1024 | tf_op jit(solution)/shard_map/attend/pallas_call | solution.py:128
  271.6 8.1 %collective-permute-done.54 = bf16[512,256]{1,0:T(8,128)(2,1)S(1)} collective-permute-done((bf16[512,256]{1,0:T(8,128)(2,1)S(1)}, bf16[512,256]{1,0:T(8,128)(2,1)S(1)}, u32[]{:S(2)}, u32[]{:S(2)}) %collective-permute-start.54) | collective-permute-done | bytes 262176 | tf_op jit(solution)/shard_map/ppermute | solution.py:69
  282.1 7.2 %collective-permute-done.55.p1 = bf16[512,256]{1,0:T(8,128)(2,1)S(1)} collective-permute-done((bf16[512,256]{1,0:T(8,128)(2,1)S(1)}, bf16[512,256]{1,0:T(8,128)(2,1)S(1)}, u32[]{:S(2)}, u32[]{:S(2)}) %collective-permute-start.55) | collective-permute-done | bytes 262176 | tf_op jit(solution)/shard_map/ppermute | solution.py:69
  290.9 9.5 %ffn.3 = (bf16[512,1024]{1,0:T(8,128)(2,1)}, bf16[512,1024]{1,0:T(8,128)(2,1)}, f32[512,1]{1,0:T(8,128)S(1)}, bf16[512,1024]{1,0:T(8,128)(2,1)}, bf16[512,1024]{...) custom-call(s32[5]{0:T(128)S(1)} %stack.168.spot, ...), custom_call_target="tpu_custom_call" | custom-call | flops 10350000128 | bytes 1024 | tf_op jit(solution)/shard_map/ffn/pallas_call | solution.py:128
  300.4 9.7 %ffn_back.2 = (bf16[512,1024]{1,0:T(8,128)(2,1)}, bf16[512,1024]{1,0:T(8,128)(2,1)}, f32[512,256]{1,0:T(8,128)S(1)}, f32[512,256]{1,0:T(8,128)S(1)}, bf16[512,25...) custom-call(s32[5]{0:T(128)S(1)} %stack.168.spot, bf16[512,1024]{1,0:T(8,128)(2,1)} %frame.3.rest_0_.refs_3_.rest_8_, ...), custom_call_target="tpu_custom_call" | custom-call | flops 11500000256 | bytes 1024 | tf_op jit(solution)/shard_map/ffn_back/pallas_call | solution.py:128
  312.5 8.9 %ffn_weights.2 = bf16[1024,3072]{1,0:T(8,128)(2,1)} custom-call(s32[5]{0:T(128)S(1)} %stack.168.spot, bf16[512,1024]{1,0:T(8,128)(2,1)S(1)} %copy-done.19, bf16[512,1024]{1,0:T(8,128)(2,1)} %get-tuple-element.342.refs_1_, bf16[512,1024]{1,0:T(8,128)(2,1)} %get-tuple-element.343.refs_2_, bf16[512,1024]{1,0:T(8,128)(2,1)} %frame.3.rest_0_.refs_3_.rest_8_, ...), custom_call_target="tpu_custom_call" | custom-call | flops 10350000128 | bytes 1024 | tf_op jit(solution)/shard_map/ffn_weights/pallas_call | solution.py:128
  322.2 8.0 %collective-permute-done.67 = bf16[512,256]{1,0:T(8,128)(2,1)} collective-permute-done((bf16[512,256]{1,0:T(8,128)(2,1)}, bf16[512,256]{1,0:T(8,128)(2,1)}, u32[]{:S(2)}, u32[]{:S(2)}) %collective-permute-start.67) | collective-permute-done | bytes 262176 | tf_op jit(solution)/shard_map/ppermute | solution.py:69
  332.9 7.1 %collective-permute-done.68.rest_5_ = bf16[512,256]{1,0:T(8,128)(2,1)S(1)} collective-permute-done((bf16[512,256]{1,0:T(8,128)(2,1)S(1)}, bf16[512,256]{1,0:T(8,128)(2,1)S(1)}, u32[]{:S(2)}, u32[]{:S(2)}) %collective-permute-start.68) | collective-permute-done | bytes 262176 | tf_op jit(solution)/shard_map/ppermute | solution.py:69
  342.2 9.3 %attend_back_far.2 = (bf16[512,1024]{1,0:T(8,128)(2,1)}, f32[512,256]{1,0:T(8,128)}, bf16[512,256]{1,0:T(8,128)(2,1)S(1)}, f32[512,4]{1,0:T(8,128)S(1)}, f32[512...) custom-call(s32[5]{0:T(128)S(1)} %stack.168.spot, f32[8]{0:T(128)S(1)} %get-tuple-element.629.bias, ...), custom_call_target="tpu_custom_call" | custom-call | flops 10350000128 | bytes 1024 | tf_op jit(solution)/shard_map/attend_back_far/pallas_call | solution.py:128
  352.1 6.2 attend_back_near.2
  358.3 15.6 %collective-permute-done.71.rest_0_ = bf16[512,512]{1,0:T(8,128)(2,1)S(1)} collective-permute-done((bf16[512,512]{1,0:T(8,128)(2,1)}, bf16[512,512]{1,0:T(8,128)(2,1)S(1)}, u32[]{:S(2)}, u32[]{:S(2)}) %collective-permute-start.71) | collective-permute-done | bytes 524320 | tf_op jit(solution)/shard_map/ppermute | solution.py:69
  402.3 11.2 %ffn_back.3 = (bf16[512,1024]{1,0:T(8,128)(2,1)}, f32[512,256]{1,0:T(8,128)}, bf16[512,1024]{1,0:T(8,128)(2,1)}, bf16[512,1024]{1,0:T(8,128)(2,1)}, f32[512,256]...) custom-call(s32[5]{0:T(128)S(1)} %stack.168.spot, ...), custom_call_target="tpu_custom_call" | custom-call | flops 11500000256 | bytes 1024 | tf_op jit(solution)/shard_map/ffn_back/pallas_call | solution.py:128
  420.7 8.8 %ffn_weights.3 = bf16[1024,3072]{1,0:T(8,128)(2,1)} custom-call(s32[5]{0:T(128)S(1)} %stack.168.spot, bf16[512,1024]{1,0:T(8,128)(2,1)S(1)} %copy-done.18, bf16[512,1024]{1,0:T(8,128)(2,1)} %get-tuple-element.393.refs_1_, bf16[512,1024]{1,0:T(8,128)(2,1)} %get-tuple-element.394.refs_2_, bf16[512,1024]{1,0:T(8,128)(2,1)} %get-tuple-element.395.refs_3_.rest_8_, ...), custom_call_target="tpu_custom_call" | custom-call | flops 10350000128 | bytes 1024 | tf_op jit(solution)/shard_map/ffn_weights/pallas_call | solution.py:128
  435.1 6.7 %collective-permute-done.60 = bf16[512,256]{1,0:T(8,128)(2,1)S(1)} collective-permute-done((bf16[512,256]{1,0:T(8,128)(2,1)S(1)}, bf16[512,256]{1,0:T(8,128)(2,1)S(1)}, u32[]{:S(2)}, u32[]{:S(2)}) %collective-permute-start.60) | collective-permute-done | bytes 262176 | tf_op jit(solution)/shard_map/ppermute | solution.py:69
  468.7 7.0 %collective-permute-done.85.rest_5_ = bf16[512,256]{1,0:T(8,128)(2,1)S(1)} collective-permute-done((bf16[512,256]{1,0:T(8,128)(2,1)S(1)}, bf16[512,256]{1,0:T(8,128)(2,1)S(1)}, u32[]{:S(2)}, u32[]{:S(2)}) %collective-permute-start.85) | collective-permute-done | bytes 262176 | tf_op jit(solution)/shard_map/ppermute | solution.py:69
  480.5 9.7 %attend_back_far.3 = (bf16[512,1024]{1,0:T(8,128)(2,1)}, f32[512,256]{1,0:T(8,128)}, bf16[512,256]{1,0:T(8,128)(2,1)S(1)}, f32[512,4]{1,0:T(8,128)S(1)}, f32[512...) custom-call(s32[5]{0:T(128)S(1)} %stack.168.spot, f32[8]{0:T(128)S(1)} %get-tuple-element.628.bias, ...), custom_call_target="tpu_custom_call" | custom-call | flops 10350000128 | bytes 1024 | tf_op jit(solution)/shard_map/attend_back_far/pallas_call | solution.py:128
  501.8 9.8 %collective-permute-done.90.rest_0_ = bf16[512,512]{1,0:T(8,128)(2,1)} collective-permute-done((bf16[512,512]{1,0:T(8,128)(2,1)}, bf16[512,512]{1,0:T(8,128)(2,1)}, u32[]{:S(2)}, u32[]{:S(2)}) %collective-permute-start.90) | collective-permute-done | bytes 524320 | tf_op jit(solution)/shard_map/ppermute | solution.py:69
  519.0 7.2 %collective-permute-done.93 = bf16[128,1024]{1,0:T(8,128)(2,1)S(1)} collective-permute-done((bf16[128,1024]{1,0:T(8,128)(2,1)}, bf16[128,1024]{1,0:T(8,128)(2,1)S(1)}, u32[]{:S(2)}, u32[]{:S(2)}) %collective-permute-start.93) | collective-permute-done | bytes 262176 | tf_op jit(solution)/shard_map/ppermute | solution.py:69
  551.0 7.0 %collective-permute-done.98.rest_1_ = bf16[512,256]{1,0:T(8,128)(2,1)S(1)} collective-permute-done((bf16[512,256]{1,0:T(8,128)(2,1)S(1)}, bf16[512,256]{1,0:T(8,128)(2,1)S(1)}, u32[]{:S(2)}, u32[]{:S(2)}) %collective-permute-start.98) | collective-permute-done | bytes 262176 | tf_op jit(solution)/shard_map/ppermute | solution.py:69
  563.9 11.2 %collective-permute-done.113 = f32[4160]{0:T(1024)S(1)} collective-permute-done((f32[4160]{0:T(1024)S(1)}, f32[4160]{0:T(1024)S(1)}, u32[]{:S(2)}, u32[]{:S(2)}) %collective-permute-start.113) | collective-permute-done | bytes 16672 | tf_op jit(solution)/shard_map/ppermute | solution.py:69
  595.0 11.4 %collective-permute-done.111 = bf16[128,1024]{1,0:T(8,128)(2,1)} collective-permute-done((bf16[128,1024]{1,0:T(8,128)(2,1)}, bf16[128,1024]{1,0:T(8,128)(2,1)}, u32[]{:S(2)}, u32[]{:S(2)}) %collective-permute-start.111) | collective-permute-done | bytes 262176 | tf_op jit(solution)/shard_map/ppermute | solution.py:69
  619.1 11.5 %collective-permute-done.107 = bf16[128,1024]{1,0:T(8,128)(2,1)S(1)} collective-permute-done((bf16[128,1024]{1,0:T(8,128)(2,1)S(1)}, bf16[128,1024]{1,0:T(8,128)(2,1)S(1)}, u32[]{:S(2)}, u32[]{:S(2)}) %collective-permute-start.107) | collective-permute-done | bytes 262176 | tf_op jit(solution)/shard_map/ppermute | solution.py:69
  (636 shorter events, 321.7 us)
Async XLA Ops:
  7.2 152.6 %all-gather.3.cloned.1.call-start = ((), (), s32[]{:S(2)}) async-start(), calls=%async_computation.2 | async-start | bytes 5242880 | tf_op jit(solution)/shard_map/all_gather | solution.py:682
  19.6 23.1 %collective-permute-start.1 = (bf16[2,1,256,256]{3,2,1,0:T(8,128)(2,1)S(1)}, bf16[2,1,256,256]{3,2,1,0:T(8,128)(2,1)S(1)}, u32[]{:S(2)}, u32[]{:S(2)}) collective-permute-start(bf16[2,1,256,256]{3,2,1,0:T(8,128)(2,1)S(1)} %get-tuple-element.599), channel_id=1, source_target_pairs={{0,1},{1,0},{2,3},{3,2},{4,5},{5,4},{6,7},{7,6},{8,9},{9,8},{10,11... | collective-permute-start | bytes 786440 | tf_op jit(solution)/shard_map/ppermute | solution.py:69
  23.6 14.2 %collective-permute-start.5 = (bf16[128,1024]{1,0:T(8,128)(2,1)S(1)}, bf16[128,1024]{1,0:T(8,128)(2,1)S(1)}, u32[]{:S(2)}, u32[]{:S(2)}) collective-permute-start(bf16[128,1024]{1,0:T(8,128)(2,1)S(1)} %pad_maximum_fusion.12), channel_id=1, source_target_pairs={{0,2},{1,3},{2,0},{3,1},{4,6},{5,7},{6,4},{7,5},{8,10},{9,11},{10,... | collective-permute-start | bytes 786440 | tf_op jit(solution)/shard_map/ppermute | solution.py:69
  51.8 18.2 %collective-permute-start.15 = (bf16[128,1024]{1,0:T(8,128)(2,1)S(1)}, bf16[128,1024]{1,0:T(8,128)(2,1)S(1)}, u32[]{:S(2)}, u32[]{:S(2)}) collective-permute-start(bf16[128,1024]{1,0:T(8,128)(2,1)S(1)} %get-tuple-element.252), channel_id=1, source_target_pairs={{0,2},{1,3},{2,0},{3,1},{4,6},{5,7},{6,4},{7,5},{8,10},{9,11},{10,... | collective-permute-start | bytes 786440 | tf_op jit(solution)/shard_map/ppermute | solution.py:69
  52.1 23.4 %collective-permute-start.17 = (bf16[128,1024]{1,0:T(8,128)(2,1)S(1)}, bf16[128,1024]{1,0:T(8,128)(2,1)S(1)}, u32[]{:S(2)}, u32[]{:S(2)}) collective-permute-start(bf16[128,1024]{1,0:T(8,128)(2,1)S(1)} %get-tuple-element.254), channel_id=1, source_target_pairs={{0,2},{1,3},{2,0},{3,1},{4,6},{5,7},{6,4},{7,5},{8,10},{9,11},{10,... | collective-permute-start | bytes 786440 | tf_op jit(solution)/shard_map/ppermute | solution.py:69
  68.5 21.7 %collective-permute-start.13 = (bf16[512,512]{1,0:T(8,128)(2,1)}, bf16[512,512]{1,0:T(8,128)(2,1)}, u32[]{:S(2)}, u32[]{:S(2)}) collective-permute-start(bf16[512,512]{1,0:T(8,128)(2,1)} %get-tuple-element.256.rest_0_.rest_3_), channel_id=1, source_target_pairs={{0,8},{1,9},{2,10},{3,11},{4,12},{5,13},{6,14},{7,15},{8,0},{9,1},... | collective-permute-start | bytes 1572872 | tf_op jit(solution)/shard_map/ppermute | solution.py:69
  91.3 199.6 %all-gather.5.cloned.1.call-start = ((), (), s32[]{:S(2)}) async-start(), calls=%async_computation.3 | async-start | bytes 7864320 | tf_op jit(solution)/shard_map/all_gather | solution.py:682
  116.2 14.1 %collective-permute-start.22 = (bf16[512,256]{1,0:T(8,128)(2,1)}, bf16[512,256]{1,0:T(8,128)(2,1)S(1)}, u32[]{:S(2)}, u32[]{:S(2)}) collective-permute-start(bf16[512,256]{1,0:T(8,128)(2,1)} %add_convert_fusion.16), channel_id=1, source_target_pairs={{0,1},{1,0},{2,3},{3,2},{4,5},{5,4},{6,7},{7,6},{8,9},{9,8},{10,11... | collective-permute-start | bytes 786440 | tf_op jit(solution)/shard_map/ppermute | solution.py:69
  118.1 14.4 %collective-permute-start.30 = (bf16[128,1024]{1,0:T(8,128)(2,1)S(1)}, bf16[128,1024]{1,0:T(8,128)(2,1)S(1)}, u32[]{:S(2)}, u32[]{:S(2)}) collective-permute-start(bf16[128,1024]{1,0:T(8,128)(2,1)S(1)} %get-tuple-element.277.rest_1_.rest_11_), channel_id=1, source_target_pairs={{0,16},{1,17},{2,18},{3,19},{4,20},{5,21},{6,22},{7,23},{8,24},{9,... | collective-permute-start | bytes 786440 | tf_op jit(solution)/shard_map/ppermute | solution.py:69
  118.7 14.5 %collective-permute-start.32 = (bf16[128,1024]{1,0:T(8,128)(2,1)S(1)}, bf16[128,1024]{1,0:T(8,128)(2,1)S(1)}, u32[]{:S(2)}, u32[]{:S(2)}) collective-permute-start(bf16[128,1024]{1,0:T(8,128)(2,1)S(1)} %get-tuple-element.279.rest_4_.rest_14_), channel_id=1, source_target_pairs={{0,8},{1,9},{2,10},{3,11},{4,12},{5,13},{6,14},{7,15},{8,0},{9,1},... | collective-permute-start | bytes 786440 | tf_op jit(solution)/shard_map/ppermute | solution.py:69
  132.6 25.9 %collective-permute-start.31 = (bf16[256,1024]{1,0:T(8,128)(2,1)S(1)}, bf16[256,1024]{1,0:T(8,128)(2,1)S(1)}, u32[]{:S(2)}, u32[]{:S(2)}) collective-permute-start(bf16[256,1024]{1,0:T(8,128)(2,1)S(1)} %pad_maximum_fusion.6), channel_id=1, source_target_pairs={{0,8},{1,9},{2,10},{3,11},{4,12},{5,13},{6,14},{7,15},{8,0},{9,1},... | collective-permute-start | bytes 1572872 | tf_op jit(solution)/shard_map/ppermute | solution.py:69
  133.3 26.0 %collective-permute-start.33 = (bf16[256,1024]{1,0:T(8,128)(2,1)S(1)}, bf16[256,1024]{1,0:T(8,128)(2,1)}, u32[]{:S(2)}, u32[]{:S(2)}) collective-permute-start(bf16[256,1024]{1,0:T(8,128)(2,1)S(1)} %pad_maximum_fusion.7), channel_id=1, source_target_pairs={{0,16},{1,17},{2,18},{3,19},{4,20},{5,21},{6,22},{7,23},{8,24},{9,... | collective-permute-start | bytes 1572872 | tf_op jit(solution)/shard_map/ppermute | solution.py:69
  172.6 14.9 %collective-permute-start.41 = (bf16[128,1024]{1,0:T(8,128)(2,1)S(1)}, bf16[128,1024]{1,0:T(8,128)(2,1)S(1)}, u32[]{:S(2)}, u32[]{:S(2)}) collective-permute-start(bf16[128,1024]{1,0:T(8,128)(2,1)S(1)} %bitcast.201), channel_id=1, source_target_pairs={{0,2},{1,3},{2,0},{3,1},{4,6},{5,7},{6,4},{7,5},{8,10},{9,11},{10,... | collective-permute-start | bytes 786440 | tf_op jit(solution)/shard_map/ppermute | solution.py:69
  190.5 274.8 %reduce-scatter.3.cloned.1.call-start = ((), (), s32[]{:S(2)}) async-start(), calls=%async_computation.4 | async-start | bytes 7864320 | tf_op jit(solution)/shard_map/reduce_scatter | solution.py:708
  191.4 18.3 %collective-permute-start.46 = (bf16[256,1024]{1,0:T(8,128)(2,1)S(1)}, bf16[256,1024]{1,0:T(8,128)(2,1)S(1)}, u32[]{:S(2)}, u32[]{:S(2)}) collective-permute-start(bf16[256,1024]{1,0:T(8,128)(2,1)S(1)} %pad_maximum_fusion.8), channel_id=1, source_target_pairs={{0,8},{1,9},{2,10},{3,11},{4,12},{5,13},{6,14},{7,15},{8,0},{9,1},... | collective-permute-start | bytes 1572872 | tf_op jit(solution)/shard_map/ppermute | solution.py:69
  192.9 20.0 %collective-permute-start.47 = (bf16[256,1024]{1,0:T(8,128)(2,1)S(1)}, bf16[256,1024]{1,0:T(8,128)(2,1)S(1)}, u32[]{:S(2)}, u32[]{:S(2)}) collective-permute-start(bf16[256,1024]{1,0:T(8,128)(2,1)S(1)} %pad_maximum_fusion.9), channel_id=1, source_target_pairs={{0,16},{1,17},{2,18},{3,19},{4,20},{5,21},{6,22},{7,23},{8,24},{9,... | collective-permute-start | bytes 1572872 | tf_op jit(solution)/shard_map/ppermute | solution.py:69
  234.0 25.9 %collective-permute-start.48 = (bf16[512,512]{1,0:T(8,128)(2,1)S(1)}, bf16[512,512]{1,0:T(8,128)(2,1)S(1)}, u32[]{:S(2)}, u32[]{:S(2)}) collective-permute-start(bf16[512,512]{1,0:T(8,128)(2,1)S(1)} %copy-done.94), channel_id=1, source_target_pairs={{0,8},{1,9},{2,10},{3,11},{4,12},{5,13},{6,14},{7,15},{8,0},{9,1},... | collective-permute-start | bytes 1572872 | tf_op jit(solution)/shard_map/ppermute | solution.py:69
  321.4 208.1 %reduce-scatter.5.cloned.1.call-start = ((), (), s32[]{:S(2)}) async-start(), calls=%async_computation.5 | async-start | bytes 7864320 | tf_op jit(solution)/shard_map/reduce_scatter | solution.py:708
  351.5 22.3 %collective-permute-start.71 = (bf16[512,512]{1,0:T(8,128)(2,1)}, bf16[512,512]{1,0:T(8,128)(2,1)S(1)}, u32[]{:S(2)}, u32[]{:S(2)}) collective-permute-start(bf16[512,512]{1,0:T(8,128)(2,1)} %get-tuple-element.355), channel_id=1, source_target_pairs={{0,8},{1,9},{2,10},{3,11},{4,12},{5,13},{6,14},{7,15},{8,0},{9,1},... | collective-permute-start | bytes 1572872 | tf_op jit(solution)/shard_map/ppermute | solution.py:69
  400.3 14.3 %collective-permute-start.78 = (bf16[256,1024]{1,0:T(8,128)(2,1)S(1)}, bf16[256,1024]{1,0:T(8,128)(2,1)S(1)}, u32[]{:S(2)}, u32[]{:S(2)}) collective-permute-start(bf16[256,1024]{1,0:T(8,128)(2,1)S(1)} %get-tuple-element.381), channel_id=1, source_target_pairs={{0,16},{1,17},{2,18},{3,19},{4,20},{5,21},{6,22},{7,23},{8,24},{9,... | collective-permute-start | bytes 1572872 | tf_op jit(solution)/shard_map/ppermute | solution.py:69
  478.2 14.8 %collective-permute-start.89 = (bf16[128,1024]{1,0:T(8,128)(2,1)S(1)}, bf16[128,1024]{1,0:T(8,128)(2,1)S(1)}, u32[]{:S(2)}, u32[]{:S(2)}) collective-permute-start(bf16[128,1024]{1,0:T(8,128)(2,1)S(1)} %get-tuple-element.413), channel_id=1, source_target_pairs={{0,2},{1,3},{2,0},{3,1},{4,6},{5,7},{6,4},{7,5},{8,10},{9,11},{10,... | collective-permute-start | bytes 786440 | tf_op jit(solution)/shard_map/ppermute | solution.py:69
  490.3 21.3 %collective-permute-start.90 = (bf16[512,512]{1,0:T(8,128)(2,1)}, bf16[512,512]{1,0:T(8,128)(2,1)}, u32[]{:S(2)}, u32[]{:S(2)}) collective-permute-start(bf16[512,512]{1,0:T(8,128)(2,1)} %get-tuple-element.419), channel_id=1, source_target_pairs={{0,8},{1,9},{2,10},{3,11},{4,12},{5,13},{6,14},{7,15},{8,0},{9,1},... | collective-permute-start | bytes 1572872 | tf_op jit(solution)/shard_map/ppermute | solution.py:69
  493.0 18.6 %collective-permute-start.91 = (bf16[128,1024]{1,0:T(8,128)(2,1)}, bf16[128,1024]{1,0:T(8,128)(2,1)}, u32[]{:S(2)}, u32[]{:S(2)}) collective-permute-start(bf16[128,1024]{1,0:T(8,128)(2,1)} %get-tuple-element.420), channel_id=1, source_target_pairs={{0,2},{1,3},{2,0},{3,1},{4,6},{5,7},{6,4},{7,5},{8,10},{9,11},{10,... | collective-permute-start | bytes 786440 | tf_op jit(solution)/shard_map/ppermute | solution.py:69
  511.6 14.7 %collective-permute-start.93 = (bf16[128,1024]{1,0:T(8,128)(2,1)}, bf16[128,1024]{1,0:T(8,128)(2,1)S(1)}, u32[]{:S(2)}, u32[]{:S(2)}) collective-permute-start(bf16[128,1024]{1,0:T(8,128)(2,1)} %get-tuple-element.428), channel_id=1, source_target_pairs={{0,2},{1,3},{2,0},{3,1},{4,6},{5,7},{6,4},{7,5},{8,10},{9,11},{10,... | collective-permute-start | bytes 786440 | tf_op jit(solution)/shard_map/ppermute | solution.py:69
  526.5 21.2 %collective-permute-start.94 = (bf16[512,256]{1,0:T(8,128)(2,1)S(1)}, bf16[512,256]{1,0:T(8,128)(2,1)}, u32[]{:S(2)}, u32[]{:S(2)}) collective-permute-start(bf16[512,256]{1,0:T(8,128)(2,1)S(1)} %get-tuple-element.430), channel_id=1, source_target_pairs={{0,4},{1,5},{2,6},{3,7},{4,0},{5,1},{6,2},{7,3},{8,12},{9,13},{10,... | collective-permute-start | bytes 786440 | tf_op jit(solution)/shard_map/ppermute | solution.py:69
  527.1 30.9 %collective-permute-start.108 = (bf16[128,1024]{1,0:T(8,128)(2,1)}, bf16[128,1024]{1,0:T(8,128)(2,1)}, u32[]{:S(2)}, u32[]{:S(2)}) collective-permute-start(bf16[128,1024]{1,0:T(8,128)(2,1)} %broadcast_select_fusion.10), channel_id=1, source_target_pairs={{0,2},{1,3},{2,0},{3,1},{4,6},{5,7},{6,4},{7,5},{8,10},{9,11},{10,... | collective-permute-start | bytes 786440 | tf_op jit(solution)/shard_map/ppermute | solution.py:69
  560.6 19.5 %collective-permute-start.102 = (bf16[256,1024]{1,0:T(8,128)(2,1)S(1)}, bf16[256,1024]{1,0:T(8,128)(2,1)S(1)}, u32[]{:S(2)}, u32[]{:S(2)}) collective-permute-start(bf16[256,1024]{1,0:T(8,128)(2,1)S(1)} %get-tuple-element.454), channel_id=1, source_target_pairs={{0,16},{1,17},{2,18},{3,19},{4,20},{5,21},{6,22},{7,23},{8,24},{9,... | collective-permute-start | bytes 1572872 | tf_op jit(solution)/shard_map/ppermute | solution.py:69
  563.6 21.4 %collective-permute-start.104 = (bf16[256,1024]{1,0:T(8,128)(2,1)S(1)}, bf16[256,1024]{1,0:T(8,128)(2,1)S(1)}, u32[]{:S(2)}, u32[]{:S(2)}) collective-permute-start(bf16[256,1024]{1,0:T(8,128)(2,1)S(1)} %get-tuple-element.456), channel_id=1, source_target_pairs={{0,8},{1,9},{2,10},{3,11},{4,12},{5,13},{6,14},{7,15},{8,0},{9,1},... | collective-permute-start | bytes 1572872 | tf_op jit(solution)/shard_map/ppermute | solution.py:69
  563.9 31.2 %collective-permute-start.109 = (bf16[128,1024]{1,0:T(8,128)(2,1)}, bf16[128,1024]{1,0:T(8,128)(2,1)S(1)}, u32[]{:S(2)}, u32[]{:S(2)}) collective-permute-start(bf16[128,1024]{1,0:T(8,128)(2,1)} %get-tuple-element.458), channel_id=1, source_target_pairs={{0,2},{1,3},{2,0},{3,1},{4,6},{5,7},{6,4},{7,5},{8,10},{9,11},{10,... | collective-permute-start | bytes 786440 | tf_op jit(solution)/shard_map/ppermute | solution.py:69
  587.6 18.9 %collective-permute-start.111 = (bf16[128,1024]{1,0:T(8,128)(2,1)}, bf16[128,1024]{1,0:T(8,128)(2,1)}, u32[]{:S(2)}, u32[]{:S(2)}) collective-permute-start(bf16[128,1024]{1,0:T(8,128)(2,1)} %get-tuple-element.464), channel_id=1, source_target_pairs={{0,2},{1,3},{2,0},{3,1},{4,6},{5,7},{6,4},{7,5},{8,10},{9,11},{10,... | collective-permute-start | bytes 786440 | tf_op jit(solution)/shard_map/ppermute | solution.py:69
  591.2 20.6 %collective-permute-start.110 = (bf16[128,1024]{1,0:T(8,128)(2,1)}, bf16[128,1024]{1,0:T(8,128)(2,1)S(1)}, u32[]{:S(2)}, u32[]{:S(2)}) collective-permute-start(bf16[128,1024]{1,0:T(8,128)(2,1)} %get-tuple-element.463), channel_id=1, source_target_pairs={{0,2},{1,3},{2,0},{3,1},{4,6},{5,7},{6,4},{7,5},{8,10},{9,11},{10,... | collective-permute-start | bytes 786440 | tf_op jit(solution)/shard_map/ppermute | solution.py:69
  595.0 20.5 %collective-permute-start.106 = (bf16[128,1024]{1,0:T(8,128)(2,1)}, bf16[128,1024]{1,0:T(8,128)(2,1)}, u32[]{:S(2)}, u32[]{:S(2)}) collective-permute-start(bf16[128,1024]{1,0:T(8,128)(2,1)} %broadcast_select_fusion.8), channel_id=1, source_target_pairs={{0,4},{1,5},{2,6},{3,7},{4,0},{5,1},{6,2},{7,3},{8,12},{9,13},{10,... | collective-permute-start | bytes 786440 | tf_op jit(solution)/shard_map/ppermute | solution.py:69
  (192 other events, 2060.6 us)
Sparse Core Ops, SparseCore 0:
  91.4 68.4 all-gather.2
  190.6 85.3 all-gather.4
  321.5 78.5 reduce-scatter.2
  430.8 78.2 reduce-scatter.4

commit v3 on v2

--- a/solution.py
+++ b/solution.py
@@ -111,6 +111,7 @@
     "attend": 8,
     "ffn": 9,
     "ffn_back": 10,
+    "ffn_both": 12,
     "ffn_weights": 9,
     "attend_back_far": 9,
     "attend_back_near": 6,
@@ -166,11 +167,8 @@
 def each_rows(total, step, body):
     step = min(step, total)
 
-    def one(i, carry):
-        body(pl.ds(pl.multiple_of(i * step, step), step))
-        return carry
-
-    lax.fori_loop(0, total // step, one, 0)
+    for start in range(0, total, step):
+        body(slice(start, start + step))
 
 
 def norm_rows(full, gain, normed, scale):
@@ -216,12 +214,7 @@
 
 
 def part_shapes(tokens, width):
-    return [
-        shape((tokens, width), F32),
-        shape((tokens, width), F32),
-        shape((tokens, width), LOW),
-        shape((tokens, width), LOW),
-    ]
+    return [shape((tokens, width), LOW)] * 4
 
 
 def qkv_body(layout, joined, spot, *rest):
@@ -338,20 +331,54 @@
     hidden = hid.shape[1]
     tile = 256
 
-    def one(i, carry):
-        start = pl.multiple_of(i * tile, tile)
-        here = pl.ds(start, tile)
+    for start in range(0, hidden, tile):
+        here = slice(start, start + tile)
         g = dot(normed[...], buffer[:, here], 1, 0)
-        u = dot(normed[...], buffer[:, pl.ds(pl.multiple_of(hidden + start, tile), tile)], 1, 0)
+        u = dot(normed[...], buffer[:, hidden + start : hidden + start + tile], 1, 0)
         gate[:, here] = g.astype(LOW)
         up[:, here] = u.astype(LOW)
         hid[:, here] = (g * jax.nn.sigmoid(g) * u).astype(LOW)
-        return carry
-
-    lax.fori_loop(0, hidden // tile, one, 0)
     share = part0.shape[1]
     store_parts(
         (part0, part1, part2, part3),
+        spot,
+        lambda start: dot(hid[...], buffer[pl.ds(start, share), 2 * hidden : 3 * hidden], 1, 1),
+        share,
+    )
+
+
+def ffn_both_body(layout, spot, p0, p1, p2, p3, gain, upstream, *rest):
+    count = 1 + max(entry[0] for entry in layout)
+    weights = rest[:count]
+    full, normed, scale, hid, gate_grad, up_grad = rest[count : count + 6]
+    sums, sums_back = rest[count + 6 : count + 10], rest[count + 10 : count + 14]
+    buffer, sems = rest[count + 14 :]
+    copies = load_rows(weights, layout, spot, buffer, sems)
+    join_feats(spot, (p0, p1, p2, p3), full)
+    norm_rows(full, gain, normed, scale)
+    for copy in copies:
+        copy.wait()
+    hidden = hid.shape[1]
+    tile = 256
+    for start in range(0, hidden, tile):
+        here = slice(start, start + tile)
+        g = dot(normed[...], buffer[:, here], 1, 0)
+        u = dot(normed[...], buffer[:, hidden + start : hidden + start + tile], 1, 0)
+        grad = dot(upstream[...], buffer[:, 2 * hidden + start : 2 * hidden + start + tile], 1, 0)
+        sig = jax.nn.sigmoid(g)
+        hid[:, here] = (g * sig * u).astype(LOW)
+        gate_grad[:, here] = (grad * u * sig * (1.0 + g * (1.0 - sig))).astype(LOW)
+        up_grad[:, here] = (grad * g * sig).astype(LOW)
+    share = sums[0].shape[1]
+    store_parts(
+        sums_back,
+        spot,
+        lambda start: dot(gate_grad[...], buffer[pl.ds(start, share), :hidden], 1, 1)
+        + dot(up_grad[...], buffer[pl.ds(start, share), hidden : 2 * hidden], 1, 1),
+        share,
+    )
+    store_parts(
+        sums,
         spot,
         lambda start: dot(hid[...], buffer[pl.ds(start, share), 2 * hidden : 3 * hidden], 1, 1),
         share,
@@ -385,21 +412,15 @@
     hidden = gate.shape[1]
     tile = 256
 
-    def one(i, carry):
-        start = pl.multiple_of(i * tile, tile)
-        here = pl.ds(start, tile)
-        grad = dot(
-            full[...], buffer[:, pl.ds(pl.multiple_of(2 * hidden + start, tile), tile)], 1, 0
-        )
+    for start in range(0, hidden, tile):
+        here = slice(start, start + tile)
+        grad = dot(full[...], buffer[:, 2 * hidden + start : 2 * hidden + start + tile], 1, 0)
         g = gate[:, here].astype(F32)
         sig = jax.nn.sigmoid(g)
         gate_grad[:, here] = (
             grad * up[:, here].astype(F32) * sig * (1.0 + g * (1.0 - sig))
         ).astype(LOW)
         up_grad[:, here] = (grad * g * sig).astype(LOW)
-        return carry
-
-    lax.fori_loop(0, hidden // tile, one, 0)
     share = part0.shape[1]
     store_parts(
         (part0, part1, part2, part3),
@@ -587,38 +608,6 @@
                 full[pl.ds(start, positions), spot_out * lanes : (spot_out + 1) * lanes] = values
 
 
-def unframe(slots, table, spot, full, keep, send):
-    positions = keep.shape[1]
-    blocks = table.shape[0]
-    lanes = full.shape[1] // blocks
-    per = blocks // 4
-    for away, out in ((0, keep), (1, send)):
-        quarter = 2 * (spot[2] ^ away) + spot[1]
-        for slot in range(slots):
-            start = pl.multiple_of((2 * slot + spot[0]) * positions, positions)
-            for i in range(per):
-                at = table[quarter * per + i]
-                lane = pl.multiple_of(at * lanes, lanes)
-                out[slot, :, i * lanes : (i + 1) * lanes] = full[
-                    pl.ds(start, positions), pl.ds(lane, lanes)
-                ]
-
-
-def leave_body(slots, finish, fit, spot, table, *rest):
-    pieces, rest = rest[:4], rest[4:]
-    if finish:
-        before_full, rows_full, scale, moved = rest[:4]
-        outs, full, own = rest[4:-2], rest[-2], rest[-1]
-        finish_back(spot, pieces, before_full, rows_full, scale, moved, full, own)
-    else:
-        outs, full = rest[:-1], rest[-1]
-        join_feats(spot, pieces, full)
-    if fit:
-        unframe(slots, table, spot, full, *outs)
-    else:
-        outs[0][...] = full[...]
-
-
 def after(value, *others):
     return lax.optimization_barrier((value, others))[0]
 
@@ -714,20 +703,24 @@
     return place.swap_dp(sent, 0), place.swap_dp(other_sent, len(place.dp) - 1)
 
 
-def scatter_rest(place, received, kept, waits=()):
+def scatter_next(place, received, kept, step):
     k = len(place.dp)
-    ends = []
-    for got, keep, order in (
-        (received[0], kept[0], list(range(k))),
-        (received[1], kept[1], list(reversed(range(k)))),
-    ):
-        part = (keep.astype(F32) + got.astype(F32)).astype(LOW)
-        for index in order[1:]:
-            middle = part.shape[0] // 2
-            got = place.swap_dp(after(part[middle:], *waits), index)
-            part = (part[:middle].astype(F32) + got.astype(F32)).astype(LOW)
-        ends.append(part)
-    return ends
+    parts = [(a.astype(F32) + b.astype(F32)).astype(LOW) for a, b in zip(kept, received)]
+    if step == k:
+        return parts, None
+    middle = parts[0].shape[0] // 2
+    got = [
+        place.swap_dp(parts[0][middle:], step),
+        place.swap_dp(parts[1][middle:], k - 1 - step),
+    ]
+    return got, [part[:middle] for part in parts]
+
+
+def scatter_rest(place, received, kept, step=1):
+    while kept is not None:
+        received, kept = scatter_next(place, received, kept, step)
+        step += 1
+    return received
 
 
 def gather_feats(place, share):
@@ -737,8 +730,8 @@
 
 def scatter_feats(place, parts, beside=None):
     kept, kept_pair, sent, sent_pair = parts
-    middle = (kept_pair + place.swap_core(sent_pair).astype(F32)).astype(LOW)
-    near = kept + place.swap_core(sent).astype(F32)
+    middle = (kept_pair.astype(F32) + place.swap_core(sent_pair).astype(F32)).astype(LOW)
+    near = kept.astype(F32) + place.swap_core(sent).astype(F32)
     received = place.swap_zl(middle)
     done = None if beside is None else beside(middle)
     return near + after(received, done).astype(F32), done
@@ -796,13 +789,13 @@
             first, second = natural[:, :half_slots], natural[:, half_slots:]
             return place.swap_zh(pick(place.zh, first, second).transpose(1, 0, 2))
 
-        def token_quarters(natural, received):
+        def two_quarters(natural, received):
             first, second = natural[:, :half_slots], natural[:, half_slots:]
             own = pick(place.zh, second, first).transpose(1, 0, 2)
-            two = jnp.stack([own, received])
-            other = place.swap_zl(two)
-            mine = jnp.stack([two, other], 1).reshape(4, half_slots, positions, quarter)
-            return mine, place.swap_core(mine), other
+            return jnp.stack([own, received])
+
+        def four_quarters(two, other):
+            return jnp.stack([two, other], 1).reshape(4, half_slots, positions, quarter)
 
         def token_rows(quarters, valid):
             mine, other = quarters[:2]
@@ -821,37 +814,23 @@
             rows = cut.transpose(3, 0, 4, 1, 2, 5).reshape(tokens, depth)
             return rows if valid is None else rows * valid.astype(LOW)
 
-        def natural_rows(pieces, pending=()):
-            outs = [shape((half_slots, positions, quarter), LOW)] * 2
-            scratch = [pltpu.VMEM((tokens, depth), LOW)]
-            if pending:
-                scratch.append(pltpu.VMEM((tokens, quarter), F32))
-            outs = launch(
-                functools.partial(leave_body, half_slots, bool(pending), lanes_fit),
-                outs if lanes_fit else [shape((tokens, depth), LOW)],
-                [spot, table, *pieces, *pending],
-                [SMEM] * 2 + [VMEM] * (4 + len(pending)),
-                scratch,
-                name="leave",
-            )
-            if lanes_fit:
-                keep, send = outs
-            else:
-                cut = outs[0].reshape(
-                    half_slots, 2, positions, 2, 2, quarter
-                )
-                cut = pick(place.c, cut[:, 1], cut[:, 0])
-                cut = pick(place.zl, cut[:, :, :, 1], cut[:, :, :, 0])
-                keep = pick(place.zh, cut[:, :, 1], cut[:, :, 0])
-                send = pick(place.zh, cut[:, :, 0], cut[:, :, 1])
-            received = place.swap_zh(send)
+        def leave_rows(rows):
+            cut = rows.reshape(half_slots, 2, positions, quarter)
+            same = (place.c == place.zh).astype(jnp.int32)
+            kept = pick(place.c, cut[:, 1], cut[:, 0])
+            other = place.swap_core(pick(place.c, cut[:, 0], cut[:, 1]))
+            mine = pick(same, kept, other)
+            received = place.swap_zh(pick(same, other, kept))
             both = jnp.concatenate(
-                [pick(place.zh, received, keep), pick(place.zh, keep, received)], 0
+                [pick(place.zh, received, mine), pick(place.zh, mine, received)], 0
             )
             return both.transpose(1, 0, 2)
 
         zh_done = swap_slots(inputs)
-        mine, other, zl_done = token_quarters(inputs, zh_done)
+        two = two_quarters(inputs, zh_done)
+        zl_done = place.swap_zl(two)
+        mine = four_quarters(two, zl_done)
+        other = place.swap_core(mine)
         small = jnp.concatenate(
             [attn_gain.reshape(-1), ffn_gain.reshape(-1), variate_bias.reshape(-1)]
         ).reshape(1, -1)
@@ -976,9 +955,10 @@
                 gate_up = gather_rows_group(place, after((gate_both, up_both), blocks))
             if layer == LAYERS - 1:
                 late_cotangent = after(cotangent, key_value)
-                cotangent_quarters = token_quarters(late_cotangent, swap_slots(late_cotangent))
-                upstream_full = token_rows(cotangent_quarters, valid)
-                blocks = after(blocks, upstream_full)
+                late_other = swap_slots(late_cotangent)
+                blocks = after(blocks, late_other)
+                late_two = two_quarters(after(late_cotangent, blocks), late_other)
+                late_other = place.swap_zl(late_two)
             if more:
                 attn_next = after(attn_packs[layer + 1], blocks)
                 attn_other = place.swap_zh(attn_next)
@@ -997,14 +977,22 @@
             if first:
                 down_both = take_rows(place, down, after(down_other, attended))
 
+            if layer == LAYERS - 1:
+                sums = after(sums, late_other)
+                late_mine = four_quarters(late_two, after(late_other, sums))
+                late_other = place.swap_core(late_mine)
+
             def reduce_side(sent):
-                return list(others) if more else []
+                return list(others) if more else [late_other]
 
             shared, _ = scatter_feats(place, sums, reduce_side)
             middle = current + shared
             if first:
                 down_w, down_lay, early = gather_rows_swap(place, down_both, (middle,))
             mid_pieces = gather_feats(place, middle.astype(LOW))
+            if layer == LAYERS - 1:
+                upstream_full = token_rows((after(late_mine, middle), late_other), valid)
+                mid_pieces = after(mid_pieces, upstream_full)
             if more:
                 others.append(place.swap_zh(after(chunks[1], middle)))
                 attn_both = take_rows(place, attn_next, after(attn_other, middle))
@@ -1017,28 +1005,36 @@
                 next_w, next_lay, early = gather_rows_swap(
                     place, after(attn_both, mid_pieces, ffn_w), nothing
                 )
-            full_mid, normed_mid, scale_mid, gate, up, hid, *sums = launch(
-                functools.partial(ffn_body, ffn_lay),
-                [
-                    rows_low,
-                    rows_low,
-                    column,
-                    *[shape((tokens, hidden), LOW)] * 3,
-                    *parts,
-                ],
-                [
-                    spot,
-                    *mid_pieces,
-                    gains[LAYERS + layer : LAYERS + layer + 1],
-                    *ffn_w,
-                ],
-                [SMEM] + [VMEM] * 5 + [HBM] * len(ffn_w),
-                ffn_buffer,
-                name="ffn",
-            )
+            operands = [
+                spot,
+                *mid_pieces,
+                gains[LAYERS + layer : LAYERS + layer + 1],
+            ]
+            specs = [SMEM] + [VMEM] * 5
+            hidden_low = shape((tokens, hidden), LOW)
+            if more:
+                full_mid, normed_mid, scale_mid, gate, up, hid, *sums = launch(
+                    functools.partial(ffn_body, ffn_lay),
+                    [rows_low, rows_low, column, *[hidden_low] * 3, *parts],
+                    [*operands, *ffn_w],
+                    specs + [HBM] * len(ffn_w),
+                    ffn_buffer,
+                    name="ffn",
+                )
+            else:
+                full_mid, normed_mid, scale_mid, hid, *outs = launch(
+                    functools.partial(ffn_both_body, ffn_lay),
+                    [rows_low, rows_low, column, *[hidden_low] * 3, *parts, *parts],
+                    [*operands, upstream_full, *ffn_w],
+                    specs + [VMEM] + [HBM] * len(ffn_w),
+                    ffn_buffer,
+                    name="ffn_both",
+                )
+                gate = up = None
+                last_grads, sums, last_sums = outs[:2], outs[2:6], outs[6:]
             weights.append((attn_w, attn_lay, ffn_w, ffn_lay))
             if more:
-                sums = after(sums, early)
+                sums = after(sums, early, others[2])
 
             def take_side(sent):
                 return [
@@ -1068,9 +1064,9 @@
                     hid,
                 )
             )
-            pieces = gather_feats(place, current.astype(LOW))
-
-        last = pieces
+            if more:
+                pieces = gather_feats(place, current.astype(LOW))
+
         natural_valid = (
             ((2 * place.o + place.c) * positions + jnp.arange(positions, dtype=jnp.int32))[:, None]
             < lengths[None, :]
@@ -1078,11 +1074,23 @@
 
         upstream = share_of(upstream_full).astype(F32)
 
-        def step_back(sums, full_rows, row_scale, gain, before, beside):
+        def step_back(sums, full_rows, row_scale, gain, before, beside, final=None):
             shared, done = scatter_feats(place, sums, beside)
             own_rows = share_of(full_rows).astype(F32) * row_scale
             gain_grad = jnp.sum(shared * own_rows, 0)
-            moved = before + row_scale * (shared * share_of(gain)[None, :])
+            part = shared * share_of(gain)[None, :]
+            moved = before + row_scale * part
+            if final:
+                dots = jnp.sum(part * own_rows, 1)
+                sums = final(gain_grad)
+                other = place.swap_zl(jnp.concatenate([dots, sums]))
+                dots = dots + other[:tokens]
+                sums = jnp.stack([sums, other[tokens:]])
+                other = place.swap_core(jnp.concatenate([dots, sums.reshape(-1)]))
+                dots = (dots + other[:tokens]).reshape(tokens, 1) * (1.0 / depth)
+                sums = jnp.stack([sums, other[tokens:].reshape(sums.shape)])
+                sums = flip_if(place.c, flip_if(place.zl, sums, 1), 0)
+                return moved, [moved - row_scale * own_rows * dots], sums, done
             return moved, gather_feats(place, moved.astype(LOW)), gain_grad, done
 
         sent_order = [row_block(place, bits, side) for bits, side in relative_order(k)]
@@ -1161,14 +1169,7 @@
             ) = kept[layer]
             hidden_low = shape((tokens, hidden), LOW)
             if pending is None:
-                gate_grad, up_grad, *sums = launch(
-                    functools.partial(ffn_back_body, False, ffn_lay),
-                    [hidden_low, hidden_low, *parts],
-                    [spot, upstream_full, gate, up, *ffn_w],
-                    [SMEM] + [VMEM] * 3 + [HBM] * len(ffn_w),
-                    ffn_buffer,
-                    name="ffn_back",
-                )
+                (gate_grad, up_grad), sums = last_grads, last_sums
             else:
                 upstream_full, upstream, gate_grad, up_grad, *sums = launch(
                     functools.partial(ffn_back_body, True, ffn_lay),
@@ -1178,10 +1179,6 @@
                     ffn_buffer,
                     name="ffn_back",
                 )
-            if layer == LAYERS - 1:
-                output = natural_rows(last)
-                sums = after(sums, output)
-                output = output * natural_valid[:, :, None].astype(LOW)
             if late is not None:
                 late_ffn, late_got, late_kept = late
                 sums = after(sums, late_got)
@@ -1197,20 +1194,20 @@
             def ffn_side(sent):
                 partial = ffn_grads(sent)
                 if late is None:
-                    return partial, None
-                ends = scatter_rest(place, after(late_got, sent), late_kept)
-                return after(partial, ends), ends
-
-            moved, pieces, ffn_gain_grad, (ffn_partial, late_ends) = step_back(
+                    return after(partial, current), None
+                rows = return_rows(place, *after(late_ffn, sent))
+                return after(partial, rows), rows
+
+            moved, pieces, ffn_gain_grad, (ffn_partial, late_rows) = step_back(
                 sums, full_mid, scale_mid, gains[LAYERS + layer], upstream, ffn_side
             )
             ffn_rows = scatter_rows_group(place, *ffn_partial)
             if late is not None:
-                own_ffn, other_ffn = return_rows(place, *after(late_ffn, moved))
-                pieces = after(pieces, other_ffn)
-                others = [
-                    place.swap_zh(after(other_ffn[:, :hidden], pieces)),
-                ]
+                own_ffn, other_ffn = late_rows
+                others = [place.swap_zh(after(other_ffn[:, :hidden], moved))]
+                late_got, late_kept = scatter_next(place, after(late_got, moved), late_kept, 1)
+                pieces = after(pieces, others[0], late_kept)
+                others.append(place.swap_zh(after(other_ffn[:, hidden : 2 * hidden], pieces)))
             common = [queries, attended, logs, own_kinds, kinds, masks]
             later = blocks[half_keys:] if n_o > 1 else blocks
             early = blocks[:half_keys] if n_o > 1 else []
@@ -1244,10 +1241,15 @@
                 attn_buffer,
                 name="attend_back_far",
             )
+            if layer == LAYERS - 1:
+                output = leave_rows(after(current, moved).astype(LOW))
+                output = output * natural_valid[:, :, None].astype(LOW)
+                out_grad = after(out_grad, output)
             if late is not None:
-                out_grad = after(out_grad, others[0])
-                others.append(place.swap_zh(after(other_ffn[:, hidden : 2 * hidden], out_grad)))
-                own_attn, other_attn = return_rows(place, *after(late_ends, out_grad))
+                out_grad = after(out_grad, others[1], late_got)
+                others.append(place.swap_zh(after(other_ffn[:, 2 * hidden :], out_grad)))
+                late_ends = scatter_rest(place, after(late_got, out_grad), late_kept, 2)
+                own_attn, other_attn = return_rows(place, *late_ends)
             query_grad, same_sum_near, *near = launch(
                 functools.partial(attend_back_body, half_slots, len(early), 0, False, []),
                 [
@@ -1270,8 +1272,8 @@
                 ]
                 near = near[:middle_at]
             if late is not None:
-                received = after(received, others[1], other_attn)
-                others.append(place.swap_zh(after(other_ffn[:, 2 * hidden :], received)))
+                received = after(received, others[2], other_attn)
+                others.append(place.swap_zh(after(other_attn, received)))
             three, *sums = launch(
                 functools.partial(qkv_back_body, attn_lay, 1),
                 [shape((tokens, 3 * width), LOW), *parts],
@@ -1281,8 +1283,7 @@
                 name="qkv_back",
             )
             if late is not None:
-                sums = after(sums, others[2])
-                others.append(place.swap_zh(after(other_attn, sums)))
+                sums = after(sums, others[3])
             attn_grads = functools.partial(
                 weight_grads_of,
                 True,
@@ -1292,6 +1293,11 @@
                 "attn_weights",
             )
 
+            def small_sums(gain_grad):
+                gain_grads[0] = (gain_grad, ffn_gain_grad)
+                mine = [gain_grads[i][j] for j in range(2) for i in range(LAYERS)]
+                return jnp.concatenate([*mine, jnp.stack(bias_grads).reshape(-1)])
+
             def attn_side(sent):
                 partial = attn_grads(sent)
                 if late is None:
@@ -1300,18 +1306,13 @@
                 return after(partial, rows), rows
 
             moved, pieces, attn_gain_grad, (attn_partial, last_rows) = step_back(
-                sums, full, scale, gains[layer], middle, attn_side
+                sums, full, scale, gains[layer], middle, attn_side, small_sums if layer == 0 else None
             )
             pending = [*pieces, middle_full, full, scale, moved]
             gain_grads[layer] = (attn_gain_grad, ffn_gain_grad)
             if late is not None:
                 last_own, last_other = last_rows
-                last_sent = [place.swap_zh(after(last_other[:, :hidden], moved))]
-                pieces = after(pieces, others[3])
-                last_sent += [
-                    place.swap_zh(after(last_other[:, i * hidden : (i + 1) * hidden], pieces))
-                    for i in range(1, 3)
-                ]
+                last_sent = place.swap_zh(after(last_other, moved))
                 keep_grads(
                     layer + 1,
                     own_ffn.astype(F32) + jnp.concatenate(others[:3], 1).astype(F32),
@@ -1320,31 +1321,22 @@
             sent, other_sent, *attn_kept = after(attn_partial, moved)
             late = (ffn_rows, scatter_start(place, sent, other_sent), attn_kept)
 
-        mine = jnp.stack([gain_grads[layer][i] for i in range(2) for layer in range(LAYERS)])
-        wide = lax.dynamic_update_slice_in_dim(
-            jnp.zeros((2 * LAYERS, depth), F32), mine, own_quarter * quarter, 1
-        )
-        bias_wide = lax.dynamic_update_slice_in_dim(
-            jnp.zeros((LAYERS, 4 * heads, 2), F32), jnp.stack(bias_grads), own_quarter * heads, 1
-        )
-        total = jnp.concatenate([wide.reshape(-1), bias_wide.reshape(-1)])
-        total = after(total, *pending)
-        total = total + place.swap_core(total)
+        input_grad = leave_rows(pending[0].astype(LOW)).astype(F32)
+        own_attn, other_attn = return_rows(place, *scatter_rest(place, *late[1:]))
+        attn_out = own_attn.astype(F32) + place.swap_zh(other_attn).astype(F32)
+        total = after(attn_gain_grad, other_attn)
         for i in range(k):
             total = total + place.swap_dp(total, i)
-        total = total + place.swap_zl(total)
-        total_zh = place.swap_zh(total)
-        input_grad = natural_rows(pending[:4], pending[4:]).astype(F32)
-        total = total + total_zh
-        own_attn, other_attn = return_rows(place, *scatter_rest(place, *late[1:]))
-        attn_out = own_attn.astype(F32) + place.swap_zh(other_attn).astype(F32)
-        ffn_out = last_own.astype(F32) + jnp.concatenate(last_sent, 1).astype(F32)
+        total = total + place.swap_zh(total)
+        small_cut = LAYERS * quarter
+        total = total.reshape(4, -1)
+        wide = total[:, : 2 * small_cut].reshape(4, 2 * LAYERS, quarter)
+        bias_wide = total[:, 2 * small_cut :].reshape(4, LAYERS, heads, 2)
+        ffn_out = last_own.astype(F32) + last_sent.astype(F32)
         keep_grads(0, ffn_out, attn_out)
-        wide = total[: wide.size].reshape(wide.shape)
-        bias_wide = total[wide.size :].reshape(bias_wide.shape)
         tensor = 2 * place.zh + place.zl
-        gains_out = lax.dynamic_slice_in_dim(wide, tensor * quarter, quarter, 1)
-        bias_out = lax.dynamic_slice_in_dim(bias_wide, tensor * heads, heads, 1)
+        gains_out = lax.dynamic_index_in_dim(wide, tensor, 0, keepdims=False)
+        bias_out = lax.dynamic_index_in_dim(bias_wide, tensor, 0, keepdims=False)
         stacks = [
             jnp.stack([weight_grads[layer][member] for layer in range(LAYERS)])
             for member in range(7)

time: 648 us -> 597 us (0.921)
  waiting for transfers between devices: 315 us -> 272 us
  Pallas kernels: 140 us -> 129 us
    ppermute x117 -> x111, waiting for transfers between devices: 314 us -> 272 us  [move(): return lax.ppermute(array, AXES, pairs)]
    pallas_call x22 -> x19, Pallas kernels: 140 us -> 129 us  [launch(): pl.pallas_call(body, out_shape=outs, in_specs=specs, out_specs=[VMEM] * l...]
    convert_element_type x15 -> x14, other arithmetic: 13.2 us -> 6.61 us  [the longest x8 4.27 us: scatter_feats(): (kept_pair.astype(F32) + place.swap_core(sent_pair).astype(F32)).astype(LOW)]
    select_n x28 -> x32, other arithmetic: 10.6 us -> 15.3 us  [pick(): return jnp.where(flag == 1, one, two)]
    ppermute x117 -> x111, starting transfers between devices: 81.9 us -> 86.4 us  [move(): return lax.ppermute(array, AXES, pairs)]
    unnamed x230 -> x231, local copies, waits for them, and re-layouts: 15.3 us -> 16.2 us
  transfers between devices with their start and end apart: 121 -> 115, of which waited for: 62 -> 60; matrix products, arithmetic and copies ran while one was open for 11% -> 9% of each run, Pallas kernels for 18% -> 20%
where the time goes in v3:
time: 597 us; the launch traced here: 591 us
  waiting for transfers between devices  272 us (46%)
  Pallas kernels  129 us (22%)
  starting transfers between devices  86.7 us (15%)
  other arithmetic  52.6 us (9%)
  local copies, waits for them, and re-layouts  34.4 us (6%)
  between operations  17.2 us (3%)
    ppermute x111, waiting for transfers between devices, move(): return lax.ppermute(array, AXES, pairs)  272 us
    pallas_call x19, Pallas kernels, launch(): pl.pallas_call(body, out_shape=outs, in_specs=specs, out_specs=[VMEM] * l...  129 us
    ppermute x111, starting transfers between devices, move(): return lax.ppermute(array, AXES, pairs)  86.4 us
    unnamed x231, local copies, waits for them, and re-layouts  16.2 us
    select_n x32, other arithmetic, pick(): return jnp.where(flag == 1, one, two)  15.3 us
  transfers between devices with their start and end apart: 115, of which 60 were waited for; matrix products, arithmetic and copies ran while one was open for 9% of the time, Pallas kernels for 20%

profile of v3, /device:TPU:0, one launch (start us, length us, event | category | flops | bytes accessed | tf_op | source)
XLA Modules:
  0.0 591.3 jit_solution(14723440391725509568)
XLA Ops:
  25.8 8.4 %collective-permute-done.4 = f32[2,1,1040]{2,1,0:T(1,128)S(1)} collective-permute-done((f32[2,1,1040]{2,1,0:T(1,128)S(1)}, f32[2,1,1040]{2,1,0:T(1,128)S(1)}, u32[]{:S(2)}, u32[]{:S(2)}) %collective-permute-start.4) | collective-permute-done | bytes 8352 | tf_op jit(solution)/shard_map/ppermute | solution.py:69
  66.4 7.3 %collective-permute-done.17 = bf16[128,1024]{1,0:T(8,128)(2,1)S(1)} collective-permute-done((bf16[128,1024]{1,0:T(8,128)(2,1)S(1)}, bf16[128,1024]{1,0:T(8,128)(2,1)S(1)}, u32[]{:S(2)}, u32[]{:S(2)}) %collective-permute-start.17) | collective-permute-done | bytes 262176 | tf_op jit(solution)/shard_map/ppermute | solution.py:69
  77.2 13.6 %collective-permute-done.14 = bf16[128,1024]{1,0:T(8,128)(2,1)S(1)} collective-permute-done((bf16[128,1024]{1,0:T(8,128)(2,1)S(1)}, bf16[128,1024]{1,0:T(8,128)(2,1)S(1)}, u32[]{:S(2)}, u32[]{:S(2)}) %collective-permute-start.14) | collective-permute-done | bytes 262176 | tf_op jit(solution)/shard_map/ppermute | solution.py:69
  100.3 7.3 %attend.2 = (bf16[512,256]{1,0:T(8,128)(2,1)S(1)}, f32[512,4]{1,0:T(8,128)S(1)}, bf16[512,256]{1,0:T(8,128)(2,1)S(1)}, bf16[512,256]{1,0:T(8,128)(2,1)S(1)}, bf1...) custom-call(s32[5]{0:T(128)S(1)} %stack.168.spot, f32[8]{0:T(128)S(1)} %get-tuple-element.638.bias, ...), custom_call_target="tpu_custom_call" | custom-call | flops 9200000000 | bytes 1024 | tf_op jit(solution)/shard_map/attend/pallas_call | solution.py:129
  120.2 8.1 %collective-permute-done.23 = bf16[128,1024]{1,0:T(8,128)(2,1)S(1)} collective-permute-done((bf16[128,1024]{1,0:T(8,128)(2,1)}, bf16[128,1024]{1,0:T(8,128)(2,1)S(1)}, u32[]{:S(2)}, u32[]{:S(2)}) %collective-permute-start.23) | collective-permute-done | bytes 262176 | tf_op jit(solution)/shard_map/ppermute | solution.py:69
  139.4 6.0 %collective-permute-done.24.p1 = bf16[512,256]{1,0:T(8,128)(2,1)S(1)} collective-permute-done((bf16[512,256]{1,0:T(8,128)(2,1)S(1)}, bf16[512,256]{1,0:T(8,128)(2,1)S(1)}, u32[]{:S(2)}, u32[]{:S(2)}) %collective-permute-start.24) | collective-permute-done | bytes 262176 | tf_op jit(solution)/shard_map/ppermute | solution.py:69
  146.5 7.0 %collective-permute-done.27 = bf16[128,1024]{1,0:T(8,128)(2,1)S(1)} collective-permute-done((bf16[128,1024]{1,0:T(8,128)(2,1)}, bf16[128,1024]{1,0:T(8,128)(2,1)S(1)}, u32[]{:S(2)}, u32[]{:S(2)}) %collective-permute-start.27) | collective-permute-done | bytes 262176 | tf_op jit(solution)/shard_map/ppermute | solution.py:69
  163.8 8.5 %ffn.1 = (bf16[512,1024]{1,0:T(8,128)(2,1)}, bf16[512,1024]{1,0:T(8,128)(2,1)}, f32[512,1]{1,0:T(8,128)S(1)}, bf16[512,1024]{1,0:T(8,128)(2,1)}, bf16[512,1024]{...) custom-call(s32[5]{0:T(128)S(1)} %stack.168.spot, ...), custom_call_target="tpu_custom_call" | custom-call | flops 10350000128 | bytes 1024 | tf_op jit(solution)/shard_map/ffn/pallas_call | solution.py:129
  191.9 7.6 %collective-permute-done.43.rest_1_ = bf16[512,256]{1,0:T(8,128)(2,1)S(1)} collective-permute-done((bf16[512,256]{1,0:T(8,128)(2,1)S(1)}, bf16[512,256]{1,0:T(8,128)(2,1)S(1)}, u32[]{:S(2)}, u32[]{:S(2)}) %collective-permute-start.43) | collective-permute-done | bytes 262176 | tf_op jit(solution)/shard_map/ppermute | solution.py:69
  222.7 6.6 %collective-permute-done.48.rest_1_.rest_3_ = bf16[512,512]{1,0:T(8,128)(2,1)S(1)} collective-permute-done((bf16[512,512]{1,0:T(8,128)(2,1)}, bf16[512,512]{1,0:T(8,128)(2,1)S(1)}, u32[]{:S(2)}, u32[]{:S(2)}) %collective-permute-start.48) | collective-permute-done | bytes 524320 | tf_op jit(solution)/shard_map/ppermute | solution.py:69
  232.4 7.3 %attend.3 = (bf16[512,256]{1,0:T(8,128)(2,1)S(1)}, f32[512,4]{1,0:T(8,128)S(1)}, bf16[512,256]{1,0:T(8,128)(2,1)S(1)}, bf16[512,256]{1,0:T(8,128)(2,1)S(1)}, bf1...) custom-call(s32[5]{0:T(128)S(1)} %stack.168.spot, f32[8]{0:T(128)S(1)} %get-tuple-element.639.bias, ...), custom_call_target="tpu_custom_call" | custom-call | flops 9200000000 | bytes 1024 | tf_op jit(solution)/shard_map/attend/pallas_call | solution.py:129
  242.7 7.7 %collective-permute-done.53 = bf16[512,256]{1,0:T(8,128)(2,1)S(1)} collective-permute-done((bf16[512,256]{1,0:T(8,128)(2,1)S(1)}, bf16[512,256]{1,0:T(8,128)(2,1)S(1)}, u32[]{:S(2)}, u32[]{:S(2)}) %collective-permute-start.53) | collective-permute-done | bytes 262176 | tf_op jit(solution)/shard_map/ppermute | solution.py:69
  252.1 7.0 %collective-permute-done.55.p1 = bf16[512,256]{1,0:T(8,128)(2,1)S(1)} collective-permute-done((bf16[512,256]{1,0:T(8,128)(2,1)S(1)}, bf16[512,256]{1,0:T(8,128)(2,1)S(1)}, u32[]{:S(2)}, u32[]{:S(2)}) %collective-permute-start.55) | collective-permute-done | bytes 262176 | tf_op jit(solution)/shard_map/ppermute | solution.py:69
  261.8 13.3 %ffn_both.1 = (bf16[512,1024]{1,0:T(8,128)(2,1)}, bf16[512,1024]{1,0:T(8,128)(2,1)}, f32[512,1]{1,0:T(8,128)S(1)}, bf16[512,1024]{1,0:T(8,128)(2,1)}, bf16[512,1...) custom-call(s32[5]{0:T(128)S(1)} %stack.168.spot, ...), custom_call_target="tpu_custom_call" | custom-call | flops 13799999488 | bytes 1024 | tf_op jit(solution)/shard_map/ffn_both/pallas_call | solution.py:129
  278.4 8.6 %ffn_weights.2 = bf16[1024,3072]{1,0:T(8,128)(2,1)} custom-call(s32[5]{0:T(128)S(1)} %stack.168.spot, bf16[512,1024]{1,0:T(8,128)(2,1)S(1)} %copy-done.18, bf16[512,1024]{1,0:T(8,128)(2,1)} %get-tuple-element.342.refs_1_, bf16[512,1024]{1,0:T(8,128)(2,1)} %get-tuple-element.343.refs_2_, bf16[512,1024]{1,0:T(8,128)(2,1)} %frame.3.upstream.refs_3_.rest_8_, ...), custom_call_target="tpu_custom_call" | custom-call | flops 10350000128 | bytes 1024 | tf_op jit(solution)/shard_map/ffn_weights/pallas_call | solution.py:129
  290.0 6.7 %collective-permute-done.63 = bf16[512,256]{1,0:T(8,128)(2,1)S(1)} collective-permute-done((bf16[512,256]{1,0:T(8,128)(2,1)S(1)}, bf16[512,256]{1,0:T(8,128)(2,1)S(1)}, u32[]{:S(2)}, u32[]{:S(2)}) %collective-permute-start.63) | collective-permute-done | bytes 262176 | tf_op jit(solution)/shard_map/ppermute | solution.py:69
  301.7 6.0 %collective-permute-start.65 = (bf16[1,256,256]{2,1,0:T(8,128)(2,1)S(1)}, bf16[1,256,256]{2,1,0:T(8,128)(2,1)S(1)}, u32[]{:S(2)}, u32[]{:S(2)}) collective-permute-start(bf16[1,256,256]{2,1,0:T(8,128)(2,1)S(1)} %get-tuple-element.532), channel_id=1, source_target_pairs={{0,2},{1,3},{2,0},{3,1},{4,6},{5,7},{6,4},{7,5},{8,10},{9,11},{10,... | collective-permute-start | bytes 393224 | tf_op jit(solution)/shard_map/ppermute | solution.py:69
  312.5 10.1 %attend_back_far.2 = (bf16[512,1024]{1,0:T(8,128)(2,1)}, f32[512,256]{1,0:T(8,128)}, bf16[512,256]{1,0:T(8,128)(2,1)S(1)}, f32[512,4]{1,0:T(8,128)S(1)}, f32[512...) custom-call(s32[5]{0:T(128)S(1)} %stack.168.spot, f32[8]{0:T(128)S(1)} %get-tuple-element.639.bias, ...), custom_call_target="tpu_custom_call" | custom-call | flops 10350000128 | bytes 1024 | tf_op jit(solution)/shard_map/attend_back_far/pallas_call | solution.py:129
  325.6 6.2 %attend_back_near.2 = (f32[512,256]{1,0:T(8,128)}, f32[4,512]{1,0:T(4,128)S(1)}, f32[512,512]{1,0:T(8,128)}) custom-call(s32[5]{0:T(128)S(1)} %stack.168.spot, f32[8]{0:T(128)S(1)} %get-tuple-element.639.bias, bf16[512,256]{1,0:T(8,128)(2,1)S(1)} %get-tuple-element.307.queries, bf16[512,256]{1,0:T(8,128)(2,1)S(1)} %get-tuple-element.372.attended.refs_3_, ...), custom_call_target="tpu_custom_call" | custom-call | flops 6899999744 | bytes 1024 | tf_op jit(solution)/shard_map/attend_back_near/pallas_call | solution.py:129
  331.9 12.3 %collective-permute-done.69.rest_0_ = bf16[512,512]{1,0:T(8,128)(2,1)S(1)} collective-permute-done((bf16[512,512]{1,0:T(8,128)(2,1)}, bf16[512,512]{1,0:T(8,128)(2,1)S(1)}, u32[]{:S(2)}, u32[]{:S(2)}) %collective-permute-start.69) | collective-permute-done | bytes 524320 | tf_op jit(solution)/shard_map/ppermute | solution.py:69
  365.2 5.9 %collective-permute-done.73.rest_1_ = bf16[512,256]{1,0:T(8,128)(2,1)S(1)} collective-permute-done((bf16[512,256]{1,0:T(8,128)(2,1)S(1)}, bf16[512,256]{1,0:T(8,128)(2,1)S(1)}, u32[]{:S(2)}, u32[]{:S(2)}) %collective-permute-start.73) | collective-permute-done | bytes 262176 | tf_op jit(solution)/shard_map/ppermute | solution.py:69
  373.5 10.0 %ffn_back.1 = (bf16[512,1024]{1,0:T(8,128)(2,1)}, f32[512,256]{1,0:T(8,128)}, bf16[512,1024]{1,0:T(8,128)(2,1)}, bf16[512,1024]{1,0:T(8,128)(2,1)}, bf16[512,256...) custom-call(s32[5]{0:T(128)S(1)} %stack.168.spot, ...), custom_call_target="tpu_custom_call" | custom-call | flops 11500000256 | bytes 1024 | tf_op jit(solution)/shard_map/ffn_back/pallas_call | solution.py:129
  392.0 8.6 %ffn_weights.3 = bf16[1024,3072]{1,0:T(8,128)(2,1)} custom-call(s32[5]{0:T(128)S(1)} %stack.168.spot, bf16[512,1024]{1,0:T(8,128)(2,1)S(1)} %copy-done.17, bf16[512,1024]{1,0:T(8,128)(2,1)} %get-tuple-element.399.refs_1_, bf16[512,1024]{1,0:T(8,128)(2,1)} %get-tuple-element.400.refs_2_, bf16[512,1024]{1,0:T(8,128)(2,1)} %get-tuple-element.401.refs_3_.rest_8_, ...), custom_call_target="tpu_custom_call" | custom-call | flops 10350000128 | bytes 1024 | tf_op jit(solution)/shard_map/ffn_weights/pallas_call | solution.py:129
  407.2 6.9 %collective-permute-done.80 = bf16[512,256]{1,0:T(8,128)(2,1)S(1)} collective-permute-done((bf16[512,256]{1,0:T(8,128)(2,1)S(1)}, bf16[512,256]{1,0:T(8,128)(2,1)S(1)}, u32[]{:S(2)}, u32[]{:S(2)}) %collective-permute-start.80) | collective-permute-done | bytes 262176 | tf_op jit(solution)/shard_map/ppermute | solution.py:69
  428.5 7.2 %collective-permute-done.85 = bf16[128,1024]{1,0:T(8,128)(2,1)S(1)} collective-permute-done((bf16[128,1024]{1,0:T(8,128)(2,1)S(1)}, bf16[128,1024]{1,0:T(8,128)(2,1)S(1)}, u32[]{:S(2)}, u32[]{:S(2)}) %collective-permute-start.85) | collective-permute-done | bytes 262176 | tf_op jit(solution)/shard_map/ppermute | solution.py:69
  436.7 9.7 %attend_back_far.3 = (bf16[512,1024]{1,0:T(8,128)(2,1)}, f32[512,256]{1,0:T(8,128)}, bf16[512,256]{1,0:T(8,128)(2,1)S(1)}, f32[512,4]{1,0:T(8,128)S(1)}, f32[512...) custom-call(s32[5]{0:T(128)S(1)} %stack.168.spot, f32[8]{0:T(128)S(1)} %get-tuple-element.638.bias, ...), custom_call_target="tpu_custom_call" | custom-call | flops 10350000128 | bytes 1024 | tf_op jit(solution)/shard_map/attend_back_far/pallas_call | solution.py:129
  450.9 6.1 %attend_back_near.3 = (f32[512,256]{1,0:T(8,128)}, f32[4,512]{1,0:T(4,128)S(1)}, f32[512,512]{1,0:T(8,128)}) custom-call(s32[5]{0:T(128)S(1)} %stack.168.spot, f32[8]{0:T(128)S(1)} %get-tuple-element.638.bias, bf16[512,256]{1,0:T(8,128)(2,1)S(1)} %get-tuple-element.247.queries, bf16[512,256]{1,0:T(8,128)(2,1)S(1)} %get-tuple-element.446.attended.refs_3_, ...), custom_call_target="tpu_custom_call" | custom-call | flops 6899999744 | bytes 1024 | tf_op jit(solution)/shard_map/attend_back_near/pallas_call | solution.py:129
  458.5 13.0 %collective-permute-done.90 = bf16[128,1024]{1,0:T(8,128)(2,1)S(1)} collective-permute-done((bf16[128,1024]{1,0:T(8,128)(2,1)}, bf16[128,1024]{1,0:T(8,128)(2,1)S(1)}, u32[]{:S(2)}, u32[]{:S(2)}) %collective-permute-start.90) | collective-permute-done | bytes 262176 | tf_op jit(solution)/shard_map/ppermute | solution.py:69
  476.7 9.2 %collective-permute-done.92 = bf16[128,1024]{1,0:T(8,128)(2,1)S(1)} collective-permute-done((bf16[128,1024]{1,0:T(8,128)(2,1)S(1)}, bf16[128,1024]{1,0:T(8,128)(2,1)S(1)}, u32[]{:S(2)}, u32[]{:S(2)}) %collective-permute-start.92) | collective-permute-done | bytes 262176 | tf_op jit(solution)/shard_map/ppermute | solution.py:69
  515.7 9.7 %collective-permute-done.101 = bf16[256,1024]{1,0:T(8,128)(2,1)S(1)} collective-permute-done((bf16[256,1024]{1,0:T(8,128)(2,1)S(1)}, bf16[256,1024]{1,0:T(8,128)(2,1)S(1)}, u32[]{:S(2)}, u32[]{:S(2)}) %collective-permute-start.101) | collective-permute-done | bytes 524320 | tf_op jit(solution)/shard_map/ppermute | solution.py:69
  527.4 27.5 %collective-permute-done.100 = bf16[1,256,256]{2,1,0:T(8,128)(2,1)S(1)} collective-permute-done((bf16[1,256,256]{2,1,0:T(8,128)(2,1)S(1)}, bf16[1,256,256]{2,1,0:T(8,128)(2,1)S(1)}, u32[]{:S(2)}, u32[]{:S(2)}) %collective-permute-start.100) | collective-permute-done | bytes 131104 | tf_op jit(solution)/shard_map/ppermute | solution.py:69
  570.9 7.9 %collective-permute-done.110 = f32[2,2,1040]{2,1,0:T(2,128)S(1)} collective-permute-done((f32[2,2,1040]{2,1,0:T(2,128)S(1)}, f32[2,2,1040]{2,1,0:T(2,128)S(1)}, u32[]{:S(2)}, u32[]{:S(2)}) %collective-permute-start.110) | collective-permute-done | bytes 16672 | tf_op jit(solution)/shard_map/ppermute | solution.py:69
  (636 shorter events, 286.8 us)
Async XLA Ops:
  7.2 154.4 %all-gather.3.cloned.1.call-start = ((), (), s32[]{:S(2)}) async-start(), calls=%async_computation.2 | async-start | bytes 5242880 | tf_op jit(solution)/shard_map/all_gather | solution.py:671
  19.5 14.7 %collective-permute-start.5 = (bf16[128,1024]{1,0:T(8,128)(2,1)S(1)}, bf16[128,1024]{1,0:T(8,128)(2,1)S(1)}, u32[]{:S(2)}, u32[]{:S(2)}) collective-permute-start(bf16[128,1024]{1,0:T(8,128)(2,1)S(1)} %pad_maximum_fusion.12), channel_id=1, source_target_pairs={{0,2},{1,3},{2,0},{3,1},{4,6},{5,7},{6,4},{7,5},{8,10},{9,11},{10,... | collective-permute-start | bytes 786440 | tf_op jit(solution)/shard_map/ppermute | solution.py:69
  22.5 16.6 %collective-permute-start.1 = (bf16[2,1,256,256]{3,2,1,0:T(8,128)(2,1)S(1)}, bf16[2,1,256,256]{3,2,1,0:T(8,128)(2,1)S(1)}, u32[]{:S(2)}, u32[]{:S(2)}) collective-permute-start(bf16[2,1,256,256]{3,2,1,0:T(8,128)(2,1)S(1)} %get-tuple-element.599), channel_id=1, source_target_pairs={{0,1},{1,0},{2,3},{3,2},{4,5},{5,4},{6,7},{7,6},{8,9},{9,8},{10,11... | collective-permute-start | bytes 786440 | tf_op jit(solution)/shard_map/ppermute | solution.py:69
  47.8 25.9 %collective-permute-start.15 = (bf16[128,1024]{1,0:T(8,128)(2,1)S(1)}, bf16[128,1024]{1,0:T(8,128)(2,1)S(1)}, u32[]{:S(2)}, u32[]{:S(2)}) collective-permute-start(bf16[128,1024]{1,0:T(8,128)(2,1)S(1)} %get-tuple-element.251), channel_id=1, source_target_pairs={{0,2},{1,3},{2,0},{3,1},{4,6},{5,7},{6,4},{7,5},{8,10},{9,11},{10,... | collective-permute-start | bytes 786440 | tf_op jit(solution)/shard_map/ppermute | solution.py:69
  51.9 21.9 %collective-permute-start.17 = (bf16[128,1024]{1,0:T(8,128)(2,1)S(1)}, bf16[128,1024]{1,0:T(8,128)(2,1)S(1)}, u32[]{:S(2)}, u32[]{:S(2)}) collective-permute-start(bf16[128,1024]{1,0:T(8,128)(2,1)S(1)} %get-tuple-element.253), channel_id=1, source_target_pairs={{0,2},{1,3},{2,0},{3,1},{4,6},{5,7},{6,4},{7,5},{8,10},{9,11},{10,... | collective-permute-start | bytes 786440 | tf_op jit(solution)/shard_map/ppermute | solution.py:69
  65.8 25.0 %collective-permute-start.13 = (bf16[512,512]{1,0:T(8,128)(2,1)}, bf16[512,512]{1,0:T(8,128)(2,1)}, u32[]{:S(2)}, u32[]{:S(2)}) collective-permute-start(bf16[512,512]{1,0:T(8,128)(2,1)} %get-tuple-element.255.rest_0_.rest_3_), channel_id=1, source_target_pairs={{0,8},{1,9},{2,10},{3,11},{4,12},{5,13},{6,14},{7,15},{8,0},{9,1},... | collective-permute-start | bytes 1572872 | tf_op jit(solution)/shard_map/ppermute | solution.py:69
  76.0 14.8 %collective-permute-start.14 = (bf16[128,1024]{1,0:T(8,128)(2,1)S(1)}, bf16[128,1024]{1,0:T(8,128)(2,1)S(1)}, u32[]{:S(2)}, u32[]{:S(2)}) collective-permute-start(bf16[128,1024]{1,0:T(8,128)(2,1)S(1)} %bitcast.220), channel_id=1, source_target_pairs={{0,2},{1,3},{2,0},{3,1},{4,6},{5,7},{6,4},{7,5},{8,10},{9,11},{10,... | collective-permute-start | bytes 786440 | tf_op jit(solution)/shard_map/ppermute | solution.py:69
  91.9 169.2 %all-gather.5.cloned.1.call-start = ((), (), s32[]{:S(2)}) async-start(), calls=%async_computation.3 | async-start | bytes 7864320 | tf_op jit(solution)/shard_map/all_gather | solution.py:671
  113.1 15.1 %collective-permute-start.23 = (bf16[128,1024]{1,0:T(8,128)(2,1)}, bf16[128,1024]{1,0:T(8,128)(2,1)S(1)}, u32[]{:S(2)}, u32[]{:S(2)}) collective-permute-start(bf16[128,1024]{1,0:T(8,128)(2,1)} %get-tuple-element.266), channel_id=1, source_target_pairs={{0,2},{1,3},{2,0},{3,1},{4,6},{5,7},{6,4},{7,5},{8,10},{9,11},{10,... | collective-permute-start | bytes 786440 | tf_op jit(solution)/shard_map/ppermute | solution.py:69
  118.2 14.6 %collective-permute-start.32 = (bf16[128,1024]{1,0:T(8,128)(2,1)S(1)}, bf16[128,1024]{1,0:T(8,128)(2,1)S(1)}, u32[]{:S(2)}, u32[]{:S(2)}) collective-permute-start(bf16[128,1024]{1,0:T(8,128)(2,1)S(1)} %get-tuple-element.278.rest_4_.rest_14_), channel_id=1, source_target_pairs={{0,8},{1,9},{2,10},{3,11},{4,12},{5,13},{6,14},{7,15},{8,0},{9,1},... | collective-permute-start | bytes 786440 | tf_op jit(solution)/shard_map/ppermute | solution.py:69
  135.9 23.3 %collective-permute-start.33 = (bf16[256,1024]{1,0:T(8,128)(2,1)}, bf16[256,1024]{1,0:T(8,128)(2,1)}, u32[]{:S(2)}, u32[]{:S(2)}) collective-permute-start(bf16[256,1024]{1,0:T(8,128)(2,1)} %pad_maximum_fusion.7), channel_id=1, source_target_pairs={{0,16},{1,17},{2,18},{3,19},{4,20},{5,21},{6,22},{7,23},{8,24},{9,... | collective-permute-start | bytes 1572872 | tf_op jit(solution)/shard_map/ppermute | solution.py:69
  137.2 22.0 %collective-permute-start.31 = (bf16[256,1024]{1,0:T(8,128)(2,1)}, bf16[256,1024]{1,0:T(8,128)(2,1)}, u32[]{:S(2)}, u32[]{:S(2)}) collective-permute-start(bf16[256,1024]{1,0:T(8,128)(2,1)} %pad_maximum_fusion.6), channel_id=1, source_target_pairs={{0,8},{1,9},{2,10},{3,11},{4,12},{5,13},{6,14},{7,15},{8,0},{9,1},... | collective-permute-start | bytes 1572872 | tf_op jit(solution)/shard_map/ppermute | solution.py:69
  138.0 15.6 %collective-permute-start.25 = (bf16[512,256]{1,0:T(8,128)(2,1)S(1)}, bf16[512,256]{1,0:T(8,128)(2,1)S(1)}, u32[]{:S(2)}, u32[]{:S(2)}) collective-permute-start(bf16[512,256]{1,0:T(8,128)(2,1)S(1)} %get-tuple-element.280.p0), channel_id=1, source_target_pairs={{0,4},{1,5},{2,6},{3,7},{4,0},{5,1},{6,2},{7,3},{8,12},{9,13},{10,... | collective-permute-start | bytes 786440 | tf_op jit(solution)/shard_map/ppermute | solution.py:69
  138.1 15.5 %collective-permute-start.27 = (bf16[128,1024]{1,0:T(8,128)(2,1)}, bf16[128,1024]{1,0:T(8,128)(2,1)S(1)}, u32[]{:S(2)}, u32[]{:S(2)}) collective-permute-start(bf16[128,1024]{1,0:T(8,128)(2,1)} %get-tuple-element.268), channel_id=1, source_target_pairs={{0,2},{1,3},{2,0},{3,1},{4,6},{5,7},{6,4},{7,5},{8,10},{9,11},{10,... | collective-permute-start | bytes 786440 | tf_op jit(solution)/shard_map/ppermute | solution.py:69
  159.2 14.9 %collective-permute-start.36 = (bf16[128,1024]{1,0:T(8,128)(2,1)S(1)}, bf16[128,1024]{1,0:T(8,128)(2,1)}, u32[]{:S(2)}, u32[]{:S(2)}) collective-permute-start(bf16[128,1024]{1,0:T(8,128)(2,1)S(1)} %bitcast.223), channel_id=1, source_target_pairs={{0,2},{1,3},{2,0},{3,1},{4,6},{5,7},{6,4},{7,5},{8,10},{9,11},{10,... | collective-permute-start | bytes 786440 | tf_op jit(solution)/shard_map/ppermute | solution.py:69
  181.8 206.7 %reduce-scatter.3.cloned.1.call-start = ((), (), s32[]{:S(2)}) async-start(), calls=%async_computation.4 | async-start | bytes 7864320 | tf_op jit(solution)/shard_map/reduce_scatter | solution.py:697
  183.3 18.8 %collective-permute-start.46 = (bf16[256,1024]{1,0:T(8,128)(2,1)S(1)}, bf16[256,1024]{1,0:T(8,128)(2,1)S(1)}, u32[]{:S(2)}, u32[]{:S(2)}) collective-permute-start(bf16[256,1024]{1,0:T(8,128)(2,1)S(1)} %pad_maximum_fusion.8), channel_id=1, source_target_pairs={{0,8},{1,9},{2,10},{3,11},{4,12},{5,13},{6,14},{7,15},{8,0},{9,1},... | collective-permute-start | bytes 1572872 | tf_op jit(solution)/shard_map/ppermute | solution.py:69
  185.8 21.4 %collective-permute-start.47 = (bf16[256,1024]{1,0:T(8,128)(2,1)S(1)}, bf16[256,1024]{1,0:T(8,128)(2,1)S(1)}, u32[]{:S(2)}, u32[]{:S(2)}) collective-permute-start(bf16[256,1024]{1,0:T(8,128)(2,1)S(1)} %pad_maximum_fusion.9), channel_id=1, source_target_pairs={{0,16},{1,17},{2,18},{3,19},{4,20},{5,21},{6,22},{7,23},{8,24},{9,... | collective-permute-start | bytes 1572872 | tf_op jit(solution)/shard_map/ppermute | solution.py:69
  191.9 15.4 %collective-permute-start.44 = (bf16[512,256]{1,0:T(8,128)(2,1)S(1)}, bf16[512,256]{1,0:T(8,128)(2,1)S(1)}, u32[]{:S(2)}, u32[]{:S(2)}) collective-permute-start(bf16[512,256]{1,0:T(8,128)(2,1)S(1)} %fusion.15.rest_0_), channel_id=1, source_target_pairs={{0,4},{1,5},{2,6},{3,7},{4,0},{5,1},{6,2},{7,3},{8,12},{9,13},{10,... | collective-permute-start | bytes 786440 | tf_op jit(solution)/shard_map/ppermute | solution.py:69
  213.7 15.6 %collective-permute-start.48 = (bf16[512,512]{1,0:T(8,128)(2,1)}, bf16[512,512]{1,0:T(8,128)(2,1)S(1)}, u32[]{:S(2)}, u32[]{:S(2)}) collective-permute-start(bf16[512,512]{1,0:T(8,128)(2,1)} %get-tuple-element.310.rest_0_.rest_3_), channel_id=1, source_target_pairs={{0,8},{1,9},{2,10},{3,11},{4,12},{5,13},{6,14},{7,15},{8,0},{9,1},... | collective-permute-start | bytes 1572872 | tf_op jit(solution)/shard_map/ppermute | solution.py:69
  288.3 200.0 %reduce-scatter.5.cloned.1.call-start = ((), (), s32[]{:S(2)}) async-start(), calls=%async_computation.5 | async-start | bytes 7864320 | tf_op jit(solution)/shard_map/reduce_scatter | solution.py:697
  322.6 21.6 %collective-permute-start.69 = (bf16[512,512]{1,0:T(8,128)(2,1)}, bf16[512,512]{1,0:T(8,128)(2,1)S(1)}, u32[]{:S(2)}, u32[]{:S(2)}) collective-permute-start(bf16[512,512]{1,0:T(8,128)(2,1)} %get-tuple-element.361), channel_id=1, source_target_pairs={{0,8},{1,9},{2,10},{3,11},{4,12},{5,13},{6,14},{7,15},{8,0},{9,1},... | collective-permute-start | bytes 1572872 | tf_op jit(solution)/shard_map/ppermute | solution.py:69
  416.3 19.5 %collective-permute-start.83 = (bf16[512,256]{1,0:T(8,128)(2,1)S(1)}, bf16[512,256]{1,0:T(8,128)(2,1)S(1)}, u32[]{:S(2)}, u32[]{:S(2)}) collective-permute-start(bf16[512,256]{1,0:T(8,128)(2,1)S(1)} %get-tuple-element.412.rest_4_), channel_id=1, source_target_pairs={{0,4},{1,5},{2,6},{3,7},{4,0},{5,1},{6,2},{7,3},{8,12},{9,13},{10,... | collective-permute-start | bytes 786440 | tf_op jit(solution)/shard_map/ppermute | solution.py:69
  420.8 15.0 %collective-permute-start.85 = (bf16[128,1024]{1,0:T(8,128)(2,1)S(1)}, bf16[128,1024]{1,0:T(8,128)(2,1)S(1)}, u32[]{:S(2)}, u32[]{:S(2)}) collective-permute-start(bf16[128,1024]{1,0:T(8,128)(2,1)S(1)} %get-tuple-element.407), channel_id=1, source_target_pairs={{0,2},{1,3},{2,0},{3,1},{4,6},{5,7},{6,4},{7,5},{8,10},{9,11},{10,... | collective-permute-start | bytes 786440 | tf_op jit(solution)/shard_map/ppermute | solution.py:69
  428.4 18.6 %collective-permute-start.87 = (bf16[128,1024]{1,0:T(8,128)(2,1)}, bf16[128,1024]{1,0:T(8,128)(2,1)S(1)}, u32[]{:S(2)}, u32[]{:S(2)}) collective-permute-start(bf16[128,1024]{1,0:T(8,128)(2,1)} %slice.357), channel_id=1, source_target_pairs={{0,8},{1,9},{2,10},{3,11},{4,12},{5,13},{6,14},{7,15},{8,0},{9,1},... | collective-permute-start | bytes 786440 | tf_op jit(solution)/shard_map/ppermute | solution.py:69
  428.4 18.5 %collective-permute-start.88 = (bf16[128,1024]{1,0:T(8,128)(2,1)}, bf16[128,1024]{1,0:T(8,128)(2,1)S(1)}, u32[]{:S(2)}, u32[]{:S(2)}) collective-permute-start(bf16[128,1024]{1,0:T(8,128)(2,1)} %slice.358), channel_id=1, source_target_pairs={{0,16},{1,17},{2,18},{3,19},{4,20},{5,21},{6,22},{7,23},{8,24},{9,... | collective-permute-start | bytes 786440 | tf_op jit(solution)/shard_map/ppermute | solution.py:69
  446.5 25.0 %collective-permute-start.89 = (bf16[512,512]{1,0:T(8,128)(2,1)}, bf16[512,512]{1,0:T(8,128)(2,1)}, u32[]{:S(2)}, u32[]{:S(2)}) collective-permute-start(bf16[512,512]{1,0:T(8,128)(2,1)} %get-tuple-element.426), channel_id=1, source_target_pairs={{0,8},{1,9},{2,10},{3,11},{4,12},{5,13},{6,14},{7,15},{8,0},{9,1},... | collective-permute-start | bytes 1572872 | tf_op jit(solution)/shard_map/ppermute | solution.py:69
  512.6 43.9 %collective-permute-start.107 = (bf16[128,3072]{1,0:T(8,128)(2,1)}, bf16[128,3072]{1,0:T(8,128)(2,1)S(1)}, u32[]{:S(2)}, u32[]{:S(2)}) collective-permute-start(bf16[128,3072]{1,0:T(8,128)(2,1)} %get-tuple-element.466), channel_id=1, source_target_pairs={{0,2},{1,3},{2,0},{3,1},{4,6},{5,7},{6,4},{7,5},{8,10},{9,11},{10,... | collective-permute-start | bytes 2359304 | tf_op jit(solution)/shard_map/ppermute | solution.py:69
  513.9 41.0 %collective-permute-start.100 = (bf16[1,256,256]{2,1,0:T(8,128)(2,1)S(1)}, bf16[1,256,256]{2,1,0:T(8,128)(2,1)S(1)}, u32[]{:S(2)}, u32[]{:S(2)}) collective-permute-start(bf16[1,256,256]{2,1,0:T(8,128)(2,1)S(1)} %get-tuple-element.518), channel_id=1, source_target_pairs={{0,2},{1,3},{2,0},{3,1},{4,6},{5,7},{6,4},{7,5},{8,10},{9,11},{10,... | collective-permute-start | bytes 393224 | tf_op jit(solution)/shard_map/ppermute | solution.py:69
  525.6 30.6 %collective-permute-start.102 = (bf16[128,1024]{1,0:T(8,128)(2,1)S(1)}, bf16[128,1024]{1,0:T(8,128)(2,1)S(1)}, u32[]{:S(2)}, u32[]{:S(2)}) collective-permute-start(bf16[128,1024]{1,0:T(8,128)(2,1)S(1)} %slice.368), channel_id=1, source_target_pairs={{0,8},{1,9},{2,10},{3,11},{4,12},{5,13},{6,14},{7,15},{8,0},{9,1},... | collective-permute-start | bytes 786440 | tf_op jit(solution)/shard_map/ppermute | solution.py:69
  526.5 29.8 %collective-permute-start.104 = (bf16[128,1024]{1,0:T(8,128)(2,1)S(1)}, bf16[128,1024]{1,0:T(8,128)(2,1)S(1)}, u32[]{:S(2)}, u32[]{:S(2)}) collective-permute-start(bf16[128,1024]{1,0:T(8,128)(2,1)S(1)} %slice.370), channel_id=1, source_target_pairs={{0,16},{1,17},{2,18},{3,19},{4,20},{5,21},{6,22},{7,23},{8,24},{9,... | collective-permute-start | bytes 786440 | tf_op jit(solution)/shard_map/ppermute | solution.py:69
  565.5 14.8 %collective-permute-start.106 = (bf16[128,1024]{1,0:T(8,128)(2,1)}, bf16[128,1024]{1,0:T(8,128)(2,1)}, u32[]{:S(2)}, u32[]{:S(2)}) collective-permute-start(bf16[128,1024]{1,0:T(8,128)(2,1)} %broadcast_select_fusion.8), channel_id=1, source_target_pairs={{0,2},{1,3},{2,0},{3,1},{4,6},{5,7},{6,4},{7,5},{8,10},{9,11},{10,... | collective-permute-start | bytes 786440 | tf_op jit(solution)/shard_map/ppermute | solution.py:69
  (185 other events, 1741.7 us)
Sparse Core Ops, SparseCore 0:
  92.0 64.8 all-gather.2
  181.9 77.6 all-gather.4
  288.4 77.8 reduce-scatter.2
  403.6 78.3 reduce-scatter.4

commit v4 on v3

--- a/solution.py
+++ b/solution.py
@@ -1193,21 +1193,17 @@
 
             def ffn_side(sent):
                 partial = ffn_grads(sent)
-                if late is None:
-                    return after(partial, current), None
-                rows = return_rows(place, *after(late_ffn, sent))
-                return after(partial, rows), rows
-
-            moved, pieces, ffn_gain_grad, (ffn_partial, late_rows) = step_back(
+                return after(partial, current) if late is None else partial
+
+            moved, pieces, ffn_gain_grad, ffn_partial = step_back(
                 sums, full_mid, scale_mid, gains[LAYERS + layer], upstream, ffn_side
             )
-            ffn_rows = scatter_rows_group(place, *ffn_partial)
+            ffn_rows = scatter_rows_group(place, *after(ffn_partial, moved))
             if late is not None:
-                own_ffn, other_ffn = late_rows
-                others = [place.swap_zh(after(other_ffn[:, :hidden], moved))]
+                own_ffn, other_ffn = return_rows(place, *after(late_ffn, moved))
                 late_got, late_kept = scatter_next(place, after(late_got, moved), late_kept, 1)
-                pieces = after(pieces, others[0], late_kept)
-                others.append(place.swap_zh(after(other_ffn[:, hidden : 2 * hidden], pieces)))
+                pieces = after(pieces, other_ffn, late_kept)
+                others = [place.swap_zh(after(other_ffn[:, :hidden], pieces))]
             common = [queries, attended, logs, own_kinds, kinds, masks]
             later = blocks[half_keys:] if n_o > 1 else blocks
             early = blocks[:half_keys] if n_o > 1 else []
@@ -1246,8 +1242,8 @@
                 output = output * natural_valid[:, :, None].astype(LOW)
                 out_grad = after(out_grad, output)
             if late is not None:
-                out_grad = after(out_grad, others[1], late_got)
-                others.append(place.swap_zh(after(other_ffn[:, 2 * hidden :], out_grad)))
+                out_grad = after(out_grad, others[0], late_got)
+                others.append(place.swap_zh(after(other_ffn[:, hidden : 2 * hidden], out_grad)))
                 late_ends = scatter_rest(place, after(late_got, out_grad), late_kept, 2)
                 own_attn, other_attn = return_rows(place, *late_ends)
             query_grad, same_sum_near, *near = launch(
@@ -1272,8 +1268,8 @@
                 ]
                 near = near[:middle_at]
             if late is not None:
-                received = after(received, others[2], other_attn)
-                others.append(place.swap_zh(after(other_attn, received)))
+                received = after(received, others[1], other_attn)
+                others.append(place.swap_zh(after(other_ffn[:, 2 * hidden :], received)))
             three, *sums = launch(
                 functools.partial(qkv_back_body, attn_lay, 1),
                 [shape((tokens, 3 * width), LOW), *parts],
@@ -1283,7 +1279,8 @@
                 name="qkv_back",
             )
             if late is not None:
-                sums = after(sums, others[3])
+                sums = after(sums, others[2])
+                others.append(place.swap_zh(after(other_attn, sums)))
             attn_grads = functools.partial(
                 weight_grads_of,
                 True,
@@ -1302,8 +1299,7 @@
                 partial = attn_grads(sent)
                 if late is None:
                     return partial, None
-                rows = return_rows(place, *after(ffn_rows, sent))
-                return after(partial, rows), rows
+                return after(partial, others[3]), None
 
             moved, pieces, attn_gain_grad, (attn_partial, last_rows) = step_back(
                 sums, full, scale, gains[layer], middle, attn_side, small_sums if layer == 0 else None
@@ -1311,7 +1307,8 @@
             pending = [*pieces, middle_full, full, scale, moved]
             gain_grads[layer] = (attn_gain_grad, ffn_gain_grad)
             if late is not None:
-                last_own, last_other = last_rows
+                last_own, last_other = return_rows(place, *after(ffn_rows, moved))
+                pending[0] = after(pending[0], last_other)
                 last_sent = place.swap_zh(after(last_other, moved))
                 keep_grads(
                     layer + 1,
@@ -1322,7 +1319,8 @@
             late = (ffn_rows, scatter_start(place, sent, other_sent), attn_kept)
 
         input_grad = leave_rows(pending[0].astype(LOW)).astype(F32)
-        own_attn, other_attn = return_rows(place, *scatter_rest(place, *late[1:]))
+        ends = scatter_rest(place, *after(late[1:], last_other))
+        own_attn, other_attn = return_rows(place, *after(ends, last_sent))
         attn_out = own_attn.astype(F32) + place.swap_zh(other_attn).astype(F32)
         total = after(attn_gain_grad, other_attn)
         for i in range(k):

time: 597 us -> 594 us (level)
  other arithmetic: 52.6 us -> 45.9 us
    unnamed x231 -> x241, local copies, waits for them, and re-layouts: 16.2 us -> 16.8 us
  transfers between devices with their start and end apart: 115 -> 115, of which waited for: 60 -> 62; matrix products, arithmetic and copies ran while one was open for 9% -> 10% of each run, Pallas kernels for 20% -> 20%
where the time goes in v4:
time: 594 us; the launch traced here: 588 us
  waiting for transfers between devices  272 us (46%)
  Pallas kernels  128 us (22%)
  starting transfers between devices  89.2 us (15%)
  other arithmetic  45.9 us (8%)
  local copies, waits for them, and re-layouts  34.8 us (6%)
  between operations  17.6 us (3%)
    ppermute x111, waiting for transfers between devices, move(): return lax.ppermute(array, AXES, pairs)  270 us
    pallas_call x19, Pallas kernels, launch(): pl.pallas_call(body, out_shape=outs, in_specs=specs, out_specs=[VMEM] * l...  128 us
    ppermute x111, starting transfers between devices, move(): return lax.ppermute(array, AXES, pairs)  88.2 us
    unnamed x241, local copies, waits for them, and re-layouts  16.8 us
  transfers between devices with their start and end apart: 115, of which 62 were waited for; matrix products, arithmetic and copies ran while one was open for 10% of the time, Pallas kernels for 20%

profile of v4, /device:TPU:0, one launch (start us, length us, event | category | flops | bytes accessed | tf_op | source)
XLA Modules:
  0.0 587.8 jit_solution(12354950843517724510)
XLA Ops:
  25.8 8.4 %collective-permute-done.4 = f32[2,1,1040]{2,1,0:T(1,128)S(1)} collective-permute-done((f32[2,1,1040]{2,1,0:T(1,128)S(1)}, f32[2,1,1040]{2,1,0:T(1,128)S(1)}, u32[]{:S(2)}, u32[]{:S(2)}) %collective-permute-start.4) | collective-permute-done | bytes 8352 | tf_op jit(solution)/shard_map/ppermute | solution.py:69
  66.4 7.3 %collective-permute-done.17 = bf16[128,1024]{1,0:T(8,128)(2,1)S(1)} collective-permute-done((bf16[128,1024]{1,0:T(8,128)(2,1)S(1)}, bf16[128,1024]{1,0:T(8,128)(2,1)S(1)}, u32[]{:S(2)}, u32[]{:S(2)}) %collective-permute-start.17) | collective-permute-done | bytes 262176 | tf_op jit(solution)/shard_map/ppermute | solution.py:69
  78.1 12.7 %collective-permute-done.14 = bf16[128,1024]{1,0:T(8,128)(2,1)S(1)} collective-permute-done((bf16[128,1024]{1,0:T(8,128)(2,1)S(1)}, bf16[128,1024]{1,0:T(8,128)(2,1)S(1)}, u32[]{:S(2)}, u32[]{:S(2)}) %collective-permute-start.14) | collective-permute-done | bytes 262176 | tf_op jit(solution)/shard_map/ppermute | solution.py:69
  100.7 7.3 %attend.2 = (bf16[512,256]{1,0:T(8,128)(2,1)S(1)}, f32[512,4]{1,0:T(8,128)S(1)}, bf16[512,256]{1,0:T(8,128)(2,1)S(1)}, bf16[512,256]{1,0:T(8,128)(2,1)S(1)}, bf1...) custom-call(s32[5]{0:T(128)S(1)} %stack.168.spot, f32[8]{0:T(128)S(1)} %get-tuple-element.650.bias, ...), custom_call_target="tpu_custom_call" | custom-call | flops 9200000000 | bytes 1024 | tf_op jit(solution)/shard_map/attend/pallas_call | solution.py:129
  121.3 8.0 %collective-permute-done.23 = bf16[128,1024]{1,0:T(8,128)(2,1)S(1)} collective-permute-done((bf16[128,1024]{1,0:T(8,128)(2,1)}, bf16[128,1024]{1,0:T(8,128)(2,1)S(1)}, u32[]{:S(2)}, u32[]{:S(2)}) %collective-permute-start.23) | collective-permute-done | bytes 262176 | tf_op jit(solution)/shard_map/ppermute | solution.py:69
  140.6 5.7 collective-permute-done.24.p1
  147.4 7.2 %collective-permute-done.27 = bf16[128,1024]{1,0:T(8,128)(2,1)S(1)} collective-permute-done((bf16[128,1024]{1,0:T(8,128)(2,1)}, bf16[128,1024]{1,0:T(8,128)(2,1)S(1)}, u32[]{:S(2)}, u32[]{:S(2)}) %collective-permute-start.27) | collective-permute-done | bytes 262176 | tf_op jit(solution)/shard_map/ppermute | solution.py:69
  163.7 8.5 %ffn.1 = (bf16[512,1024]{1,0:T(8,128)(2,1)}, bf16[512,1024]{1,0:T(8,128)(2,1)}, f32[512,1]{1,0:T(8,128)S(1)}, bf16[512,1024]{1,0:T(8,128)(2,1)}, bf16[512,1024]{...) custom-call(s32[5]{0:T(128)S(1)} %stack.168.spot, ...), custom_call_target="tpu_custom_call" | custom-call | flops 10350000128 | bytes 1024 | tf_op jit(solution)/shard_map/ffn/pallas_call | solution.py:129
  184.0 5.9 %collective-permute-done.39 = bf16[512,256]{1,0:T(8,128)(2,1)S(1)} collective-permute-done((bf16[512,256]{1,0:T(8,128)(2,1)S(1)}, bf16[512,256]{1,0:T(8,128)(2,1)S(1)}, u32[]{:S(2)}, u32[]{:S(2)}) %collective-permute-start.39) | collective-permute-done | bytes 262176 | tf_op jit(solution)/shard_map/ppermute | solution.py:69
  190.4 7.6 %collective-permute-done.43.rest_1_ = bf16[512,256]{1,0:T(8,128)(2,1)S(1)} collective-permute-done((bf16[512,256]{1,0:T(8,128)(2,1)S(1)}, bf16[512,256]{1,0:T(8,128)(2,1)S(1)}, u32[]{:S(2)}, u32[]{:S(2)}) %collective-permute-start.43) | collective-permute-done | bytes 262176 | tf_op jit(solution)/shard_map/ppermute | solution.py:69
  218.0 7.6 %collective-permute-done.48.rest_1_.rest_3_ = bf16[512,512]{1,0:T(8,128)(2,1)S(1)} collective-permute-done((bf16[512,512]{1,0:T(8,128)(2,1)}, bf16[512,512]{1,0:T(8,128)(2,1)S(1)}, u32[]{:S(2)}, u32[]{:S(2)}) %collective-permute-start.48) | collective-permute-done | bytes 524320 | tf_op jit(solution)/shard_map/ppermute | solution.py:69
  227.5 7.3 %attend.3 = (bf16[512,256]{1,0:T(8,128)(2,1)S(1)}, f32[512,4]{1,0:T(8,128)S(1)}, bf16[512,256]{1,0:T(8,128)(2,1)S(1)}, bf16[512,256]{1,0:T(8,128)(2,1)S(1)}, bf1...) custom-call(s32[5]{0:T(128)S(1)} %stack.168.spot, f32[8]{0:T(128)S(1)} %get-tuple-element.651.bias, ...), custom_call_target="tpu_custom_call" | custom-call | flops 9200000000 | bytes 1024 | tf_op jit(solution)/shard_map/attend/pallas_call | solution.py:129
  237.8 7.7 %collective-permute-done.53 = bf16[512,256]{1,0:T(8,128)(2,1)S(1)} collective-permute-done((bf16[512,256]{1,0:T(8,128)(2,1)S(1)}, bf16[512,256]{1,0:T(8,128)(2,1)S(1)}, u32[]{:S(2)}, u32[]{:S(2)}) %collective-permute-start.53) | collective-permute-done | bytes 262176 | tf_op jit(solution)/shard_map/ppermute | solution.py:69
  247.2 7.0 %collective-permute-done.55.p1 = bf16[512,256]{1,0:T(8,128)(2,1)S(1)} collective-permute-done((bf16[512,256]{1,0:T(8,128)(2,1)S(1)}, bf16[512,256]{1,0:T(8,128)(2,1)S(1)}, u32[]{:S(2)}, u32[]{:S(2)}) %collective-permute-start.55) | collective-permute-done | bytes 262176 | tf_op jit(solution)/shard_map/ppermute | solution.py:69
  258.1 13.3 %ffn_both.1 = (bf16[512,1024]{1,0:T(8,128)(2,1)}, bf16[512,1024]{1,0:T(8,128)(2,1)}, f32[512,1]{1,0:T(8,128)S(1)}, bf16[512,1024]{1,0:T(8,128)(2,1)}, bf16[512,1...) custom-call(s32[5]{0:T(128)S(1)} %stack.168.spot, ...), custom_call_target="tpu_custom_call" | custom-call | flops 13799999488 | bytes 1024 | tf_op jit(solution)/shard_map/ffn_both/pallas_call | solution.py:129
  278.7 8.9 %ffn_weights.2 = bf16[1024,3072]{1,0:T(8,128)(2,1)} custom-call(s32[5]{0:T(128)S(1)} %stack.168.spot, bf16[512,1024]{1,0:T(8,128)(2,1)S(1)} %copy-done.18, bf16[512,1024]{1,0:T(8,128)(2,1)} %get-tuple-element.350.refs_1_, bf16[512,1024]{1,0:T(8,128)(2,1)} %get-tuple-element.351.refs_2_, bf16[512,1024]{1,0:T(8,128)(2,1)} %frame.3.upstream.refs_3_.rest_8_, ...), custom_call_target="tpu_custom_call" | custom-call | flops 10350000128 | bytes 1024 | tf_op jit(solution)/shard_map/ffn_weights/pallas_call | solution.py:129
  297.1 6.4 %collective-permute-done.66.rest_5_ = bf16[512,256]{1,0:T(8,128)(2,1)S(1)} collective-permute-done((bf16[512,256]{1,0:T(8,128)(2,1)S(1)}, bf16[512,256]{1,0:T(8,128)(2,1)S(1)}, u32[]{:S(2)}, u32[]{:S(2)}) %collective-permute-start.66) | collective-permute-done | bytes 262176 | tf_op jit(solution)/shard_map/ppermute | solution.py:69
  305.9 10.1 %attend_back_far.2 = (bf16[512,1024]{1,0:T(8,128)(2,1)}, f32[512,256]{1,0:T(8,128)}, bf16[512,256]{1,0:T(8,128)(2,1)S(1)}, f32[512,4]{1,0:T(8,128)S(1)}, f32[512...) custom-call(s32[5]{0:T(128)S(1)} %stack.168.spot, f32[8]{0:T(128)S(1)} %get-tuple-element.651.bias, ...), custom_call_target="tpu_custom_call" | custom-call | flops 10350000128 | bytes 1024 | tf_op jit(solution)/shard_map/attend_back_far/pallas_call | solution.py:129
  317.7 6.1 %attend_back_near.2 = (f32[512,256]{1,0:T(8,128)}, f32[4,512]{1,0:T(4,128)S(1)}, f32[512,512]{1,0:T(8,128)}) custom-call(s32[5]{0:T(128)S(1)} %stack.168.spot, f32[8]{0:T(128)S(1)} %get-tuple-element.651.bias, bf16[512,256]{1,0:T(8,128)(2,1)S(1)} %copy-done.22, bf16[512,256]{1,0:T(8,128)(2,1)S(1)} %get-tuple-element.380.attended.refs_3_, ...), custom_call_target="tpu_custom_call" | custom-call | flops 6899999744 | bytes 1024 | tf_op jit(solution)/shard_map/attend_back_near/pallas_call | solution.py:129
  323.8 18.1 %collective-permute-done.69.rest_0_ = bf16[512,512]{1,0:T(8,128)(2,1)S(1)} collective-permute-done((bf16[512,512]{1,0:T(8,128)(2,1)}, bf16[512,512]{1,0:T(8,128)(2,1)S(1)}, u32[]{:S(2)}, u32[]{:S(2)}) %collective-permute-start.69) | collective-permute-done | bytes 524320 | tf_op jit(solution)/shard_map/ppermute | solution.py:69
  361.4 6.2 %collective-permute-done.73.rest_1_ = bf16[512,256]{1,0:T(8,128)(2,1)S(1)} collective-permute-done((bf16[512,256]{1,0:T(8,128)(2,1)S(1)}, bf16[512,256]{1,0:T(8,128)(2,1)S(1)}, u32[]{:S(2)}, u32[]{:S(2)}) %collective-permute-start.73) | collective-permute-done | bytes 262176 | tf_op jit(solution)/shard_map/ppermute | solution.py:69
  370.3 10.2 %ffn_back.1 = (bf16[512,1024]{1,0:T(8,128)(2,1)}, f32[512,256]{1,0:T(8,128)}, bf16[512,1024]{1,0:T(8,128)(2,1)}, bf16[512,1024]{1,0:T(8,128)(2,1)}, bf16[512,256...) custom-call(s32[5]{0:T(128)S(1)} %stack.168.spot, ...), custom_call_target="tpu_custom_call" | custom-call | flops 11500000256 | bytes 1024 | tf_op jit(solution)/shard_map/ffn_back/pallas_call | solution.py:129
  388.7 8.8 %ffn_weights.3 = bf16[1024,3072]{1,0:T(8,128)(2,1)} custom-call(s32[5]{0:T(128)S(1)} %stack.168.spot, bf16[512,1024]{1,0:T(8,128)(2,1)S(1)} %copy-done.17, bf16[512,1024]{1,0:T(8,128)(2,1)} %get-tuple-element.407.refs_1_, bf16[512,1024]{1,0:T(8,128)(2,1)} %get-tuple-element.408.refs_2_, bf16[512,1024]{1,0:T(8,128)(2,1)} %get-tuple-element.409.refs_3_.rest_8_, ...), custom_call_target="tpu_custom_call" | custom-call | flops 10350000128 | bytes 1024 | tf_op jit(solution)/shard_map/ffn_weights/pallas_call | solution.py:129
  417.7 9.7 %attend_back_far.3 = (bf16[512,1024]{1,0:T(8,128)(2,1)}, f32[512,256]{1,0:T(8,128)}, bf16[512,256]{1,0:T(8,128)(2,1)S(1)}, f32[512,4]{1,0:T(8,128)S(1)}, f32[512...) custom-call(s32[5]{0:T(128)S(1)} %stack.168.spot, f32[8]{0:T(128)S(1)} %get-tuple-element.650.bias, ...), custom_call_target="tpu_custom_call" | custom-call | flops 10350000128 | bytes 1024 | tf_op jit(solution)/shard_map/attend_back_far/pallas_call | solution.py:129
  431.1 6.1 %attend_back_near.3 = (f32[512,256]{1,0:T(8,128)}, f32[4,512]{1,0:T(4,128)S(1)}, f32[512,512]{1,0:T(8,128)}) custom-call(s32[5]{0:T(128)S(1)} %stack.168.spot, f32[8]{0:T(128)S(1)} %get-tuple-element.650.bias, bf16[512,256]{1,0:T(8,128)(2,1)S(1)} %copy-done.20, bf16[512,256]{1,0:T(8,128)(2,1)S(1)} %get-tuple-element.453.attended.refs_3_, ...), custom_call_target="tpu_custom_call" | custom-call | flops 6899999744 | bytes 1024 | tf_op jit(solution)/shard_map/attend_back_near/pallas_call | solution.py:129
  439.3 14.3 %collective-permute-done.88.rest_0_ = bf16[512,512]{1,0:T(8,128)(2,1)} collective-permute-done((bf16[512,512]{1,0:T(8,128)(2,1)}, bf16[512,512]{1,0:T(8,128)(2,1)}, u32[]{:S(2)}, u32[]{:S(2)}) %collective-permute-start.88) | collective-permute-done | bytes 524320 | tf_op jit(solution)/shard_map/ppermute | solution.py:69
  459.1 8.6 %collective-permute-done.91 = bf16[128,1024]{1,0:T(8,128)(2,1)S(1)} collective-permute-done((bf16[128,1024]{1,0:T(8,128)(2,1)}, bf16[128,1024]{1,0:T(8,128)(2,1)S(1)}, u32[]{:S(2)}, u32[]{:S(2)}) %collective-permute-start.91) | collective-permute-done | bytes 262176 | tf_op jit(solution)/shard_map/ppermute | solution.py:69
  476.5 5.6 collective-permute-done.95
  499.4 8.3 %collective-permute-done.101 = bf16[256,1024]{1,0:T(8,128)(2,1)} collective-permute-done((bf16[256,1024]{1,0:T(8,128)(2,1)S(1)}, bf16[256,1024]{1,0:T(8,128)(2,1)}, u32[]{:S(2)}, u32[]{:S(2)}) %collective-permute-start.101) | collective-permute-done | bytes 524320 | tf_op jit(solution)/shard_map/ppermute | solution.py:69
  516.3 21.3 %collective-permute-done.100 = bf16[1,256,256]{2,1,0:T(8,128)(2,1)S(1)} collective-permute-done((bf16[1,256,256]{2,1,0:T(8,128)(2,1)S(1)}, bf16[1,256,256]{2,1,0:T(8,128)(2,1)S(1)}, u32[]{:S(2)}, u32[]{:S(2)}) %collective-permute-start.100) | collective-permute-done | bytes 131104 | tf_op jit(solution)/shard_map/ppermute | solution.py:69
  539.0 15.3 %collective-permute-done.105 = bf16[128,3072]{1,0:T(8,128)(2,1)S(1)} collective-permute-done((bf16[128,3072]{1,0:T(8,128)(2,1)S(1)}, bf16[128,3072]{1,0:T(8,128)(2,1)S(1)}, u32[]{:S(2)}, u32[]{:S(2)}) %collective-permute-start.105) | collective-permute-done | bytes 786464 | tf_op jit(solution)/shard_map/ppermute | solution.py:69
  567.8 8.3 %collective-permute-done.110 = f32[2,2,1040]{2,1,0:T(2,128)S(1)} collective-permute-done((f32[2,2,1040]{2,1,0:T(2,128)S(1)}, f32[2,2,1040]{2,1,0:T(2,128)S(1)}, u32[]{:S(2)}, u32[]{:S(2)}) %collective-permute-start.110) | collective-permute-done | bytes 16672 | tf_op jit(solution)/shard_map/ppermute | solution.py:69
  (648 shorter events, 276.4 us)
Async XLA Ops:
  7.2 154.4 %all-gather.3.cloned.1.call-start = ((), (), s32[]{:S(2)}) async-start(), calls=%async_computation.2 | async-start | bytes 5242880 | tf_op jit(solution)/shard_map/all_gather | solution.py:671
  22.5 16.6 %collective-permute-start.1 = (bf16[2,1,256,256]{3,2,1,0:T(8,128)(2,1)S(1)}, bf16[2,1,256,256]{3,2,1,0:T(8,128)(2,1)S(1)}, u32[]{:S(2)}, u32[]{:S(2)}) collective-permute-start(bf16[2,1,256,256]{3,2,1,0:T(8,128)(2,1)S(1)} %get-tuple-element.611), channel_id=1, source_target_pairs={{0,1},{1,0},{2,3},{3,2},{4,5},{5,4},{6,7},{7,6},{8,9},{9,8},{10,11... | collective-permute-start | bytes 786440 | tf_op jit(solution)/shard_map/ppermute | solution.py:69
  47.8 25.9 %collective-permute-start.15 = (bf16[128,1024]{1,0:T(8,128)(2,1)S(1)}, bf16[128,1024]{1,0:T(8,128)(2,1)S(1)}, u32[]{:S(2)}, u32[]{:S(2)}) collective-permute-start(bf16[128,1024]{1,0:T(8,128)(2,1)S(1)} %get-tuple-element.259), channel_id=1, source_target_pairs={{0,2},{1,3},{2,0},{3,1},{4,6},{5,7},{6,4},{7,5},{8,10},{9,11},{10,... | collective-permute-start | bytes 786440 | tf_op jit(solution)/shard_map/ppermute | solution.py:69
  51.9 21.9 %collective-permute-start.17 = (bf16[128,1024]{1,0:T(8,128)(2,1)S(1)}, bf16[128,1024]{1,0:T(8,128)(2,1)S(1)}, u32[]{:S(2)}, u32[]{:S(2)}) collective-permute-start(bf16[128,1024]{1,0:T(8,128)(2,1)S(1)} %get-tuple-element.261), channel_id=1, source_target_pairs={{0,2},{1,3},{2,0},{3,1},{4,6},{5,7},{6,4},{7,5},{8,10},{9,11},{10,... | collective-permute-start | bytes 786440 | tf_op jit(solution)/shard_map/ppermute | solution.py:69
  65.8 25.0 %collective-permute-start.13 = (bf16[512,512]{1,0:T(8,128)(2,1)}, bf16[512,512]{1,0:T(8,128)(2,1)}, u32[]{:S(2)}, u32[]{:S(2)}) collective-permute-start(bf16[512,512]{1,0:T(8,128)(2,1)} %get-tuple-element.263.rest_0_.rest_3_), channel_id=1, source_target_pairs={{0,8},{1,9},{2,10},{3,11},{4,12},{5,13},{6,14},{7,15},{8,0},{9,1},... | collective-permute-start | bytes 1572872 | tf_op jit(solution)/shard_map/ppermute | solution.py:69
  91.9 166.2 %all-gather.5.cloned.1.call-start = ((), (), s32[]{:S(2)}) async-start(), calls=%async_computation.3 | async-start | bytes 7864320 | tf_op jit(solution)/shard_map/all_gather | solution.py:671
  114.2 15.1 %collective-permute-start.23 = (bf16[128,1024]{1,0:T(8,128)(2,1)}, bf16[128,1024]{1,0:T(8,128)(2,1)S(1)}, u32[]{:S(2)}, u32[]{:S(2)}) collective-permute-start(bf16[128,1024]{1,0:T(8,128)(2,1)} %get-tuple-element.274), channel_id=1, source_target_pairs={{0,2},{1,3},{2,0},{3,1},{4,6},{5,7},{6,4},{7,5},{8,10},{9,11},{10,... | collective-permute-start | bytes 786440 | tf_op jit(solution)/shard_map/ppermute | solution.py:69
  136.9 22.3 %collective-permute-start.33 = (bf16[256,1024]{1,0:T(8,128)(2,1)}, bf16[256,1024]{1,0:T(8,128)(2,1)}, u32[]{:S(2)}, u32[]{:S(2)}) collective-permute-start(bf16[256,1024]{1,0:T(8,128)(2,1)} %pad_maximum_fusion.7), channel_id=1, source_target_pairs={{0,16},{1,17},{2,18},{3,19},{4,20},{5,21},{6,22},{7,23},{8,24},{9,... | collective-permute-start | bytes 1572872 | tf_op jit(solution)/shard_map/ppermute | solution.py:69
  138.3 20.9 %collective-permute-start.31 = (bf16[256,1024]{1,0:T(8,128)(2,1)}, bf16[256,1024]{1,0:T(8,128)(2,1)}, u32[]{:S(2)}, u32[]{:S(2)}) collective-permute-start(bf16[256,1024]{1,0:T(8,128)(2,1)} %pad_maximum_fusion.6), channel_id=1, source_target_pairs={{0,8},{1,9},{2,10},{3,11},{4,12},{5,13},{6,14},{7,15},{8,0},{9,1},... | collective-permute-start | bytes 1572872 | tf_op jit(solution)/shard_map/ppermute | solution.py:69
  139.1 15.6 %collective-permute-start.25 = (bf16[512,256]{1,0:T(8,128)(2,1)S(1)}, bf16[512,256]{1,0:T(8,128)(2,1)S(1)}, u32[]{:S(2)}, u32[]{:S(2)}) collective-permute-start(bf16[512,256]{1,0:T(8,128)(2,1)S(1)} %get-tuple-element.288.p0), channel_id=1, source_target_pairs={{0,4},{1,5},{2,6},{3,7},{4,0},{5,1},{6,2},{7,3},{8,12},{9,13},{10,... | collective-permute-start | bytes 786440 | tf_op jit(solution)/shard_map/ppermute | solution.py:69
  139.2 15.5 %collective-permute-start.27 = (bf16[128,1024]{1,0:T(8,128)(2,1)}, bf16[128,1024]{1,0:T(8,128)(2,1)S(1)}, u32[]{:S(2)}, u32[]{:S(2)}) collective-permute-start(bf16[128,1024]{1,0:T(8,128)(2,1)} %get-tuple-element.276), channel_id=1, source_target_pairs={{0,2},{1,3},{2,0},{3,1},{4,6},{5,7},{6,4},{7,5},{8,10},{9,11},{10,... | collective-permute-start | bytes 786440 | tf_op jit(solution)/shard_map/ppermute | solution.py:69
  181.1 221.1 %reduce-scatter.3.cloned.1.call-start = ((), (), s32[]{:S(2)}) async-start(), calls=%async_computation.4 | async-start | bytes 7864320 | tf_op jit(solution)/shard_map/reduce_scatter | solution.py:697
  181.8 17.9 %collective-permute-start.46 = (bf16[256,1024]{1,0:T(8,128)(2,1)S(1)}, bf16[256,1024]{1,0:T(8,128)(2,1)S(1)}, u32[]{:S(2)}, u32[]{:S(2)}) collective-permute-start(bf16[256,1024]{1,0:T(8,128)(2,1)S(1)} %pad_maximum_fusion.8), channel_id=1, source_target_pairs={{0,8},{1,9},{2,10},{3,11},{4,12},{5,13},{6,14},{7,15},{8,0},{9,1},... | collective-permute-start | bytes 1572872 | tf_op jit(solution)/shard_map/ppermute | solution.py:69
  183.4 19.6 %collective-permute-start.47 = (bf16[256,1024]{1,0:T(8,128)(2,1)S(1)}, bf16[256,1024]{1,0:T(8,128)(2,1)S(1)}, u32[]{:S(2)}, u32[]{:S(2)}) collective-permute-start(bf16[256,1024]{1,0:T(8,128)(2,1)S(1)} %pad_maximum_fusion.9), channel_id=1, source_target_pairs={{0,16},{1,17},{2,18},{3,19},{4,20},{5,21},{6,22},{7,23},{8,24},{9,... | collective-permute-start | bytes 1572872 | tf_op jit(solution)/shard_map/ppermute | solution.py:69
  209.2 16.4 %collective-permute-start.48 = (bf16[512,512]{1,0:T(8,128)(2,1)}, bf16[512,512]{1,0:T(8,128)(2,1)S(1)}, u32[]{:S(2)}, u32[]{:S(2)}) collective-permute-start(bf16[512,512]{1,0:T(8,128)(2,1)} %get-tuple-element.318.rest_0_.rest_3_), channel_id=1, source_target_pairs={{0,8},{1,9},{2,10},{3,11},{4,12},{5,13},{6,14},{7,15},{8,0},{9,1},... | collective-permute-start | bytes 1572872 | tf_op jit(solution)/shard_map/ppermute | solution.py:69
  272.1 15.5 %collective-permute-start.58 = (bf16[512,256]{1,0:T(8,128)(2,1)S(1)}, bf16[512,256]{1,0:T(8,128)(2,1)}, u32[]{:S(2)}, u32[]{:S(2)}) collective-permute-start(bf16[512,256]{1,0:T(8,128)(2,1)S(1)} %get-tuple-element.337), channel_id=1, source_target_pairs={{0,4},{1,5},{2,6},{3,7},{4,0},{5,1},{6,2},{7,3},{8,12},{9,13},{10,... | collective-permute-start | bytes 786440 | tf_op jit(solution)/shard_map/ppermute | solution.py:69
  272.2 17.0 %collective-permute-start.61 = (bf16[512,256]{1,0:T(8,128)(2,1)}, bf16[512,256]{1,0:T(8,128)(2,1)S(1)}, u32[]{:S(2)}, u32[]{:S(2)}) collective-permute-start(bf16[512,256]{1,0:T(8,128)(2,1)} %get-tuple-element.342), channel_id=1, source_target_pairs={{0,4},{1,5},{2,6},{3,7},{4,0},{5,1},{6,2},{7,3},{8,12},{9,13},{10,... | collective-permute-start | bytes 786440 | tf_op jit(solution)/shard_map/ppermute | solution.py:69
  291.5 203.8 %reduce-scatter.5.cloned.1.call-start = ((), (), s32[]{:S(2)}) async-start(), calls=%async_computation.5 | async-start | bytes 7864320 | tf_op jit(solution)/shard_map/reduce_scatter | solution.py:697
  315.9 26.0 %collective-permute-start.69 = (bf16[512,512]{1,0:T(8,128)(2,1)}, bf16[512,512]{1,0:T(8,128)(2,1)S(1)}, u32[]{:S(2)}, u32[]{:S(2)}) collective-permute-start(bf16[512,512]{1,0:T(8,128)(2,1)} %get-tuple-element.369), channel_id=1, source_target_pairs={{0,8},{1,9},{2,10},{3,11},{4,12},{5,13},{6,14},{7,15},{8,0},{9,1},... | collective-permute-start | bytes 1572872 | tf_op jit(solution)/shard_map/ppermute | solution.py:69
  367.6 15.7 %collective-permute-start.76 = (bf16[256,1024]{1,0:T(8,128)(2,1)S(1)}, bf16[256,1024]{1,0:T(8,128)(2,1)S(1)}, u32[]{:S(2)}, u32[]{:S(2)}) collective-permute-start(bf16[256,1024]{1,0:T(8,128)(2,1)S(1)} %get-tuple-element.395), channel_id=1, source_target_pairs={{0,16},{1,17},{2,18},{3,19},{4,20},{5,21},{6,22},{7,23},{8,24},{9,... | collective-permute-start | bytes 1572872 | tf_op jit(solution)/shard_map/ppermute | solution.py:69
  368.3 14.9 %collective-permute-start.77 = (bf16[256,1024]{1,0:T(8,128)(2,1)S(1)}, bf16[256,1024]{1,0:T(8,128)(2,1)S(1)}, u32[]{:S(2)}, u32[]{:S(2)}) collective-permute-start(bf16[256,1024]{1,0:T(8,128)(2,1)S(1)} %get-tuple-element.396), channel_id=1, source_target_pairs={{0,8},{1,9},{2,10},{3,11},{4,12},{5,13},{6,14},{7,15},{8,0},{9,1},... | collective-permute-start | bytes 1572872 | tf_op jit(solution)/shard_map/ppermute | solution.py:69
  407.4 21.8 %collective-permute-start.86 = (bf16[128,1024]{1,0:T(8,128)(2,1)}, bf16[128,1024]{1,0:T(8,128)(2,1)S(1)}, u32[]{:S(2)}, u32[]{:S(2)}) collective-permute-start(bf16[128,1024]{1,0:T(8,128)(2,1)} %slice.356), channel_id=1, source_target_pairs={{0,8},{1,9},{2,10},{3,11},{4,12},{5,13},{6,14},{7,15},{8,0},{9,1},... | collective-permute-start | bytes 786440 | tf_op jit(solution)/shard_map/ppermute | solution.py:69
  408.9 20.3 %collective-permute-start.87 = (bf16[128,1024]{1,0:T(8,128)(2,1)}, bf16[128,1024]{1,0:T(8,128)(2,1)S(1)}, u32[]{:S(2)}, u32[]{:S(2)}) collective-permute-start(bf16[128,1024]{1,0:T(8,128)(2,1)} %slice.357), channel_id=1, source_target_pairs={{0,16},{1,17},{2,18},{3,19},{4,20},{5,21},{6,22},{7,23},{8,24},{9,... | collective-permute-start | bytes 786440 | tf_op jit(solution)/shard_map/ppermute | solution.py:69
  415.3 15.1 %collective-permute-start.85 = (bf16[128,1024]{1,0:T(8,128)(2,1)}, bf16[128,1024]{1,0:T(8,128)(2,1)S(1)}, u32[]{:S(2)}, u32[]{:S(2)}) collective-permute-start(bf16[128,1024]{1,0:T(8,128)(2,1)} %get-tuple-element.427), channel_id=1, source_target_pairs={{0,2},{1,3},{2,0},{3,1},{4,6},{5,7},{6,4},{7,5},{8,10},{9,11},{10,... | collective-permute-start | bytes 786440 | tf_op jit(solution)/shard_map/ppermute | solution.py:69
  427.6 26.0 %collective-permute-start.88 = (bf16[512,512]{1,0:T(8,128)(2,1)}, bf16[512,512]{1,0:T(8,128)(2,1)}, u32[]{:S(2)}, u32[]{:S(2)}) collective-permute-start(bf16[512,512]{1,0:T(8,128)(2,1)} %get-tuple-element.433), channel_id=1, source_target_pairs={{0,8},{1,9},{2,10},{3,11},{4,12},{5,13},{6,14},{7,15},{8,0},{9,1},... | collective-permute-start | bytes 1572872 | tf_op jit(solution)/shard_map/ppermute | solution.py:69
  437.8 15.8 %collective-permute-start.89 = (bf16[128,1024]{1,0:T(8,128)(2,1)}, bf16[128,1024]{1,0:T(8,128)(2,1)S(1)}, u32[]{:S(2)}, u32[]{:S(2)}) collective-permute-start(bf16[128,1024]{1,0:T(8,128)(2,1)} %get-tuple-element.434), channel_id=1, source_target_pairs={{0,2},{1,3},{2,0},{3,1},{4,6},{5,7},{6,4},{7,5},{8,10},{9,11},{10,... | collective-permute-start | bytes 786440 | tf_op jit(solution)/shard_map/ppermute | solution.py:69
  467.8 16.2 %collective-permute-start.92 = (bf16[512,256]{1,0:T(8,128)(2,1)S(1)}, bf16[512,256]{1,0:T(8,128)(2,1)S(1)}, u32[]{:S(2)}, u32[]{:S(2)}) collective-permute-start(bf16[512,256]{1,0:T(8,128)(2,1)S(1)} %get-tuple-element.444), channel_id=1, source_target_pairs={{0,4},{1,5},{2,6},{3,7},{4,0},{5,1},{6,2},{7,3},{8,12},{9,13},{10,... | collective-permute-start | bytes 786440 | tf_op jit(solution)/shard_map/ppermute | solution.py:69
  511.0 27.8 %collective-permute-start.103 = (bf16[128,1024]{1,0:T(8,128)(2,1)S(1)}, bf16[128,1024]{1,0:T(8,128)(2,1)S(1)}, u32[]{:S(2)}, u32[]{:S(2)}) collective-permute-start(bf16[128,1024]{1,0:T(8,128)(2,1)S(1)} %slice.368), channel_id=1, source_target_pairs={{0,8},{1,9},{2,10},{3,11},{4,12},{5,13},{6,14},{7,15},{8,0},{9,1},... | collective-permute-start | bytes 786440 | tf_op jit(solution)/shard_map/ppermute | solution.py:69
  511.7 25.8 %collective-permute-start.100 = (bf16[1,256,256]{2,1,0:T(8,128)(2,1)S(1)}, bf16[1,256,256]{2,1,0:T(8,128)(2,1)S(1)}, u32[]{:S(2)}, u32[]{:S(2)}) collective-permute-start(bf16[1,256,256]{2,1,0:T(8,128)(2,1)S(1)} %get-tuple-element.534), channel_id=1, source_target_pairs={{0,2},{1,3},{2,0},{3,1},{4,6},{5,7},{6,4},{7,5},{8,10},{9,11},{10,... | collective-permute-start | bytes 393224 | tf_op jit(solution)/shard_map/ppermute | solution.py:69
  512.8 26.1 %collective-permute-start.104 = (bf16[128,1024]{1,0:T(8,128)(2,1)S(1)}, bf16[128,1024]{1,0:T(8,128)(2,1)S(1)}, u32[]{:S(2)}, u32[]{:S(2)}) collective-permute-start(bf16[128,1024]{1,0:T(8,128)(2,1)S(1)} %slice.370), channel_id=1, source_target_pairs={{0,16},{1,17},{2,18},{3,19},{4,20},{5,21},{6,22},{7,23},{8,24},{9,... | collective-permute-start | bytes 786440 | tf_op jit(solution)/shard_map/ppermute | solution.py:69
  514.0 40.3 %collective-permute-start.105 = (bf16[128,3072]{1,0:T(8,128)(2,1)S(1)}, bf16[128,3072]{1,0:T(8,128)(2,1)S(1)}, u32[]{:S(2)}, u32[]{:S(2)}) collective-permute-start(bf16[128,3072]{1,0:T(8,128)(2,1)S(1)} %broadcast_select_fusion), channel_id=1, source_target_pairs={{0,2},{1,3},{2,0},{3,1},{4,6},{5,7},{6,4},{7,5},{8,10},{9,11},{10,... | collective-permute-start | bytes 2359304 | tf_op jit(solution)/shard_map/ppermute | solution.py:69
  562.4 15.2 %collective-permute-start.107 = (bf16[128,1024]{1,0:T(8,128)(2,1)S(1)}, bf16[128,1024]{1,0:T(8,128)(2,1)S(1)}, u32[]{:S(2)}, u32[]{:S(2)}) collective-permute-start(bf16[128,1024]{1,0:T(8,128)(2,1)S(1)} %broadcast_select_fusion.6), channel_id=1, source_target_pairs={{0,2},{1,3},{2,0},{3,1},{4,6},{5,7},{6,4},{7,5},{8,10},{9,11},{10,... | collective-permute-start | bytes 786440 | tf_op jit(solution)/shard_map/ppermute | solution.py:69
  (190 other events, 1869.0 us)
Sparse Core Ops, SparseCore 0:
  92.0 63.8 all-gather.2
  181.2 76.8 all-gather.4
  291.6 83.5 reduce-scatter.2
  400.8 86.1 reduce-scatter.4
